TPU v7x, 32 devices: a whole 2x2x4 slice. The times are simulated.
32 devices in a mesh: grp: 4 (over y, core), rep: 8 (over z, x).
Axes of the slice: x: 2, y: 2, z: 4, core: 2. Of those that a mesh axis runs over, the one named last changes fastest.
Arguments:
- tokens: bfloat16 [4096, 2048], P(('grp', 'rep')), may hold values from -6 to 6
- cotangent: bfloat16 [4096, 2048], P(('grp', 'rep')), may hold values from -6 to 6
- gain_attn: float32 [2048], replicated, may hold values from 0.5 to 1.5
- gain_ffn: float32 [2048], replicated, may hold values from 0.5 to 1.5
- w_query: bfloat16 [2048, 2048], P('grp'), may hold values from -0.125 to 0.125
- w_out: bfloat16 [2048, 2048], P('grp'), may hold values from -1 to 1
- w_gate: bfloat16 [2048, 5504], P('grp'), may hold values from -0.125 to 0.125
- w_up: bfloat16 [2048, 5504], P('grp'), may hold values from -0.125 to 0.125
- w_down: bfloat16 [5504, 2048], P('grp'), may hold values from -0.078125 to 0.078125
- keys: bfloat16 [4096, 512], P(('grp', 'rep')), may hold values from -6 to 6
- values: bfloat16 [4096, 512], P(('grp', 'rep')), may hold values from -6 to 6
- starts: int32 [8], replicated, may hold values from 0 to 4095, as said below
Outputs:
- output: bfloat16 [4096, 2048], P(('grp', 'rep'))
- d_tokens: bfloat16 [4096, 2048], P(('grp', 'rep'))
- d_gain_attn: float32 [2048], P(('grp', 'rep'))
- d_gain_ffn: float32 [2048], P(('grp', 'rep'))
- d_w_query: float32 [2048, 2048], P(('grp', 'rep'))
- d_w_out: float32 [2048, 2048], P(('grp', 'rep'))
- d_w_gate: float32 [2048, 5504], P(('grp', 'rep'))
- d_w_up: float32 [2048, 5504], P(('grp', 'rep'))
- d_w_down: float32 [5504, 2048], P(('grp', 'rep'))
- d_keys: bfloat16 [4096, 512], P(('grp', 'rep'))
- d_values: bfloat16 [4096, 512], P(('grp', 'rep'))
Inputs may be any that keep to these rules, and one draw needn't show every extreme that they name: `starts`: strictly increasing with first entry 0; every document (from one start to the next, the last one to 4096) holds at most min(4096, 2048) tokens, and one holds exactly that many.
All inputs are finite; a program needn't handle non-finite values.
Results may differ from a plain program's by a relative error of at most 0.03.
Values may be sent and summed in bfloat16 or wider, within the bound.
No kernel may reach another device: no remote copies, remote signals or barrier semaphores. Data moves between devices by JAX's collectives and lax.ppermute only.
A program may use at most 448 MiB of HBM per device.

v0:
```python
import jax
import jax.numpy as jnp
from jax import lax
from jax.sharding import PartitionSpec as P

HD = 128
MAXDOC = 4096


EPSILON = 1e-06
NEGATIVE = -1e30


def from_behind(value, axis, by):
    count = lax.axis_size(axis)
    pairs = [(i, i + by) for i in range(count) if 0 <= i + by < count]
    return lax.ppermute(value, axis, pairs)


def doc_numbers(starts, positions):
    return jnp.sum((starts[None, :] <= positions[:, None]).astype(jnp.int32), axis=1) - 1


def on_device(
    tokens,
    cotangent,
    gain_attn,
    gain_ffn,
    w_query,
    w_out,
    w_gate,
    w_up,
    w_down,
    keys,
    values,
    starts,
):
    rows, width = tokens.shape
    kv_width = keys.shape[1]
    groups = kv_width // HD
    heads = width // HD
    share = heads // groups
    scale = HD ** (-0.5)
    devices_all = lax.axis_size(("grp", "rep"))
    total_rows = rows * devices_all
    longest = min(MAXDOC, total_rows // 2)
    reach = min((longest - 2) // rows + 1, devices_all - 1)
    offsets = jnp.arange(1, reach + 1, dtype=jnp.int32)
    wq_full, wo_full, wg_full, wu_full, wd_full = (
        lax.all_gather(w_query, "grp", axis=0, tiled=True),
        lax.all_gather(w_out, "grp", axis=0, tiled=True),
        lax.all_gather(w_gate, "grp", axis=0, tiled=True),
        lax.all_gather(w_up, "grp", axis=0, tiled=True),
        lax.all_gather(w_down, "grp", axis=0, tiled=True),
    )
    myself = lax.axis_index(("grp", "rep"))
    query_pos = myself * rows + jnp.arange(rows, dtype=jnp.int32)
    query_doc = doc_numbers(starts, query_pos)
    x_full = tokens.astype(jnp.float32)
    inv_one = lax.rsqrt(jnp.mean(x_full * x_full, axis=1, keepdims=True) + EPSILON)
    normed_one = x_full * inv_one
    h_one = (normed_one * gain_attn).astype(jnp.bfloat16)
    query = jnp.dot(h_one, wq_full, preferred_element_type=jnp.float32).astype(jnp.bfloat16)
    query_four = query.reshape(rows, groups, share, HD)

    def scores_of(key_piece, owner):
        key_pos = owner * rows + jnp.arange(rows, dtype=jnp.int32)
        key_doc = doc_numbers(starts, key_pos)
        allowed = (key_doc[None, :] == query_doc[:, None]) & (
            key_pos[None, :] <= query_pos[:, None]
        )
        key_three = key_piece.reshape(rows, groups, HD)
        scores = (
            jnp.einsum("qgsd,kgd->gsqk", query_four, key_three, preferred_element_type=jnp.float32)
            * scale
        )
        return (scores, allowed[None, None], key_three)

    def attend(carry, pair, owner):
        best, running, accum = carry
        scores, allowed, key_three = scores_of(pair[0], owner)
        scores = jnp.where(allowed, scores, NEGATIVE)
        new_best = jnp.maximum(best, jnp.max(scores, axis=3))
        weights = jnp.where(allowed, jnp.exp(scores - new_best[..., None]), 0.0)
        factor = jnp.exp(best - new_best)
        value_three = pair[1].reshape(rows, groups, HD)
        mixed = jnp.einsum(
            "gsqk,kgd->gsqd",
            weights.astype(jnp.bfloat16),
            value_three,
            preferred_element_type=jnp.float32,
        )
        accum = accum * factor[..., None] + mixed
        running = running * factor + jnp.sum(weights, axis=3)
        return (new_best, running, accum)

    own_pair = jnp.stack([keys, values])
    start_carry = (
        jnp.full((groups, share, rows), NEGATIVE, jnp.float32),
        jnp.zeros((groups, share, rows), jnp.float32),
        jnp.zeros((groups, share, rows, HD), jnp.float32),
    )
    first_carry = attend(start_carry, own_pair, myself)

    def forward_step(state, offset):
        pair, carry = state
        pair = from_behind(pair, ("grp", "rep"), 1)
        carry = attend(carry, pair, myself - offset)
        return ((pair, carry), pair)

    (last_pair, final_carry), kept_pairs = lax.scan(forward_step, (own_pair, first_carry), offsets)
    best, running, accum = final_carry
    attn_four = accum / running[..., None]
    log_total = best + jnp.log(running)
    attn_low = jnp.transpose(attn_four, (2, 0, 1, 3)).reshape(rows, width).astype(jnp.bfloat16)
    branch = jnp.dot(attn_low, wo_full, preferred_element_type=jnp.float32)
    resid = x_full + branch
    inv_two = lax.rsqrt(jnp.mean(resid * resid, axis=1, keepdims=True) + EPSILON)
    normed_two = resid * inv_two
    h_two = (normed_two * gain_ffn).astype(jnp.bfloat16)
    gate = jnp.dot(h_two, wg_full, preferred_element_type=jnp.float32)
    upper = jnp.dot(h_two, wu_full, preferred_element_type=jnp.float32)
    sigma = jax.nn.sigmoid(gate)
    swish = gate * sigma
    hidden = (swish * upper).astype(jnp.bfloat16)
    output = (resid + jnp.dot(hidden, wd_full, preferred_element_type=jnp.float32)).astype(
        jnp.bfloat16
    )
    d_output = cotangent.astype(jnp.float32)
    d_wdown = jnp.einsum("tf,td->fd", hidden, cotangent, preferred_element_type=jnp.float32)
    d_hidden = jnp.einsum("td,fd->tf", cotangent, wd_full, preferred_element_type=jnp.float32)
    d_gate = (d_hidden * upper * sigma * (1.0 + gate * (1.0 - sigma))).astype(jnp.bfloat16)
    d_upper = (d_hidden * swish).astype(jnp.bfloat16)
    d_wgate = jnp.einsum("td,tf->df", h_two, d_gate, preferred_element_type=jnp.float32)
    d_wup = jnp.einsum("td,tf->df", h_two, d_upper, preferred_element_type=jnp.float32)
    d_h_two = jnp.einsum("tf,df->td", d_gate, wg_full, preferred_element_type=jnp.float32)
    d_h_two = d_h_two + jnp.einsum(
        "tf,df->td", d_upper, wu_full, preferred_element_type=jnp.float32
    )
    d_gain_two = jnp.sum(d_h_two * normed_two, axis=0)
    scaled_two = d_h_two * gain_ffn
    d_resid = d_output + inv_two * (
        scaled_two - normed_two * jnp.mean(scaled_two * normed_two, axis=1, keepdims=True)
    )
    inner_ffn = (
        lax.psum_scatter(
            d_wgate.astype(jnp.bfloat16), "grp", scatter_dimension=0, tiled=True
        ).astype(jnp.float32),
        lax.psum_scatter(d_wup.astype(jnp.bfloat16), "grp", scatter_dimension=0, tiled=True).astype(
            jnp.float32
        ),
        lax.psum_scatter(
            d_wdown.astype(jnp.bfloat16), "grp", scatter_dimension=0, tiled=True
        ).astype(jnp.float32),
        lax.psum_scatter(
            d_gain_two.astype(jnp.bfloat16), "grp", scatter_dimension=0, tiled=True
        ).astype(jnp.float32),
    )
    ffn_grads = (
        lax.psum_scatter(
            inner_ffn[0].astype(jnp.bfloat16), "rep", scatter_dimension=0, tiled=True
        ).astype(jnp.float32),
        lax.psum_scatter(
            inner_ffn[1].astype(jnp.bfloat16), "rep", scatter_dimension=0, tiled=True
        ).astype(jnp.float32),
        lax.psum_scatter(
            inner_ffn[2].astype(jnp.bfloat16), "rep", scatter_dimension=0, tiled=True
        ).astype(jnp.float32),
        lax.psum_scatter(
            inner_ffn[3].astype(jnp.bfloat16), "rep", scatter_dimension=0, tiled=True
        ).astype(jnp.float32),
    )
    d_branch = d_resid.astype(jnp.bfloat16)
    d_wout = jnp.einsum("td,te->de", attn_low, d_branch, preferred_element_type=jnp.float32)
    d_attn = jnp.einsum("te,de->td", d_branch, wo_full, preferred_element_type=jnp.float32).astype(
        jnp.bfloat16
    )
    d_attn_four = jnp.transpose(d_attn.reshape(rows, groups, share, HD), (1, 2, 0, 3))
    delta = jnp.sum(d_attn_four.astype(jnp.float32) * attn_four, axis=3)

    def attend_back(pair, owner):
        scores, allowed, key_three = scores_of(pair[0], owner)
        probs = jnp.where(allowed, jnp.exp(scores - log_total[..., None]), 0.0)
        value_three = pair[1].reshape(rows, groups, HD)
        d_probs = jnp.einsum(
            "gsqd,kgd->gsqk", d_attn_four, value_three, preferred_element_type=jnp.float32
        )
        d_scores = (probs * (d_probs - delta[..., None])).astype(jnp.bfloat16)
        d_query_piece = scale * jnp.einsum(
            "gsqk,kgd->gsqd", d_scores, key_three, preferred_element_type=jnp.float32
        )
        d_key_piece = scale * jnp.einsum(
            "gsqk,qgsd->kgd", d_scores, query_four, preferred_element_type=jnp.float32
        )
        d_value_piece = jnp.einsum(
            "gsqk,gsqd->kgd",
            probs.astype(jnp.bfloat16),
            d_attn_four,
            preferred_element_type=jnp.float32,
        )
        both = jnp.stack(
            [d_key_piece.reshape(rows, kv_width), d_value_piece.reshape(rows, kv_width)]
        )
        return (d_query_piece, both)

    def backward_step(state, items):
        d_query_acc, travelling = state
        offset, pair = items
        d_query_piece, both = attend_back(pair, myself - offset)
        travelling = from_behind(
            (travelling + both).astype(jnp.bfloat16), ("grp", "rep"), -1
        ).astype(jnp.float32)
        return ((d_query_acc + d_query_piece, travelling), None)

    back_start = (
        jnp.zeros((groups, share, rows, HD), jnp.float32),
        jnp.zeros((2, rows, kv_width), jnp.float32),
    )
    (d_query_acc, travelling), unused = lax.scan(
        backward_step, back_start, (offsets, kept_pairs), reverse=True
    )
    own_query, own_both = attend_back(own_pair, myself)
    d_query_acc = d_query_acc + own_query
    kv_grads = travelling + own_both
    d_query = jnp.transpose(d_query_acc, (2, 0, 1, 3)).reshape(rows, width).astype(jnp.bfloat16)
    d_wquery = jnp.einsum("td,te->de", h_one, d_query, preferred_element_type=jnp.float32)
    d_h_one = jnp.einsum("te,de->td", d_query, wq_full, preferred_element_type=jnp.float32)
    d_gain_one = jnp.sum(d_h_one * normed_one, axis=0)
    scaled_one = d_h_one * gain_attn
    d_tokens = (
        d_resid
        + inv_one
        * (scaled_one - normed_one * jnp.mean(scaled_one * normed_one, axis=1, keepdims=True))
    ).astype(jnp.bfloat16)
    inner_attn = (
        lax.psum_scatter(
            d_wquery.astype(jnp.bfloat16), "grp", scatter_dimension=0, tiled=True
        ).astype(jnp.float32),
        lax.psum_scatter(
            d_wout.astype(jnp.bfloat16), "grp", scatter_dimension=0, tiled=True
        ).astype(jnp.float32),
        lax.psum_scatter(
            d_gain_one.astype(jnp.bfloat16), "grp", scatter_dimension=0, tiled=True
        ).astype(jnp.float32),
    )
    attn_grads = (
        lax.psum_scatter(
            inner_attn[0].astype(jnp.bfloat16), "rep", scatter_dimension=0, tiled=True
        ).astype(jnp.float32),
        lax.psum_scatter(
            inner_attn[1].astype(jnp.bfloat16), "rep", scatter_dimension=0, tiled=True
        ).astype(jnp.float32),
        lax.psum_scatter(
            inner_attn[2].astype(jnp.bfloat16), "rep", scatter_dimension=0, tiled=True
        ).astype(jnp.float32),
    )
    return (
        output,
        d_tokens,
        attn_grads[2],
        ffn_grads[3],
        attn_grads[0],
        attn_grads[1],
        ffn_grads[0],
        ffn_grads[1],
        ffn_grads[2],
        kv_grads[0].astype(jnp.bfloat16),
        kv_grads[1].astype(jnp.bfloat16),
    )


def solution(mesh):
    in_specs = (
        P(("grp", "rep"), None),
        P(("grp", "rep"), None),
        P(),
        P(),
        P("grp", None),
        P("grp", None),
        P("grp", None),
        P("grp", None),
        P("grp", None),
        P(("grp", "rep"), None),
        P(("grp", "rep"), None),
        P(),
    )
    out_specs = (
        P(("grp", "rep"), None),
        P(("grp", "rep"), None),
        P(("grp", "rep")),
        P(("grp", "rep")),
        P(("grp", "rep"), None),
        P(("grp", "rep"), None),
        P(("grp", "rep"), None),
        P(("grp", "rep"), None),
        P(("grp", "rep"), None),
        P(("grp", "rep"), None),
        P(("grp", "rep"), None),
    )
    return jax.shard_map(
        on_device, mesh=mesh, in_specs=in_specs, out_specs=out_specs, check_vma=False
    )
```

profile of v0, /device:TPU:0, one launch (start us, length us, event | category | flops | bytes accessed | tf_op | source)
XLA Modules:
  0.0 1965.1 jit_solution(13861435718509080366)
XLA Ops:
  14.9 55.7 %all-gather.6.cloned.1.call-done = bf16[2048,2048]{1,0:T(8,128)(2,1)} async-done(((bf16[512,2048]{1,0:T(8,128)(2,1)}), bf16[2048,2048]{1,0:T(8,128)(2,1)}) %all-gather.6.cloned.1.call-update) | async-done | bytes 8388624 | tf_op jit(solution)/shard_map/all_gather | solution.py:50
  79.8 228.5 %while.39 = (s32[]{:T(128)}, bf16[2,128,512]{1,2,0:T(8,128)(2,1)}, f32[4,4,128]{2,1,0:T(4,128)S(1)}, f32[4,4,128]{2,1,0:T(4,128)S(1)}, f32[4,4,128,128]{3,2,1,0:...) while((s32[]{:T(128)}, bf16[2,128,512]{1,2,0:T(8,128)(2,1)}, ...), condition=%wide.region_8.9_spmd.clone, body=%wide.region_4.8_spmd.clone.sunk | while | flops 137157888 | bytes 8854817 | solution.py:111
  320.2 13.7 fusion.75
  333.9 108.9 %all-gather.12.cloned.1.call-done = bf16[2048,5504]{1,0:T(8,128)(2,1)} async-done(((bf16[512,5504]{1,0:T(8,128)(2,1)}), bf16[2048,5504]{1,0:T(8,128)(2,1)}) %all-gather.12.cloned.1.call-update) | async-done | bytes 22544400 | tf_op jit(solution)/shard_map/all_gather | solution.py:53
  442.9 12.7 fusion.76
  455.6 129.0 %all-gather.14.cloned.1.call-done = bf16[5504,2048]{1,0:T(8,128)(2,1)} async-done(((bf16[1376,2048]{1,0:T(8,128)(2,1)}), bf16[5504,2048]{1,0:T(8,128)(2,1)}) %all-gather.14.cloned.1.call-update) | async-done | bytes 22544400 | tf_op jit(solution)/shard_map/all_gather | solution.py:54
  584.7 15.1 multiply_convert_fusion
  599.7 12.0 fusion.77
  611.7 13.9 multiply_reduce_fusion
  643.4 306.3 %while.40 = (s32[]{:T(128)}, f32[4,4,128,128]{3,2,1,0:T(8,128)S(1)}, f32[2,128,512]{1,2,0:T(8,128)}, s32[8]{0:T(128)}, s32[16]{0:T(128)}, /*index=5*/s32[]{:T(12...) while((s32[]{:T(128)}, ...), condition=%wide.region_14.15_spmd.clone, body=%wide.region_12.14_spmd.clone.sunk | while | flops 338939136 | bytes 15652192 | solution.py:219
  899.6 9.5 collective-permute-done.1
  962.0 11.9 convolution_convert_fusion.2
  974.0 13.8 convolution_convert_fusion.1
  989.6 12.4 convolution_convert_fusion
  1002.8 46.7 %reduce-scatter.12.cloned.1.call-done = bf16[512,2048]{1,0:T(8,128)(2,1)} async-done(((bf16[2048,2048]{1,0:T(8,128)(2,1)}), bf16[512,2048]{1,0:T(8,128)(2,1)}) %reduce-scatter.12.cloned.1.call-update) | async-done | bytes 2097168 | tf_op jit(solution)/shard_map/reduce_scatter | solution.py:236
  1049.5 165.9 %reduce-scatter.20.cloned.1.call-done = bf16[512,5504]{1,0:T(8,128)(2,1)} async-done(((bf16[2048,5504]{1,0:T(8,128)(2,1)}), bf16[512,5504]{1,0:T(8,128)(2,1)}) %reduce-scatter.20.cloned.1.call-update) | async-done | bytes 5636112 | tf_op jit(solution)/shard_map/reduce_scatter | solution.py:146
  1215.6 166.1 %reduce-scatter.24.cloned.1.call-done = bf16[512,5504]{1,0:T(8,128)(2,1)} async-done(((bf16[2048,5504]{1,0:T(8,128)(2,1)}), bf16[512,5504]{1,0:T(8,128)(2,1)}) %reduce-scatter.24.cloned.1.call-update) | async-done | bytes 5636112 | tf_op jit(solution)/shard_map/reduce_scatter | solution.py:149
  1397.2 16.9 fusion.27
  1414.2 133.4 %reduce-scatter.28.cloned.1.call-done = bf16[1376,2048]{1,0:T(8,128)(2,1)} async-done(((bf16[5504,2048]{1,0:T(8,128)(2,1)}), bf16[1376,2048]{1,0:T(8,128)(2,1)}) %reduce-scatter.28.cloned.1.call-update) | async-done | bytes 5636112 | tf_op jit(solution)/shard_map/reduce_scatter | solution.py:152
  1547.6 138.1 %fusion.4 = bf16[176,2048]{1,0:T(8,128)(2,1)S(1)} fusion(bf16[1376,2048]{1,0:T(8,128)(2,1)} %reduce-scatter.28.cloned.1.call-done), kind=kCustom, calls=%all-reduce-scatter | all-reduce-scatter fusion | flops 2883585 | bytes 6357504
  1693.8 20.7 %all-reduce.6 = (bf16[512]{0:T(512)(128)(2,1)S(1)}, bf16[512]{0:T(512)(128)(2,1)S(1)}) all-reduce(bf16[512]{0:T(512)(128)(2,1)S(1)} %dynamic-slice.1, bf16[512]{0:T(512)(128)(2,1)S(1)} %dynamic-slice.5), channel_id=3, replica_groups=mesh['grp'=4,'rep'=8] {'rep'}, use_global_device_ids=true, to_apply=%region_18.19.clone | all-reduce | flops 1024 | bytes 4096
  1716.8 15.7 reduce-scatter.14.cloned.1.call-done
  1737.1 106.8 %reduce-scatter.22.cloned.1.call-done = bf16[64,5504]{1,0:T(8,128)(2,1)} async-done(((bf16[512,5504]{1,0:T(8,128)(2,1)}), bf16[64,5504]{1,0:T(8,128)(2,1)}) %reduce-scatter.22.cloned.1.call-update) | async-done | bytes 704528 | tf_op jit(solution)/shard_map/reduce_scatter | solution.py:160
  1846.2 109.6 %reduce-scatter.26.cloned.1.call-done = bf16[64,5504]{1,0:T(8,128)(2,1)} async-done(((bf16[512,5504]{1,0:T(8,128)(2,1)}), bf16[64,5504]{1,0:T(8,128)(2,1)}) %reduce-scatter.26.cloned.1.call-update) | async-done | bytes 704528 | tf_op jit(solution)/shard_map/reduce_scatter | solution.py:163
  (719 shorter events, 595.5 us)
Async XLA Ops:
  7.2 63.4 %all-gather.6.cloned.1.call-start = ((), (), s32[]{:S(2)}) async-start(), calls=%async_computation.9 | async-start | bytes 10485760 | tf_op jit(solution)/shard_map/all_gather | solution.py:50
  7.9 304.0 %all-gather.8.cloned.1.call-start = ((), (), s32[]{:S(2)}) async-start(), calls=%async_computation.10 | async-start | bytes 10485760 | tf_op jit(solution)/shard_map/all_gather | solution.py:51
  8.7 311.6 %all-gather.10.cloned.1.call-start = ((), (), s32[]{:S(2)}) async-start(), calls=%async_computation.11 | async-start | bytes 28180480 | tf_op jit(solution)/shard_map/all_gather | solution.py:52
  9.4 433.5 %all-gather.12.cloned.1.call-start = ((), (), s32[]{:S(2)}) async-start(), calls=%async_computation.12 | async-start | bytes 28180480 | tf_op jit(solution)/shard_map/all_gather | solution.py:53
  10.0 574.6 %all-gather.14.cloned.1.call-start = ((), (), s32[]{:S(2)}) async-start(), calls=%async_computation.13 | async-start | bytes 28180480 | tf_op jit(solution)/shard_map/all_gather | solution.py:54
  10.6 991.5 %reduce-scatter.16.cloned.1.call-start = ((), (), s32[]{:S(2)}) async-start(), calls=%async_computation.16 | async-start | bytes 10485760 | tf_op jit(solution)/shard_map/reduce_scatter | solution.py:239
  93.7 11.0 collective-permute-start
  134.3 10.8 collective-permute-start
  149.0 11.1 collective-permute-start
  164.0 10.9 collective-permute-start
  178.7 11.0 collective-permute-start
  642.8 406.7 %reduce-scatter.12.cloned.1.call-start = ((), (), s32[]{:S(2)}) async-start(), calls=%async_computation.14 | async-start | bytes 10485760 | tf_op jit(solution)/shard_map/reduce_scatter | solution.py:236
  706.6 10.7 collective-permute-start.1
  897.9 11.3 collective-permute-start.1
  917.6 11.2 collective-permute-start.1
  937.2 10.8 collective-permute-start.1
  961.0 254.4 %reduce-scatter.20.cloned.1.call-start = ((), (), s32[]{:S(2)}) async-start(), calls=%async_computation.18 | async-start | bytes 28180480 | tf_op jit(solution)/shard_map/reduce_scatter | solution.py:146
  974.0 407.7 %reduce-scatter.24.cloned.1.call-start = ((), (), s32[]{:S(2)}) async-start(), calls=%async_computation.20 | async-start | bytes 28180480 | tf_op jit(solution)/shard_map/reduce_scatter | solution.py:149
  987.9 559.7 %reduce-scatter.28.cloned.1.call-start = ((), (), s32[]{:S(2)}) async-start(), calls=%async_computation.22 | async-start | bytes 28180480 | tf_op jit(solution)/shard_map/reduce_scatter | solution.py:152
  1002.0 713.0 %reduce-scatter.18.cloned.1.call-start = ((), (), s32[]{:S(2)}) async-start(), calls=%async_computation.17 | async-start | bytes 2359296 | tf_op jit(solution)/shard_map/reduce_scatter | solution.py:250
  1002.7 729.8 %reduce-scatter.14.cloned.1.call-start = ((), (), s32[]{:S(2)}) async-start(), calls=%async_computation.15 | async-start | bytes 2359296 | tf_op jit(solution)/shard_map/reduce_scatter | solution.py:247
  1049.5 794.4 %reduce-scatter.22.cloned.1.call-start = ((), (), s32[]{:S(2)}) async-start(), calls=%async_computation.19 | async-start | bytes 6340608 | tf_op jit(solution)/shard_map/reduce_scatter | solution.py:160
  1215.5 740.3 %reduce-scatter.26.cloned.1.call-start = ((), (), s32[]{:S(2)}) async-start(), calls=%async_computation.21 | async-start | bytes 6340608 | tf_op jit(solution)/shard_map/reduce_scatter | solution.py:163
  1685.7 48.6 %collective-permute-start.2 = (bf16[28,2048]{1,0:T(8,128)(2,1)S(1)}, bf16[28,2048]{1,0:T(8,128)(2,1)S(1)}, u32[]{:S(2)}, u32[]{:S(2)}) collective-permute-start(bf16[28,2048]{1,0:T(8,128)(2,1)S(1)} %slice.52), channel_id=1, source_target_pairs={{0,1},{1,2},{2,3},{3,4},{4,5},{5,6},{6,7},{8,9},{9,10},{10,11},{11... | collective-permute-start | bytes 344072
  (86 other events, 1886.5 us)
Sparse Core Ops, SparseCore 0:
  9.6 60.9 all-gather.5
  72.2 62.8 all-gather.7
  136.7 163.8 all-gather.9
  302.0 140.8 all-gather.11
  444.3 140.3 all-gather.13
  642.9 71.7 reduce-scatter.15
  961.1 88.2 reduce-scatter.11
  1052.1 163.3 reduce-scatter.19
  1218.3 163.3 reduce-scatter.23
  1384.2 163.3 reduce-scatter.27
  1551.5 105.2 reduce-scatter.17
  1660.7 71.8 reduce-scatter.13
  1736.6 107.2 reduce-scatter.21
  1847.8 107.9 reduce-scatter.25
where the time goes:
time: 1970 us
  waiting for transfers between devices  1190 us (60%)
  matrix products  230 us (12%)
  blocking collectives  165 us (8%)
  other arithmetic  133 us (7%)
  starting transfers between devices  107 us (5%)
  local copies, waits for them, and re-layouts  103 us (5%)
  loops' own time  24 us (1%)
    reduce_scatter x1, waiting for transfers between devices, on_device(): lax.psum_scatter(d_wup.astype(jnp.bfloat16), 'grp', scatter_dimension=0,...  166 us
    reduce_scatter x1, waiting for transfers between devices, on_device(): lax.psum_scatter(d_wgate.astype(jnp.bfloat16), 'grp', scatter_dimension=0...  166 us
    unnamed x3, blocking collectives  165 us
    ppermute x32, waiting for transfers between devices, from_behind(): return lax.ppermute(value, axis, pairs)  146 us
    reduce_scatter x1, waiting for transfers between devices, on_device(): lax.psum_scatter(d_wdown.astype(jnp.bfloat16), 'grp', scatter_dimension=0...  133 us
    all_gather x1, waiting for transfers between devices, on_device(): lax.all_gather(w_down, 'grp', axis=0, tiled=True)  129 us
    reduce_scatter x1, waiting for transfers between devices, on_device(): lax.psum_scatter(inner_ffn[1].astype(jnp.bfloat16), 'rep', scatter_dimens...  110 us
    all_gather x1, waiting for transfers between devices, on_device(): lax.all_gather(w_up, 'grp', axis=0, tiled=True)  109 us
  transfers between devices with their start and end apart: 47, of which 28 were waited for; matrix products, arithmetic and copies ran while one was open for 27% of the time, Pallas kernels for 0%

commit v1 on v0

v1 whole, which is shorter than its diff:
```python
import functools

import jax
import jax.numpy as jnp
from jax import lax
from jax.experimental import pallas as pl
from jax.experimental.pallas import tpu as pltpu
from jax.sharding import PartitionSpec as P

HD = 128
EPSILON = 1e-06
NEGATIVE = -1e30
F32 = jnp.float32
BF16 = jnp.bfloat16
BOTH = ("grp", "rep")


def swap(value, mask):
    count = lax.axis_size(BOTH)
    return lax.ppermute(value, BOTH, [(i, i ^ mask) for i in range(count)])


def after(value, *earlier):
    return lax.optimization_barrier((value,) + earlier)[0]


def dot(a, b):
    return jnp.dot(a, b, preferred_element_type=F32)


def dot_t(a, b):
    return lax.dot_general(a, b, (((1,), (1,)), ((), ())), preferred_element_type=F32)


def t_dot(a, b):
    return lax.dot_general(a, b, (((0,), (0,)), ((), ())), preferred_element_type=F32)


def pick(value, index, axis):
    return lax.dynamic_index_in_dim(value, index, axis, keepdims=False)


def gather_four(block, core, yy):
    over_y = swap(block, yy)
    over_c = swap(block, core)
    diagonal = swap(over_y, core)
    return jnp.stack([block, over_c, over_y, diagonal])


def scatter_four(parts, core, yy):
    parts = parts.reshape((2, 2) + parts.shape[1:])
    got = swap(parts[:, 1].astype(BF16), core)
    parts = parts[:, 0] + got.astype(F32)
    got = swap(parts[1].astype(BF16), yy)
    return parts[0] + got.astype(F32)


def gather_eight(block, core, yy, zz):
    half = block.shape[0] // 2
    over_y = swap(block, yy)
    over_z = swap(block, zz)
    low = swap(over_y[:half], zz)
    high = swap(over_z[half:], yy)
    near = jnp.stack([block, over_y])
    far = jnp.stack([over_z, jnp.concatenate([low, high])])
    near_c = swap(near, core)
    far_c = swap(far, core)
    whole = jnp.stack([jnp.stack([near, near_c], 1), jnp.stack([far, far_c], 1)])
    return whole.reshape((8,) + block.shape)


def scatter_eight(parts, core, yy, zz):
    rows = parts.shape[1]
    half = rows // 2
    parts = parts.reshape((2, 2, 2) + parts.shape[1:])
    got = swap(parts[:, :, 1].astype(BF16), core)
    parts = parts[:, :, 0] + got.astype(F32)
    corner = parts[1, 1].astype(BF16)
    to_z = swap(corner[:half], yy)
    to_y = swap(corner[half:], zz)
    for_z = jnp.concatenate([parts[1, 0, :half] + to_z.astype(F32), parts[1, 0, half:]])
    for_y = jnp.concatenate([parts[0, 1, :half], parts[0, 1, half:] + to_y.astype(F32)])
    from_z = swap(for_z.astype(BF16), zz)
    from_y = swap(for_y.astype(BF16), yy)
    return parts[0, 0] + from_z.astype(F32) + from_y.astype(F32)


def exchange_four(pieces, core, yy):
    from_y = swap(jnp.stack([pieces[2], pieces[3]]), yy)
    from_c = swap(jnp.stack([pieces[1], from_y[1]]), core)
    return [pieces[0], from_c[0], from_y[0], from_c[1]]


def absolute(pieces, g):
    odd, upper = (g & 1) == 1, (g >> 1) == 1
    a = jnp.where(odd, pieces[1], pieces[0])
    b = jnp.where(odd, pieces[0], pieces[1])
    c = jnp.where(odd, pieces[3], pieces[2])
    d = jnp.where(odd, pieces[2], pieces[3])
    return [
        jnp.where(upper, c, a),
        jnp.where(upper, d, b),
        jnp.where(upper, a, c),
        jnp.where(upper, b, d),
    ]


def halve(value, bit, mask, axis):
    got = swap(pick(value, 1 - bit, axis).astype(BF16), mask)
    return pick(value, bit, axis).astype(F32) + got.astype(F32)


def block_bounds(info_ref, starts_ref, j, reps):
    place = ((info_ref[0] ^ j) * reps + info_ref[1]) * HD
    docs = starts_ref.shape[0]
    first = jnp.int32(0)
    for d in range(docs):
        first = jnp.maximum(first, jnp.where(starts_ref[d] <= place, starts_ref[d], 0))
    position = place + lax.broadcasted_iota(jnp.int32, (4, HD, 1), 1).reshape(4 * HD, 1)
    lowest = jnp.zeros_like(position)
    for d in range(docs):
        lowest = jnp.maximum(lowest, jnp.where(starts_ref[d] <= position, starts_ref[d], 0))
    return place, first, position, lowest


def key_tile(info_ref, kv_ref, tile, reps):
    per = reps // 4
    member = (tile // per) ^ info_ref[0]
    piece = kv_ref[pl.ds(4 * (tile % per), 4), member]
    piece = piece.reshape(4 * HD, 2 * HD)
    return piece[:, :HD], piece[:, HD:]


def head_rows(ref):
    return jnp.concatenate([ref[0, :, h * HD : (h + 1) * HD] for h in range(4)], axis=0)


def attend_kernel(reps, info_ref, starts_ref, q_ref, kv_ref, o_ref, lse_ref):
    j = pl.program_id(0)
    place, first, position, lowest = block_bounds(info_ref, starts_ref, j, reps)
    query = head_rows(q_ref)
    rows = 4 * HD
    scale = HD ** (-0.5)

    def step(tile, carry):
        best, total, accum = carry
        key, value = key_tile(info_ref, kv_ref, tile, reps)
        scores = dot_t(query, key) * scale
        at = tile * 512 + lax.broadcasted_iota(jnp.int32, (1, 512), 1)
        scores = jnp.where((at >= lowest) & (at <= position), scores, NEGATIVE)
        new_best = jnp.maximum(best, jnp.max(scores, axis=1, keepdims=True))
        weights = jnp.exp(scores - new_best)
        factor = jnp.exp(best - new_best)
        total = total * factor + jnp.sum(weights, axis=1, keepdims=True)
        accum = accum * factor + dot(weights.astype(BF16), value)
        return new_best, total, accum

    init = (
        jnp.full((rows, 1), NEGATIVE, F32),
        jnp.zeros((rows, 1), F32),
        jnp.zeros((rows, HD), F32),
    )
    best, total, accum = lax.fori_loop(first // 512, place // 512 + 1, step, init)
    out = accum / total
    for h in range(4):
        o_ref[0, :, h * HD : (h + 1) * HD] = out[h * HD : (h + 1) * HD].astype(BF16)
    lse_ref[0] = best + jnp.log(total)


def attend(info, starts, query, kv):
    reps = kv.shape[0]
    return pl.pallas_call(
        functools.partial(attend_kernel, reps),
        grid=(4,),
        in_specs=[
            pl.BlockSpec(memory_space=pltpu.SMEM),
            pl.BlockSpec(memory_space=pltpu.SMEM),
            pl.BlockSpec((1, HD, 4 * HD), lambda j: (j, 0, 0)),
            pl.BlockSpec(kv.shape, lambda j: (0, 0, 0, 0)),
        ],
        out_specs=[
            pl.BlockSpec((1, HD, 4 * HD), lambda j: (j, 0, 0)),
            pl.BlockSpec((1, 4 * HD, 1), lambda j: (j, 0, 0)),
        ],
        out_shape=[
            jax.ShapeDtypeStruct((4, HD, 4 * HD), BF16),
            jax.ShapeDtypeStruct((4, 4 * HD, 1), F32),
        ],
        compiler_params=pltpu.CompilerParams(vmem_limit_bytes=48 << 20),
        name="attend",
    )(info, starts, query, kv)


def attend_back_kernel(
    reps, info_ref, starts_ref, q_ref, do_ref, o_ref, lse_ref, kv_ref, dq_ref, dkv_ref, sums
):
    j = pl.program_id(0)

    @pl.when(j == 0)
    def _():
        sums[...] = jnp.zeros_like(sums)

    place, first, position, lowest = block_bounds(info_ref, starts_ref, j, reps)
    query = head_rows(q_ref)
    d_out = head_rows(do_ref)
    out = head_rows(o_ref)
    lse = lse_ref[0]
    delta = jnp.sum(d_out.astype(F32) * out.astype(F32), axis=1, keepdims=True)
    scale = HD ** (-0.5)
    per = reps // 4

    def step(tile, d_query):
        key, value = key_tile(info_ref, kv_ref, tile, reps)
        scores = dot_t(query, key) * scale
        at = tile * 512 + lax.broadcasted_iota(jnp.int32, (1, 512), 1)
        probs = jnp.where((at >= lowest) & (at <= position), jnp.exp(scores - lse), 0.0)
        d_probs = dot_t(d_out, value)
        d_scores = (probs * (d_probs - delta)).astype(BF16)
        d_query = d_query + dot(d_scores, key)
        d_key = t_dot(d_scores, query) * scale
        d_value = t_dot(probs.astype(BF16), d_out)
        where = (pl.ds(4 * (tile % per), 4), (tile // per) ^ info_ref[0])
        both = jnp.concatenate([d_key, d_value], axis=1)
        sums[where] = sums[where] + both.reshape(4, HD, 2 * HD)
        return d_query

    d_query = lax.fori_loop(
        first // 512, place // 512 + 1, step, jnp.zeros((4 * HD, HD), F32)
    )
    d_query = (d_query * scale).astype(BF16)
    for h in range(4):
        dq_ref[0, :, h * HD : (h + 1) * HD] = d_query[h * HD : (h + 1) * HD]

    @pl.when(j == 3)
    def _():
        dkv_ref[...] = sums[...].astype(BF16)


def attend_back(info, starts, query, d_out, out, lse, kv):
    reps = kv.shape[0]
    rows = pl.BlockSpec((1, HD, 4 * HD), lambda j: (j, 0, 0))
    whole = pl.BlockSpec(kv.shape, lambda j: (0, 0, 0, 0))
    return pl.pallas_call(
        functools.partial(attend_back_kernel, reps),
        grid=(4,),
        in_specs=[
            pl.BlockSpec(memory_space=pltpu.SMEM),
            pl.BlockSpec(memory_space=pltpu.SMEM),
            rows,
            rows,
            rows,
            pl.BlockSpec((1, 4 * HD, 1), lambda j: (j, 0, 0)),
            whole,
        ],
        out_specs=[rows, whole],
        out_shape=[
            jax.ShapeDtypeStruct((4, HD, 4 * HD), BF16),
            jax.ShapeDtypeStruct(kv.shape, BF16),
        ],
        scratch_shapes=[pltpu.VMEM(kv.shape, F32)],
        compiler_params=pltpu.CompilerParams(vmem_limit_bytes=60 << 20),
        name="attend_back",
    )(info, starts, query, d_out, out, lse, kv)


def on_device(
    tokens,
    cotangent,
    gain_attn,
    gain_ffn,
    w_query,
    w_out,
    w_gate,
    w_up,
    w_down,
    keys,
    values,
    starts,
):
    reps = lax.axis_size("rep")
    rows, width = tokens.shape
    hidden_all = w_gate.shape[1]
    g = lax.axis_index("grp")
    r = lax.axis_index("rep")
    core, yy, xx, zz = reps, 2 * reps, 1, 2
    high = [1 << k for k in range(2, 16) if (1 << k) < reps]
    outer = reps // 4
    x_bit, z_bit = r & 1, (r >> 1) & 1
    share = width // 4
    out_rows = width // (4 * reps)
    chunk = hidden_all // (4 * reps)
    run = 2 * chunk
    mine = outer * run
    info = jnp.stack([g, r]).astype(jnp.int32)

    x_full = tokens.astype(F32)
    inv_one = lax.rsqrt(jnp.mean(x_full * x_full, axis=1, keepdims=True) + EPSILON)
    normed_one = x_full * inv_one
    h_one = (normed_one * gain_attn).astype(BF16)

    kv_parts = [
        jnp.concatenate(
            [
                lax.dynamic_slice_in_dim(keys, (g ^ j) * HD, HD, 1),
                lax.dynamic_slice_in_dim(values, (g ^ j) * HD, HD, 1),
            ],
            axis=1,
        )
        for j in range(4)
    ]
    kv_own = jnp.stack(exchange_four(kv_parts, core, yy))
    kv = lax.all_gather(kv_own, "rep", axis=0, tiled=False)

    h_group = gather_four(h_one, core, yy).reshape(4 * rows, width)
    wq_parts = exchange_four(
        [lax.dynamic_slice_in_dim(w_query, (g ^ j) * share, share, 1) for j in range(4)], core, yy
    )
    wq_cols = jnp.concatenate(absolute(wq_parts, g), axis=0)
    query = dot(h_group, wq_cols).astype(BF16).reshape(4, rows, share)

    def columns(weight):
        def of(member, bit):
            base = member * (hidden_all // 4)
            return jnp.concatenate(
                [
                    weight[:, base + o * 2 * run + bit * run : base + o * 2 * run + (bit + 1) * run]
                    for o in range(outer)
                ],
                axis=1,
            )

        packed = jnp.stack([jnp.where(z_bit == 1, of(m, 1), of(m, 0)) for m in range(4)])
        packed = after(packed, h_group, wq_cols)
        got = exchange_four([pick(packed, g ^ j, 0) for j in range(4)], core, yy)
        return jnp.concatenate(absolute(got, g), axis=0)

    wg = columns(w_gate)
    wu = columns(w_up)
    wd = pick(w_down.reshape(outer, 2, run, width), z_bit, 1).reshape(mine, width)
    dy_group = gather_eight(after(cotangent, query), core, yy, zz).reshape(8 * rows, width)

    attn, lse = attend(info, starts, query, kv)
    attn_rows = attn.reshape(4 * rows, share)
    branch = scatter_four(dot(attn_rows, w_out).reshape(4, rows, width), core, yy)
    resid = x_full + branch
    inv_two = lax.rsqrt(jnp.mean(resid * resid, axis=1, keepdims=True) + EPSILON)
    normed_two = resid * inv_two
    h_two = (normed_two * gain_ffn).astype(BF16)

    h_eight = gather_eight(h_two, core, yy, zz).reshape(8 * rows, width)
    d_hidden = dot_t(dy_group, wd)
    gate = dot(h_eight, wg)
    upper = dot(h_eight, wu)
    sigma = jax.nn.sigmoid(gate)
    swish = gate * sigma
    hidden = (swish * upper).astype(BF16)
    d_gate = (d_hidden * upper * sigma * (1.0 + gate * (1.0 - sigma))).astype(BF16)
    d_upper = (d_hidden * swish).astype(BF16)
    d_h_parts = dot_t(d_gate, wg) + dot_t(d_upper, wu)
    d_h_two = scatter_eight(d_h_parts.reshape(8, rows, width), core, yy, zz)

    d_wdown = t_dot(hidden, dy_group).reshape(outer, 2, chunk, width)
    d_wdown = halve(d_wdown, x_bit, xx, 1)
    d_wg = t_dot(h_eight, d_gate).reshape(4 * outer * 2, 2, out_rows, mine)
    d_wg = halve(d_wg, x_bit, xx, 1)
    d_wu = t_dot(h_eight, d_upper).reshape(4 * outer * 2, 2, out_rows, mine)
    d_wu = halve(d_wu, x_bit, xx, 1)
    d_gu = jnp.stack([d_wg, d_wu]).reshape(2, 4, outer, 2, out_rows, mine)
    size = outer
    for mask in reversed(high):
        size //= 2
        bit = (r & mask) // mask
        d_wdown = halve(d_wdown.reshape(2, size, chunk, width), bit, mask, 0)
        d_gu = halve(d_gu.reshape(2, 4, 2, size, 2, out_rows, mine), bit, mask, 2)
    d_wdown = d_wdown.reshape(chunk, width)
    d_gu = d_gu.reshape(2, 4, 2, out_rows, mine).astype(BF16)
    other = swap(pick(d_gu, 1 - z_bit, 2), zz)
    d_gu = jnp.stack([pick(d_gu, z_bit, 2), other], axis=2)
    got = exchange_four([pick(d_gu, g ^ j, 1) for j in range(4)], core, yy)
    got = absolute(got, g)

    def assemble(which):
        out = []
        for member in range(4):
            near, far = got[member][which, 0], got[member][which, 1]
            low = jnp.where(z_bit == 0, near, far)
            upp = jnp.where(z_bit == 0, far, near)
            for o in range(outer):
                out.append(low[:, o * run : (o + 1) * run])
                out.append(upp[:, o * run : (o + 1) * run])
        return jnp.concatenate(out, axis=1).astype(F32)

    d_wgate, d_wup = assemble(0), assemble(1)

    output = (
        resid + scatter_eight(dot(hidden, wd).reshape(8, rows, width), core, yy, zz)
    ).astype(BF16)

    d_gain_two = jnp.sum(d_h_two * normed_two, axis=0)
    scaled_two = d_h_two * gain_ffn
    d_resid = cotangent.astype(F32) + inv_two * (
        scaled_two - normed_two * jnp.mean(scaled_two * normed_two, axis=1, keepdims=True)
    )

    d_group = gather_four(d_resid.astype(BF16), core, yy).reshape(4 * rows, width)
    d_attn = dot_t(d_group, w_out).astype(BF16).reshape(4, rows, share)
    d_query, d_kv = attend_back(info, starts, query, d_attn, attn, lse, kv)
    d_query = d_query.reshape(4 * rows, share)
    d_h_one = scatter_four(dot_t(d_query, wq_cols).reshape(4, rows, width), core, yy)
    d_wout = lax.psum_scatter(
        t_dot(attn_rows, d_group).astype(BF16), "rep", scatter_dimension=0, tiled=True
    ).astype(F32)
    d_kv = lax.psum_scatter(d_kv, "rep", scatter_dimension=0, tiled=False)
    d_kv = absolute(exchange_four([d_kv[j] for j in range(4)], core, yy), g)
    d_keys = jnp.concatenate([piece[:, :HD] for piece in d_kv], axis=1)
    d_values = jnp.concatenate([piece[:, HD:] for piece in d_kv], axis=1)
    d_wq = t_dot(h_group, d_query).astype(BF16).reshape(4, reps, out_rows, share)
    d_wq = lax.psum_scatter(jnp.swapaxes(d_wq, 0, 1), "rep", scatter_dimension=0, tiled=False)
    d_wq = absolute(exchange_four([pick(d_wq, g ^ j, 0) for j in range(4)], core, yy), g)
    d_wquery = jnp.concatenate(d_wq, axis=1).astype(F32)

    d_gain_one = jnp.sum(d_h_one * normed_one, axis=0)
    scaled_one = d_h_one * gain_attn
    d_tokens = (
        d_resid
        + inv_one
        * (scaled_one - normed_one * jnp.mean(scaled_one * normed_one, axis=1, keepdims=True))
    ).astype(BF16)
    gains = jnp.stack(
        [d_gain_one.reshape(4 * reps, out_rows), d_gain_two.reshape(4 * reps, out_rows)], axis=1
    )
    gains = lax.psum_scatter(gains, BOTH, scatter_dimension=0, tiled=False)
    return (
        output,
        d_tokens,
        gains[0],
        gains[1],
        d_wquery,
        d_wout,
        d_wgate,
        d_wup,
        d_wdown,
        d_keys,
        d_values,
    )


def solution(mesh):
    spread = P(BOTH, None)
    member = P("grp", None)
    in_specs = (
        spread,
        spread,
        P(),
        P(),
        member,
        member,
        member,
        member,
        member,
        spread,
        spread,
        P(),
    )
    out_specs = (
        spread,
        spread,
        P(BOTH),
        P(BOTH),
        spread,
        spread,
        spread,
        spread,
        spread,
        spread,
        spread,
    )
    return jax.shard_map(
        on_device, mesh=mesh, in_specs=in_specs, out_specs=out_specs, check_vma=False
    )
```

time: 1970 us -> 748 us (0.38)
  waiting for transfers between devices: 1190 us -> 339 us
  matrix products: 230 us -> 54.2 us
  blocking collectives: 165 us -> 37 us
  starting transfers between devices: 107 us -> 40.3 us
  other arithmetic: 133 us -> 81.1 us
  local copies, waits for them, and re-layouts: 103 us -> 144 us
  Pallas kernels: 0 us -> 26.1 us
  loops' own time: 24 us -> 0 us
    reduce_scatter x9 -> x2, waiting for transfers between devices: 744 us -> 56.7 us  [the longest x1 56.7 us: on_device(): lax.psum_scatter(t_dot(attn_rows, d_group).astype(BF16), 'rep', scatter_d...]
    all_gather x5 -> x1, waiting for transfers between devices: 294 us -> 0.01 us  [on_device(): kv = lax.all_gather(kv_own, 'rep', axis=0, tiled=False)]
    dot_general x133 -> x15, matrix products: 230 us -> 54.2 us  [the longest x5 20.7 us: t_dot(): lax.dot_general(a, b, (((0,), (0,)), ((), ())), preferred_element_type=F32)]
    ppermute x32 -> x52, waiting for transfers between devices: 146 us -> 283 us  [swap(): return lax.ppermute(value, BOTH, [(i, i ^ mask) for i in range(count)])]
    unnamed x3 -> x1, blocking collectives: 165 us -> 37 us
    unnamed x70 -> x196, local copies, waits for them, and re-layouts: 8.59 us -> 77.3 us
    ppermute x32 -> x52, starting transfers between devices: 104 us -> 39.7 us  [swap(): return lax.ppermute(value, BOTH, [(i, i ^ mask) for i in range(count)])]
    convert_element_type x40 -> x9, other arithmetic: 54.2 us -> 13.3 us  [the longest x1 2.91 us: on_device(): d_gu = d_gu.reshape(2, 4, 2, out_rows, mine).astype(BF16)]
  transfers between devices with their start and end apart: 47 -> 56, of which waited for: 28 -> 26; matrix products, arithmetic and copies ran while one was open for 27% -> 31% of each run, Pallas kernels for 0% -> 4%
where the time goes in v1:
time: 748 us; the launch traced here: 739 us
  waiting for transfers between devices  339 us (45%)
  local copies, waits for them, and re-layouts  144 us (19%)
  other arithmetic  81.1 us (11%)
  matrix products  54.2 us (7%)
  starting transfers between devices  40.3 us (5%)
  blocking collectives  37 us (5%)
  Pallas kernels  26.1 us (3%)
  between operations  16.5 us (2%)
    ppermute x52, waiting for transfers between devices, swap(): return lax.ppermute(value, BOTH, [(i, i ^ mask) for i in range(count)])  283 us
    unnamed x196, local copies, waits for them, and re-layouts  77.3 us
    reduce_scatter x1, waiting for transfers between devices, on_device(): lax.psum_scatter(t_dot(attn_rows, d_group).astype(BF16), 'rep', scatter_d...  56.7 us
    ppermute x52, starting transfers between devices, swap(): return lax.ppermute(value, BOTH, [(i, i ^ mask) for i in range(count)])  39.7 us
    unnamed x1, blocking collectives  37 us
    dot_general x5, matrix products, t_dot(): lax.dot_general(a, b, (((0,), (0,)), ((), ())), preferred_element_type=F32)  20.7 us
    dot_general x5, matrix products, dot_t(): lax.dot_general(a, b, (((1,), (1,)), ((), ())), preferred_element_type=F32)  17.7 us
    pallas_call x1, Pallas kernels, attend_back(): pl.pallas_call(functools.partial(attend_back_kernel, reps), grid=(4,), in...  16.1 us
  transfers between devices with their start and end apart: 56, of which 26 were waited for; matrix products, arithmetic and copies ran while one was open for 31% of the time, Pallas kernels for 4%

profile of v1, /device:TPU:0, one launch (start us, length us, event | category | flops | bytes accessed | tf_op | source)
XLA Modules:
  0.0 738.5 jit_solution(11039524566433658534)
XLA Ops:
  20.2 9.2 %collective-permute-done.5 = bf16[2,128,256]{2,1,0:T(8,128)(2,1)S(1)} collective-permute-done((bf16[2,128,256]{2,1,0:T(8,128)(2,1)S(1)}, bf16[2,128,256]{2,1,0:T(8,128)(2,1)S(1)}, u32[]{:S(2)}, u32[]{:S(2)}) %collective-permute-start.5) | collective-permute-done | bytes 131104 | tf_op jit(solution)/shard_map/ppermute | solution.py:20
  30.1 5.8 fusion.82
  49.3 9.7 %fusion.83 = (bf16[512,344]{1,0:T(8,128)(2,1)}, bf16[512,344]{1,0:T(8,128)(2,1)}, bf16[512,344]{1,0:T(8,128)(2,1)}, bf16[512,344]{1,0:T(8,128)(2,1)}, bf16[512,3...) fusion(bf16[512,5504]{1,0:T(8,128)(2,1)} %param.19), kind=kLoop, calls=%fused_computation.310 | loop fusion | bytes 11272192 | tf_op jit(solution)/shard_map/slice | solution.py:326
  131.6 10.0 %attend.1 = (bf16[4,128,512]{2,1,0:T(8,128)(2,1)S(1)}, f32[4,512,1]{2,1,0:T(8,128)S(1)}) custom-call(s32[2]{0:T(128)S(1)} %pad_add_fusion.info_ref, s32[8]{0:T(128)S(1)} %copy-done.6, bf16[4,128,512]{2,1,0:T(8,128)(2,1)S(1)} %bitcast.517, bf16[8,4,128,256]{3,2,1,0:T(8,128)(2,1)S(1)} %bitcast.516), custom_call_target="tpu_custom_call" | custom-call | tf_op jit(solution)/shard_map/attend/pallas_call | solution.py:172
  151.7 32.2 %collective-permute-done.28 = bf16[64,2048]{1,0:T(8,128)(2,1)S(1)} collective-permute-done((bf16[64,2048]{1,0:T(8,128)(2,1)S(1)}, bf16[64,2048]{1,0:T(8,128)(2,1)S(1)}, u32[]{:S(2)}, u32[]{:S(2)}) %collective-permute-start.28) | collective-permute-done | bytes 262176 | tf_op jit(solution)/shard_map/ppermute | solution.py:20
  186.9 27.1 %collective-permute-done.17 = bf16[2,512,688]{1,2,0:T(8,128)(2,1)S(1)} collective-permute-done((bf16[2,512,688]{1,2,0:T(8,128)(2,1)S(1)}, bf16[2,512,688]{1,2,0:T(8,128)(2,1)S(1)}, u32[]{:S(2)}, u32[]{:S(2)}) %collective-permute-start.17) | collective-permute-done | bytes 1409056 | tf_op jit(solution)/shard_map/ppermute | solution.py:20
  214.4 9.6 %collective-permute-done.8 = bf16[128,2048]{1,0:T(8,128)(2,1)S(1)} collective-permute-done((bf16[128,2048]{1,0:T(8,128)(2,1)S(1)}, bf16[128,2048]{1,0:T(8,128)(2,1)S(1)}, u32[]{:S(2)}, u32[]{:S(2)}) %collective-permute-start.8) | collective-permute-done | bytes 524320 | tf_op jit(solution)/shard_map/ppermute | solution.py:20
  225.6 11.6 %collective-permute-done.11 = bf16[128,2048]{1,0:T(8,128)(2,1)S(1)} collective-permute-done((bf16[128,2048]{1,0:T(8,128)(2,1)S(1)}, bf16[128,2048]{1,0:T(8,128)(2,1)S(1)}, u32[]{:S(2)}, u32[]{:S(2)}) %collective-permute-start.11) | collective-permute-done | bytes 524320 | tf_op jit(solution)/shard_map/ppermute | solution.py:20
  258.0 4.5 fusion.6
  262.5 5.5 multiply_convert_fusion
  280.8 4.8 dot_general.66
  285.6 5.7 fusion.31
  296.3 6.4 copy.167
  335.6 7.8 %collective-permute-done.23 = bf16[128,2048]{1,0:T(8,128)(2,1)S(1)} collective-permute-done((bf16[128,2048]{1,0:T(8,128)(2,1)S(1)}, bf16[128,2048]{1,0:T(8,128)(2,1)S(1)}, u32[]{:S(2)}, u32[]{:S(2)}) %collective-permute-start.23) | collective-permute-done | bytes 524320 | tf_op jit(solution)/shard_map/ppermute | solution.py:20
  349.2 10.3 %collective-permute-done.36 = bf16[128,2048]{1,0:T(8,128)(2,1)} collective-permute-done((bf16[128,2048]{1,0:T(8,128)(2,1)}, bf16[128,2048]{1,0:T(8,128)(2,1)}, u32[]{:S(2)}, u32[]{:S(2)}) %collective-permute-start.36) | collective-permute-done | bytes 524320 | tf_op jit(solution)/shard_map/ppermute | solution.py:20
  359.5 5.5 fusion.27
  371.2 14.8 %collective-permute-done.42 = bf16[16,64,688]{2,1,0:T(8,128)(2,1)} collective-permute-done((bf16[16,64,688]{2,1,0:T(8,128)(2,1)}, bf16[16,64,688]{2,1,0:T(8,128)(2,1)}, u32[]{:S(2)}, u32[]{:S(2)}) %collective-permute-start.42) | collective-permute-done | bytes 1409056 | tf_op jit(solution)/shard_map/ppermute | solution.py:20
  394.2 16.1 %attend_back.1 = (bf16[4,128,512]{2,1,0:T(8,128)(2,1)}, bf16[8,4,128,256]{3,2,1,0:T(8,128)(2,1)}) custom-call(s32[2]{0:T(128)} %copy-done.7, s32[8]{0:T(128)} %starts_ref.3, bf16[4,128,512]{2,1,0:T(8,128)(2,1)} %bitcast.518, bf16[4,128,512]{2,1,0:T(8,128)(2,1)} %bitcast.581, bf16[4,128,512]{2,1,0:T(8,128)(2,1)} %copy-done.3, f32[4,512,1]{2,1,0:T(8,128)} %copy-done.5, ...), custom_call_target="tpu_custom_call" | custom-call | tf_op jit(solution)/shard_map/attend_back/pallas_call | solution.py:243
  432.0 84.6 %collective-permute-done.44 = bf16[2,4,1,2,64,688]{5,4,1,0,3,2:T(8,128)(2,1)} collective-permute-done((bf16[2,4,1,2,64,688]{5,4,1,0,3,2:T(8,128)(2,1)}, bf16[2,4,1,2,64,688]{5,4,1,0,3,2:T(8,128)(2,1)}, u32[]{:S(2)}, u32[]{:S(2)}) %collective-permute-start.44) | collective-permute-done | bytes 1409056 | tf_op jit(solution)/shard_map/ppermute | solution.py:20
  528.2 30.1 %collective-permute-done.45 = bf16[2,4,64,688]{3,2,1,0:T(8,128)(2,1)} collective-permute-done((bf16[2,4,64,688]{3,2,1,0:T(8,128)(2,1)}, bf16[2,4,64,688]{3,2,1,0:T(8,128)(2,1)}, u32[]{:S(2)}, u32[]{:S(2)}) %collective-permute-start.45) | collective-permute-done | bytes 704544 | tf_op jit(solution)/shard_map/ppermute | solution.py:20
  563.4 12.9 %collective-permute-done.49 = bf16[1,172,2048]{2,1,0:T(8,128)(2,1)} collective-permute-done((bf16[1,172,2048]{2,1,0:T(8,128)(2,1)}, bf16[1,172,2048]{2,1,0:T(8,128)(2,1)}, u32[]{:S(2)}, u32[]{:S(2)}) %collective-permute-start.49) | collective-permute-done | bytes 704544 | tf_op jit(solution)/shard_map/ppermute | solution.py:20
  608.5 6.2 collective-permute-done.39
  616.3 37.0 %all-reduce = f32[32,2,64]{2,1,0:T(2,128)S(1)} all-reduce(f32[32,2,64]{2,1,0:T(2,128)S(1)} %pad_maximum_fusion.38), channel_id=3, replica_groups=mesh['grp'=4,'rep'=8] {'grp','rep'}, use_global_device_ids=true, to_apply=%region_6.7.clone | all-reduce | flops 4096 | bytes 32768
  670.8 56.7 %reduce-scatter.6.cloned.1.call-done = bf16[64,2048]{1,0:T(8,128)(2,1)} async-done(((bf16[512,2048]{1,0:T(8,128)(2,1)}), bf16[64,2048]{1,0:T(8,128)(2,1)}) %reduce-scatter.6.cloned.1.call-update) | async-done | bytes 262160 | tf_op jit(solution)/shard_map/reduce_scatter | solution.py:410
  (463 shorter events, 297.8 us)
Async XLA Ops:
  7.2 122.8 %all-gather.3.cloned.1.call-start = ((), (), s32[]{:S(2)}) async-start(), calls=%async_computation.4 | async-start | bytes 2359296 | tf_op jit(solution)/shard_map/all_gather | solution.py:312
  10.6 108.4 %collective-permute-start.1 = (bf16[128,2048]{1,0:T(8,128)(2,1)}, bf16[128,2048]{1,0:T(8,128)(2,1)}, u32[]{:S(2)}, u32[]{:S(2)}) collective-permute-start(bf16[128,2048]{1,0:T(8,128)(2,1)} %fusion.33), channel_id=1, source_target_pairs={{0,16},{1,17},{2,18},{3,19},{4,20},{5,21},{6,22},{7,23},{8,24},{9,... | collective-permute-start | bytes 1572872 | tf_op jit(solution)/shard_map/ppermute | solution.py:20
  13.6 105.7 %collective-permute-start = (bf16[128,2048]{1,0:T(8,128)(2,1)}, bf16[128,2048]{1,0:T(8,128)(2,1)}, u32[]{:S(2)}, u32[]{:S(2)}) collective-permute-start(bf16[128,2048]{1,0:T(8,128)(2,1)} %fusion.33), channel_id=1, source_target_pairs={{0,8},{1,9},{2,10},{3,11},{4,12},{5,13},{6,14},{7,15},{8,0},{9,1},... | collective-permute-start | bytes 1572872 | tf_op jit(solution)/shard_map/ppermute | solution.py:20
  18.2 96.5 %collective-permute-start.3 = (bf16[2,512,512]{2,1,0:T(8,128)(2,1)}, bf16[2,512,512]{2,1,0:T(8,128)(2,1)}, u32[]{:S(2)}, u32[]{:S(2)}) collective-permute-start(bf16[2,512,512]{2,1,0:T(8,128)(2,1)} %pad_maximum_fusion.13), channel_id=1, source_target_pairs={{0,16},{1,17},{2,18},{3,19},{4,20},{5,21},{6,22},{7,23},{8,24},{9,... | collective-permute-start | bytes 3145736 | tf_op jit(solution)/shard_map/ppermute | solution.py:20
  49.0 607.4 %all-reduce.4.cloned.1.call-start = ((), (), s32[]{:S(2)}) async-start(), calls=%async_computation.5 | async-start | bytes 4194304
  143.2 40.8 %collective-permute-start.7 = (bf16[2,128,2048]{2,1,0:T(8,128)(2,1)S(1)}, bf16[2,128,2048]{2,1,0:T(8,128)(2,1)S(1)}, u32[]{:S(2)}, u32[]{:S(2)}) collective-permute-start(bf16[2,128,2048]{2,1,0:T(8,128)(2,1)S(1)} %fusion.41), channel_id=1, source_target_pairs={{0,8},{1,9},{2,10},{3,11},{4,12},{5,13},{6,14},{7,15},{8,0},{9,1},... | collective-permute-start | bytes 3145736 | tf_op jit(solution)/shard_map/ppermute | solution.py:20
  144.4 42.0 %collective-permute-start.15 = (bf16[2,512,688]{1,2,0:T(8,128)(2,1)S(1)}, bf16[2,512,688]{1,2,0:T(8,128)(2,1)S(1)}, u32[]{:S(2)}, u32[]{:S(2)}) collective-permute-start(bf16[2,512,688]{1,2,0:T(8,128)(2,1)S(1)} %pad_maximum_fusion.9), channel_id=1, source_target_pairs={{0,16},{1,17},{2,18},{3,19},{4,20},{5,21},{6,22},{7,23},{8,24},{9,... | collective-permute-start | bytes 4227080 | tf_op jit(solution)/shard_map/ppermute | solution.py:20
  147.2 36.7 %collective-permute-start.28 = (bf16[64,2048]{1,0:T(8,128)(2,1)S(1)}, bf16[64,2048]{1,0:T(8,128)(2,1)S(1)}, u32[]{:S(2)}, u32[]{:S(2)}) collective-permute-start(bf16[64,2048]{1,0:T(8,128)(2,1)S(1)} %slice.689), channel_id=1, source_target_pairs={{0,16},{1,17},{2,18},{3,19},{4,20},{5,21},{6,22},{7,23},{8,24},{9,... | collective-permute-start | bytes 786440 | tf_op jit(solution)/shard_map/ppermute | solution.py:20
  148.7 35.1 %collective-permute-start.27 = (bf16[64,2048]{1,0:T(8,128)(2,1)S(1)}, bf16[64,2048]{1,0:T(8,128)(2,1)S(1)}, u32[]{:S(2)}, u32[]{:S(2)}) collective-permute-start(bf16[64,2048]{1,0:T(8,128)(2,1)S(1)} %slice.688), channel_id=1, source_target_pairs={{0,2},{1,3},{2,0},{3,1},{4,6},{5,7},{6,4},{7,5},{8,10},{9,11},{10,... | collective-permute-start | bytes 786440 | tf_op jit(solution)/shard_map/ppermute | solution.py:20
  149.0 65.1 %collective-permute-start.17 = (bf16[2,512,688]{1,2,0:T(8,128)(2,1)S(1)}, bf16[2,512,688]{1,2,0:T(8,128)(2,1)S(1)}, u32[]{:S(2)}, u32[]{:S(2)}) collective-permute-start(bf16[2,512,688]{1,2,0:T(8,128)(2,1)S(1)} %pad_maximum_fusion.11), channel_id=1, source_target_pairs={{0,16},{1,17},{2,18},{3,19},{4,20},{5,21},{6,22},{7,23},{8,24},{9,... | collective-permute-start | bytes 4227080 | tf_op jit(solution)/shard_map/ppermute | solution.py:20
  183.9 40.7 %collective-permute-start.25 = (bf16[2,128,2048]{2,1,0:T(8,128)(2,1)S(1)}, bf16[2,128,2048]{2,1,0:T(8,128)(2,1)S(1)}, u32[]{:S(2)}, u32[]{:S(2)}) collective-permute-start(bf16[2,128,2048]{2,1,0:T(8,128)(2,1)S(1)} %get-tuple-element.124), channel_id=1, source_target_pairs={{0,8},{1,9},{2,10},{3,11},{4,12},{5,13},{6,14},{7,15},{8,0},{9,1},... | collective-permute-start | bytes 3145736 | tf_op jit(solution)/shard_map/ppermute | solution.py:20
  184.3 39.7 %collective-permute-start.8 = (bf16[128,2048]{1,0:T(8,128)(2,1)S(1)}, bf16[128,2048]{1,0:T(8,128)(2,1)S(1)}, u32[]{:S(2)}, u32[]{:S(2)}) collective-permute-start(bf16[128,2048]{1,0:T(8,128)(2,1)S(1)} %fusion.51), channel_id=1, source_target_pairs={{0,16},{1,17},{2,18},{3,19},{4,20},{5,21},{6,22},{7,23},{8,24},{9,... | collective-permute-start | bytes 1572872 | tf_op jit(solution)/shard_map/ppermute | solution.py:20
  186.1 39.3 %collective-permute-start.29 = (bf16[2,128,2048]{2,1,0:T(8,128)(2,1)S(1)}, bf16[2,128,2048]{2,1,0:T(8,128)(2,1)S(1)}, u32[]{:S(2)}, u32[]{:S(2)}) collective-permute-start(bf16[2,128,2048]{2,1,0:T(8,128)(2,1)S(1)} %get-tuple-element.126), channel_id=1, source_target_pairs={{0,8},{1,9},{2,10},{3,11},{4,12},{5,13},{6,14},{7,15},{8,0},{9,1},... | collective-permute-start | bytes 3145736 | tf_op jit(solution)/shard_map/ppermute | solution.py:20
  186.6 59.8 %collective-permute-start.16 = (bf16[2,512,688]{1,2,0:T(8,128)(2,1)S(1)}, bf16[2,512,688]{1,2,0:T(8,128)(2,1)S(1)}, u32[]{:S(2)}, u32[]{:S(2)}) collective-permute-start(bf16[2,512,688]{1,2,0:T(8,128)(2,1)S(1)} %pad_maximum_fusion.10), channel_id=1, source_target_pairs={{0,8},{1,9},{2,10},{3,11},{4,12},{5,13},{6,14},{7,15},{8,0},{9,1},... | collective-permute-start | bytes 4227080 | tf_op jit(solution)/shard_map/ppermute | solution.py:20
  348.3 37.6 %collective-permute-start.42 = (bf16[16,64,688]{2,1,0:T(8,128)(2,1)}, bf16[16,64,688]{2,1,0:T(8,128)(2,1)}, u32[]{:S(2)}, u32[]{:S(2)}) collective-permute-start(bf16[16,64,688]{2,1,0:T(8,128)(2,1)} %fusion.19), channel_id=1, source_target_pairs={{0,1},{1,0},{2,3},{3,2},{4,5},{5,4},{6,7},{7,6},{8,9},{9,8},{10,11... | collective-permute-start | bytes 4227080 | tf_op jit(solution)/shard_map/ppermute | solution.py:20
  349.2 41.2 %collective-permute-start.35 = (bf16[128,2048]{1,0:T(8,128)(2,1)}, bf16[128,2048]{1,0:T(8,128)(2,1)}, u32[]{:S(2)}, u32[]{:S(2)}) collective-permute-start(bf16[128,2048]{1,0:T(8,128)(2,1)} %get-tuple-element.29), channel_id=1, source_target_pairs={{0,8},{1,9},{2,10},{3,11},{4,12},{5,13},{6,14},{7,15},{8,0},{9,1},... | collective-permute-start | bytes 1572872 | tf_op jit(solution)/shard_map/ppermute | solution.py:20
  369.1 48.3 %collective-permute-start.43 = (bf16[16,64,688]{2,1,0:T(8,128)(2,1)}, bf16[16,64,688]{2,1,0:T(8,128)(2,1)}, u32[]{:S(2)}, u32[]{:S(2)}) collective-permute-start(bf16[16,64,688]{2,1,0:T(8,128)(2,1)} %fusion.20), channel_id=1, source_target_pairs={{0,1},{1,0},{2,3},{3,2},{4,5},{5,4},{6,7},{7,6},{8,9},{9,8},{10,11... | collective-permute-start | bytes 4227080 | tf_op jit(solution)/shard_map/ppermute | solution.py:20
  414.5 248.2 %reduce-scatter.8.cloned.1.call-start = ((), (), s32[]{:S(2)}) async-start(), calls=%async_computation.3 | async-start | bytes 2359296 | tf_op jit(solution)/shard_map/reduce_scatter | solution.py:413
  422.5 94.1 %collective-permute-start.44 = (bf16[2,4,1,2,64,688]{5,4,1,0,3,2:T(8,128)(2,1)}, bf16[2,4,1,2,64,688]{5,4,1,0,3,2:T(8,128)(2,1)}, u32[]{:S(2)}, u32[]{:S(2)}) collective-permute-start(bf16[2,4,1,2,64,688]{5,4,1,0,3,2:T(8,128)(2,1)} %fusion.21), channel_id=1, source_target_pairs={{0,4},{1,5},{2,6},{3,7},{4,0},{5,1},{6,2},{7,3},{8,12},{9,13},{10,... | collective-permute-start | bytes 4227080 | tf_op jit(solution)/shard_map/ppermute | solution.py:20
  430.9 89.6 %collective-permute-start.48 = (bf16[2,172,2048]{2,0,1:T(2,128)(2,1)}, bf16[2,172,2048]{2,0,1:T(2,128)(2,1)}, u32[]{:S(2)}, u32[]{:S(2)}) collective-permute-start(bf16[2,172,2048]{2,0,1:T(2,128)(2,1)} %copy.174), channel_id=1, source_target_pairs={{0,1},{1,0},{2,3},{3,2},{4,5},{5,4},{6,7},{7,6},{8,9},{9,8},{10,11... | collective-permute-start | bytes 4227080 | tf_op jit(solution)/shard_map/ppermute | solution.py:20
  431.7 295.8 %reduce-scatter.6.cloned.1.call-start = ((), (), s32[]{:S(2)}) async-start(), calls=%async_computation.2 | async-start | bytes 2359296 | tf_op jit(solution)/shard_map/reduce_scatter | solution.py:410
  520.6 37.7 %collective-permute-start.45 = (bf16[2,4,64,688]{3,2,1,0:T(8,128)(2,1)}, bf16[2,4,64,688]{3,2,1,0:T(8,128)(2,1)}, u32[]{:S(2)}, u32[]{:S(2)}) collective-permute-start(bf16[2,4,64,688]{3,2,1,0:T(8,128)(2,1)} %get-tuple-element.120), channel_id=1, source_target_pairs={{0,2},{1,3},{2,0},{3,1},{4,6},{5,7},{6,4},{7,5},{8,10},{9,11},{10,... | collective-permute-start | bytes 2113544 | tf_op jit(solution)/shard_map/ppermute | solution.py:20
  525.6 50.6 %collective-permute-start.49 = (bf16[1,172,2048]{2,1,0:T(8,128)(2,1)}, bf16[1,172,2048]{2,1,0:T(8,128)(2,1)}, u32[]{:S(2)}, u32[]{:S(2)}) collective-permute-start(bf16[1,172,2048]{2,1,0:T(8,128)(2,1)} %dynamic-slice_convert_fusion.3), channel_id=1, source_target_pairs={{0,4},{1,5},{2,6},{3,7},{4,0},{5,1},{6,2},{7,3},{8,12},{9,13},{10,... | collective-permute-start | bytes 2113544 | tf_op jit(solution)/shard_map/ppermute | solution.py:20
  669.9 59.4 %collective-permute-start.51 = (bf16[2,128,256]{2,1,0:T(8,128)(2,1)S(1)}, bf16[2,128,256]{2,1,0:T(8,128)(2,1)S(1)}, u32[]{:S(2)}, u32[]{:S(2)}) collective-permute-start(bf16[2,128,256]{2,1,0:T(8,128)(2,1)S(1)} %pad_maximum_fusion.35), channel_id=1, source_target_pairs={{0,8},{1,9},{2,10},{3,11},{4,12},{5,13},{6,14},{7,15},{8,0},{9,1},... | collective-permute-start | bytes 393224 | tf_op jit(solution)/shard_map/ppermute | solution.py:20
  (113 other events, 1215.0 us)
Sparse Core Ops, SparseCore 0:
  49.1 51.2 all-gather.2
  414.7 172.4 all-reduce.3
  590.7 66.5 reduce-scatter.7
  660.7 66.7 reduce-scatter.5

commit v2 on v1

v2 whole, which is shorter than its diff:
```python
import functools

import jax
import jax.numpy as jnp
from jax import lax
from jax.experimental import pallas as pl
from jax.experimental.pallas import tpu as pltpu
from jax.sharding import PartitionSpec as P

HD = 128
EPSILON = 1e-06
NEGATIVE = -1e30
F32 = jnp.float32
BF16 = jnp.bfloat16
BOTH = ("grp", "rep")
BRIEF = pl.CostEstimate(flops=1, transcendentals=0, bytes_accessed=1)


def swap(value, mask):
    count = lax.axis_size(BOTH)
    return lax.ppermute(value, BOTH, [(i, i ^ mask) for i in range(count)])


def after(value, *earlier):
    return lax.optimization_barrier((value,) + earlier)[0]


def together(*values):
    return lax.optimization_barrier(values)


def dot(a, b):
    return jnp.dot(a, b, preferred_element_type=F32)


def dot_t(a, b):
    return lax.dot_general(a, b, (((1,), (1,)), ((), ())), preferred_element_type=F32)


def t_dot(a, b):
    return lax.dot_general(a, b, (((0,), (0,)), ((), ())), preferred_element_type=F32)


def pick(value, index, axis):
    return lax.dynamic_index_in_dim(value, index, axis, keepdims=False)


def scatter_four_core(parts, core):
    parts = parts.reshape((2, 2) + parts.shape[1:])
    got = swap(parts[:, 1].astype(BF16), core)
    return parts[:, 0] + got.astype(F32)


def corner_step(parts, yy, zz):
    half = parts.shape[1] // 2
    corner = parts[3].astype(BF16)
    return swap(corner[:half], yy), swap(corner[half:], zz)


def side_step(parts, to_z, to_y, yy, zz):
    half = parts.shape[1] // 2
    for_z = jnp.concatenate([parts[2, :half] + to_z.astype(F32), parts[2, half:]])
    for_y = jnp.concatenate([parts[1, :half], parts[1, half:] + to_y.astype(F32)])
    return swap(for_z.astype(BF16), zz), swap(for_y.astype(BF16), yy)


def exchange_four(pieces, core, yy):
    from_y = swap(jnp.stack([pieces[2], pieces[3]]), yy)
    from_c = swap(pieces[1], core)
    return [pieces[0], from_c, from_y[0], swap(from_y[1], core)]


def absolute(pieces, g):
    odd, upper = (g & 1) == 1, (g >> 1) == 1
    a = jnp.where(odd, pieces[1], pieces[0])
    b = jnp.where(odd, pieces[0], pieces[1])
    c = jnp.where(odd, pieces[3], pieces[2])
    d = jnp.where(odd, pieces[2], pieces[3])
    return [
        jnp.where(upper, c, a),
        jnp.where(upper, d, b),
        jnp.where(upper, a, c),
        jnp.where(upper, b, d),
    ]


def halve(value, bit, mask, axis, hold=None):
    got = swap(pick(value, 1 - bit, axis).astype(BF16), mask)
    if hold is not None:
        got = after(got, hold)
    return pick(value, bit, axis).astype(F32) + got.astype(F32)


def scatter_high(value, r, high, axis, hold=None):
    for mask in reversed(high):
        shape = value.shape
        value = value.reshape(shape[:axis] + (2, shape[axis] // 2) + shape[axis + 1 :])
        value = halve(value, (r & mask) // mask, mask, axis, hold)
    return jnp.squeeze(value, axis)


def scatter_rep(value, r, high, hold=None):
    reps = value.shape[0]
    rest = value.shape[1:]
    value = halve(value.reshape((reps // 4, 2, 2) + rest), r & 1, 1, 2, hold)
    value = halve(value, (r >> 1) & 1, 2, 1)
    return scatter_high(value, r, high, 0)


def ring_of(reps):
    ring = (0, 1, 3, 2)
    pairs = []
    for member in range(4):
        for k in range(4):
            for x in range(2):
                base = member * reps + x
                pairs.append((base + 2 * ring[k], base + 2 * ring[(k + 1) % 4]))
    return pairs


def ring_slots(r, reps):
    order = jnp.array((0, 1, 3, 2), jnp.int32)
    other = jnp.arange(reps, dtype=jnp.int32)
    steps = (order[r >> 1] - order[other >> 1]) & 3
    return 2 * steps + ((other ^ r) & 1)


def pack_kernel(
    outer, chunk, wide, info_ref, gate_ref, up_ref, stay_ref, core_ref, y_ref, relay_ref, held
):
    step = pl.program_id(0)
    g, bit, x = info_ref[0], (info_ref[1] >> 1) & 1, info_ref[1] & 1
    rows = gate_ref.shape[0]
    quarter = outer * 4 * chunk
    fill = jnp.zeros((rows, wide - chunk), BF16)

    for b in range(2):

        @pl.when(bit == b)
        def _():
            for which, ref in enumerate((gate_ref, up_ref)):
                block = ref[...]
                for member in range(4):
                    parts = []
                    for xd in range(2):
                        for o in range(outer):
                            at = member * quarter + (o * 4 + b * 2 + xd) * chunk
                            parts += [block[:, at : at + chunk], fill]
                    span = 2 * outer * wide
                    held[member ^ g, :, which * span : (which + 1) * span] = jnp.concatenate(
                        parts, axis=1
                    )

    stay_ref[...] = held[0]
    core_ref[...] = held[1]

    @pl.when(step // (pl.num_programs(0) // 2) == x)
    def _():
        y_ref[...] = held[2]
        relay_ref[...] = held[3]


def pack(info, w_gate, w_up, outer, chunk, wide):
    rows, width = w_gate.shape
    span = 4 * outer * wide
    steps = 8
    part = rows // steps

    def lower(i, info):
        return jnp.clip(i - (info[1] & 1) * (steps // 2), 0, steps // 2 - 1), 0

    def plain(i, info):
        return i, 0

    shape = jax.ShapeDtypeStruct((rows, span), BF16)
    small = jax.ShapeDtypeStruct((rows // 2, span), BF16)
    return pl.pallas_call(
        functools.partial(pack_kernel, outer, chunk, wide),
        grid_spec=pltpu.PrefetchScalarGridSpec(
            num_scalar_prefetch=1,
            grid=(steps,),
            in_specs=[pl.BlockSpec((part, width), plain), pl.BlockSpec((part, width), plain)],
            out_specs=[
                pl.BlockSpec((part, span), plain),
                pl.BlockSpec((part, span), plain),
                pl.BlockSpec((part, span), lower),
                pl.BlockSpec((part, span), lower),
            ],
            scratch_shapes=[pltpu.VMEM((4, part, span), BF16)],
        ),
        out_shape=[shape, shape, small, small],
        compiler_params=pltpu.CompilerParams(vmem_limit_bytes=32 << 20),
        cost_estimate=BRIEF,
        name="pack",
    )(info, w_gate, w_up)


def pack_down_kernel(outer, chunk, wide, info_ref, down_ref, out_ref):
    bit = (info_ref[1] >> 1) & 1
    block = down_ref[...]
    fill = jnp.zeros((wide - chunk, block.shape[1]), BF16)
    for b in range(2):

        @pl.when(bit == b)
        def _():
            for xd in range(2):
                for o in range(outer):
                    at = (o * 4 + b * 2 + xd) * chunk
                    piece = jnp.concatenate([block[at : at + chunk], fill], axis=0)
                    to = (xd * outer + o) * wide
                    out_ref[to : to + wide] = piece


def pack_down(info, w_down, outer, chunk, wide):
    rows, width = w_down.shape
    steps = 4
    part = width // steps
    mine = 2 * outer * wide
    return pl.pallas_call(
        functools.partial(pack_down_kernel, outer, chunk, wide),
        grid=(steps,),
        in_specs=[
            pl.BlockSpec(memory_space=pltpu.SMEM),
            pl.BlockSpec((rows, part), lambda i: (0, i)),
        ],
        out_specs=pl.BlockSpec((mine, part), lambda i: (0, i)),
        out_shape=jax.ShapeDtypeStruct((mine, width), BF16),
        compiler_params=pltpu.CompilerParams(vmem_limit_bytes=32 << 20),
        cost_estimate=BRIEF,
        name="pack_down",
    )(info, w_down)


def columns_grad_kernel(rows, mine, info_ref, ha, hb, da, db, send_g, send_u, keep_g, keep_u):
    odd = (info_ref[1] & 1) == 1
    grad = t_dot(ha[...], da[...]) + t_dot(hb[...], db[...])
    count, width = grad.shape
    grad = grad.reshape(count // (2 * rows), 2, rows, width)
    low, upp = grad[:, 0], grad[:, 1]
    send = jnp.where(odd, low, upp).astype(BF16).reshape(count // 2, width)
    keep = jnp.where(odd, upp, low).reshape(count // 2, width)
    send_g[...] = send[:, :mine]
    send_u[...] = send[:, mine:]
    keep_g[...] = keep[:, :mine]
    keep_u[...] = keep[:, mine:]


def columns_grad(info, ha, hb, da, db, rows):
    tokens, width = ha.shape
    mine = da.shape[1] // 2
    part = min(512, width)
    half = pl.BlockSpec((part // 2, mine), lambda i: (i, 0))
    lhs = pl.BlockSpec((tokens, part), lambda i: (0, i))
    rhs = pl.BlockSpec(da.shape, lambda i: (0, 0))
    return pl.pallas_call(
        functools.partial(columns_grad_kernel, rows, mine),
        grid=(width // part,),
        in_specs=[pl.BlockSpec(memory_space=pltpu.SMEM), lhs, lhs, rhs, rhs],
        out_specs=[half] * 4,
        out_shape=[jax.ShapeDtypeStruct((width // 2, mine), BF16)] * 2
        + [jax.ShapeDtypeStruct((width // 2, mine), F32)] * 2,
        compiler_params=pltpu.CompilerParams(vmem_limit_bytes=56 << 20),
        cost_estimate=BRIEF,
        name="columns_grad",
    )(info, ha, hb, da, db)


def rows_grad_kernel(info_ref, ha, hb, da, db, send_ref, keep_ref):
    odd = (info_ref[1] & 1) == 1
    grad = t_dot(ha[...], da[...]) + t_dot(hb[...], db[...])
    half = grad.shape[0] // 2
    low, upp = grad[:half], grad[half:]
    send_ref[...] = jnp.where(odd, low, upp).astype(BF16)
    keep_ref[...] = jnp.where(odd, upp, low)


def rows_grad(info, ha, hb, da, db):
    tokens, mine = ha.shape
    width = da.shape[1]
    part = min(512, width)
    half = pl.BlockSpec((mine // 2, part), lambda i: (0, i))
    lhs = pl.BlockSpec(ha.shape, lambda i: (0, 0))
    rhs = pl.BlockSpec((tokens, part), lambda i: (0, i))
    return pl.pallas_call(
        rows_grad_kernel,
        grid=(width // part,),
        in_specs=[pl.BlockSpec(memory_space=pltpu.SMEM), lhs, lhs, rhs, rhs],
        out_specs=[half] * 2,
        out_shape=[
            jax.ShapeDtypeStruct((mine // 2, width), BF16),
            jax.ShapeDtypeStruct((mine // 2, width), F32),
        ],
        compiler_params=pltpu.CompilerParams(vmem_limit_bytes=48 << 20),
        cost_estimate=BRIEF,
        name="rows_grad",
    )(info, ha, hb, da, db)


def unpack_kernel(
    outer, chunk, wide, info_ref, got_g, got_u, w_gate, w_up, gain, gate_ref, up_ref, dg_ref
):
    g, bit = info_ref[0], (info_ref[1] >> 1) & 1
    total = 0.0
    for got, ref, weight in ((got_g, gate_ref, w_gate), (got_u, up_ref, w_up)):
        parts = []
        for member in range(4):
            pieces = [got[member ^ g, b ^ bit] for b in range(2)]
            for o in range(outer):
                for b in range(2):
                    for xd in range(2):
                        at = (xd * outer + o) * wide
                        parts.append(pieces[b][:, at : at + chunk])
        grad = jnp.concatenate(parts, axis=1).astype(F32)
        ref[...] = grad
        total = total + jnp.sum(grad * weight[...].astype(F32), axis=1, keepdims=True)
    dg_ref[...] = total / gain[...]


def unpack(info, got_g, got_u, w_gate, w_up, gain, outer, chunk, wide):
    rows = got_g.shape[2]
    shape = jax.ShapeDtypeStruct((rows, 16 * outer * chunk), F32)
    vmem = pl.BlockSpec(memory_space=pltpu.VMEM)
    return pl.pallas_call(
        functools.partial(unpack_kernel, outer, chunk, wide),
        in_specs=[pl.BlockSpec(memory_space=pltpu.SMEM)] + [vmem] * 5,
        out_specs=[vmem] * 3,
        out_shape=[shape, shape, jax.ShapeDtypeStruct((rows, 1), F32)],
        compiler_params=pltpu.CompilerParams(vmem_limit_bytes=32 << 20),
        cost_estimate=BRIEF,
        name="unpack",
    )(info, got_g, got_u, w_gate, w_up, gain)


def block_bounds(info_ref, starts_ref, j, reps):
    place = ((info_ref[0] ^ j) * reps + info_ref[1]) * HD
    docs = starts_ref.shape[0]
    first = jnp.int32(0)
    for d in range(docs):
        first = jnp.maximum(first, jnp.where(starts_ref[d] <= place, starts_ref[d], 0))
    position = place + lax.broadcasted_iota(jnp.int32, (4, HD, 1), 1).reshape(4 * HD, 1)
    lowest = jnp.zeros_like(position)
    for d in range(docs):
        lowest = jnp.maximum(lowest, jnp.where(starts_ref[d] <= position, starts_ref[d], 0))
    return place, first, position, lowest


def key_tile(info_ref, slots_ref, kv_ref, tile, reps):
    per = reps // 4
    member = (tile // per) ^ info_ref[0]
    base = 4 * (tile % per)
    piece = jnp.concatenate([kv_ref[slots_ref[base + k], member] for k in range(4)], axis=0)
    return piece[:, :HD], piece[:, HD:]


def head_rows(ref):
    return jnp.concatenate([ref[0, :, h * HD : (h + 1) * HD] for h in range(4)], axis=0)


def attend_kernel(reps, info_ref, slots_ref, starts_ref, q_ref, kv_ref, o_ref, lse_ref):
    j = pl.program_id(0)
    place, first, position, lowest = block_bounds(info_ref, starts_ref, j, reps)
    query = head_rows(q_ref)
    rows = 4 * HD
    scale = HD ** (-0.5)

    def step(tile, carry):
        best, total, accum = carry
        key, value = key_tile(info_ref, slots_ref, kv_ref, tile, reps)
        scores = dot_t(query, key) * scale
        at = tile * 512 + lax.broadcasted_iota(jnp.int32, (1, 512), 1)
        scores = jnp.where((at >= lowest) & (at <= position), scores, NEGATIVE)
        new_best = jnp.maximum(best, jnp.max(scores, axis=1, keepdims=True))
        weights = jnp.exp(scores - new_best)
        factor = jnp.exp(best - new_best)
        total = total * factor + jnp.sum(weights, axis=1, keepdims=True)
        accum = accum * factor + dot(weights.astype(BF16), value)
        return new_best, total, accum

    init = (
        jnp.full((rows, 1), NEGATIVE, F32),
        jnp.zeros((rows, 1), F32),
        jnp.zeros((rows, HD), F32),
    )
    best, total, accum = lax.fori_loop(first // 512, place // 512 + 1, step, init)
    out = accum / total
    for h in range(4):
        o_ref[0, :, h * HD : (h + 1) * HD] = out[h * HD : (h + 1) * HD].astype(BF16)
    lse_ref[0] = best + jnp.log(total)


def attend(info, slots, starts, query, kv):
    reps = kv.shape[0]
    return pl.pallas_call(
        functools.partial(attend_kernel, reps),
        grid=(4,),
        in_specs=[
            pl.BlockSpec(memory_space=pltpu.SMEM),
            pl.BlockSpec(memory_space=pltpu.SMEM),
            pl.BlockSpec(memory_space=pltpu.SMEM),
            pl.BlockSpec((1, HD, 4 * HD), lambda j: (j, 0, 0)),
            pl.BlockSpec(kv.shape, lambda j: (0, 0, 0, 0)),
        ],
        out_specs=[
            pl.BlockSpec((1, HD, 4 * HD), lambda j: (j, 0, 0)),
            pl.BlockSpec((1, 4 * HD, 1), lambda j: (j, 0, 0)),
        ],
        out_shape=[
            jax.ShapeDtypeStruct((4, HD, 4 * HD), BF16),
            jax.ShapeDtypeStruct((4, 4 * HD, 1), F32),
        ],
        compiler_params=pltpu.CompilerParams(vmem_limit_bytes=48 << 20),
        cost_estimate=BRIEF,
        name="attend",
    )(info, slots, starts, query, kv)


def attend_back_kernel(
    reps,
    info_ref,
    slots_ref,
    starts_ref,
    q_ref,
    do_ref,
    o_ref,
    lse_ref,
    kv_ref,
    dq_ref,
    dkv_ref,
    sums,
):
    j = pl.program_id(0)

    @pl.when(j == 0)
    def _():
        sums[...] = jnp.zeros_like(sums)

    place, first, position, lowest = block_bounds(info_ref, starts_ref, j, reps)
    query = head_rows(q_ref)
    d_out = head_rows(do_ref)
    out = head_rows(o_ref)
    lse = lse_ref[0]
    delta = jnp.sum(d_out.astype(F32) * out.astype(F32), axis=1, keepdims=True)
    scale = HD ** (-0.5)
    per = reps // 4

    def step(tile, d_query):
        key, value = key_tile(info_ref, slots_ref, kv_ref, tile, reps)
        scores = dot_t(query, key) * scale
        at = tile * 512 + lax.broadcasted_iota(jnp.int32, (1, 512), 1)
        probs = jnp.where((at >= lowest) & (at <= position), jnp.exp(scores - lse), 0.0)
        d_probs = dot_t(d_out, value)
        d_scores = (probs * (d_probs - delta)).astype(BF16)
        d_query = d_query + dot(d_scores, key)
        d_key = t_dot(d_scores, query) * scale
        d_value = t_dot(probs.astype(BF16), d_out)
        member = (tile // per) ^ info_ref[0]
        both = jnp.concatenate([d_key, d_value], axis=1)
        for k in range(4):
            slot = (4 * (tile % per) + k) ^ info_ref[1]
            sums[slot, member] = sums[slot, member] + both[k * HD : (k + 1) * HD]
        return d_query

    d_query = lax.fori_loop(
        first // 512, place // 512 + 1, step, jnp.zeros((4 * HD, HD), F32)
    )
    d_query = (d_query * scale).astype(BF16)
    for h in range(4):
        dq_ref[0, :, h * HD : (h + 1) * HD] = d_query[h * HD : (h + 1) * HD]

    @pl.when(j == 3)
    def _():
        dkv_ref[...] = sums[...].astype(BF16)


def attend_back(info, slots, starts, query, d_out, out, lse, kv):
    reps = kv.shape[0]
    rows = pl.BlockSpec((1, HD, 4 * HD), lambda j: (j, 0, 0))
    whole = pl.BlockSpec(kv.shape, lambda j: (0, 0, 0, 0))
    return pl.pallas_call(
        functools.partial(attend_back_kernel, reps),
        grid=(4,),
        in_specs=[
            pl.BlockSpec(memory_space=pltpu.SMEM),
            pl.BlockSpec(memory_space=pltpu.SMEM),
            pl.BlockSpec(memory_space=pltpu.SMEM),
            rows,
            rows,
            rows,
            pl.BlockSpec((1, 4 * HD, 1), lambda j: (j, 0, 0)),
            whole,
        ],
        out_specs=[rows, whole],
        out_shape=[
            jax.ShapeDtypeStruct((4, HD, 4 * HD), BF16),
            jax.ShapeDtypeStruct(kv.shape, BF16),
        ],
        scratch_shapes=[pltpu.VMEM(kv.shape, F32)],
        compiler_params=pltpu.CompilerParams(vmem_limit_bytes=60 << 20),
        cost_estimate=BRIEF,
        name="attend_back",
    )(info, slots, starts, query, d_out, out, lse, kv)


def on_device(
    tokens,
    cotangent,
    gain_attn,
    gain_ffn,
    w_query,
    w_out,
    w_gate,
    w_up,
    w_down,
    keys,
    values,
    starts,
):
    reps = lax.axis_size("rep")
    rows, width = tokens.shape
    hidden_all = w_gate.shape[1]
    g = lax.axis_index("grp")
    r = lax.axis_index("rep")
    core, yy, xx, zz = reps, 2 * reps, 1, 2
    high = [1 << k for k in range(2, 16) if (1 << k) < reps]
    outer = reps // 4
    x_bit, z_bit = r & 1, (r >> 1) & 1
    share = width // 4
    out_rows = width // (4 * reps)
    chunk = hidden_all // (4 * reps)
    wide = -(-(2 * outer * chunk) // 256) * 256 // (2 * outer)
    mine = 2 * outer * wide
    info = jnp.stack([g, r]).astype(jnp.int32)

    kv_parts = [
        jnp.concatenate(
            [
                lax.dynamic_slice_in_dim(keys, (g ^ j) * HD, HD, 1),
                lax.dynamic_slice_in_dim(values, (g ^ j) * HD, HD, 1),
            ],
            axis=1,
        )
        for j in range(4)
    ]
    kv_own = jnp.stack(exchange_four(kv_parts, core, yy))

    x_full = tokens.astype(F32)
    inv_one = lax.rsqrt(jnp.mean(x_full * x_full, axis=1, keepdims=True) + EPSILON)
    normed_one = x_full * inv_one
    h_one = (normed_one * gain_attn).astype(BF16)

    h_y = swap(h_one, yy)
    wq_half = share // 2
    wq_y = jnp.stack(
        [
            lax.dynamic_slice(w_query, (x_bit * wq_half, (g ^ j) * share), (wq_half, share))
            for j in (2, 3)
        ]
    )
    stay, to_core, to_y, relay = pack(info, w_gate, w_up, outer, chunk, wide)
    wd = pack_down(info, w_down, outer, chunk, wide)
    dy_y = cotangent
    if reps == 8:
        pairs = ring_of(reps)
        wq_y = swap(after(wq_y, kv_own), yy)
        one = lax.ppermute(kv_own, BOTH, pairs)
        one, h_y = together(one, h_y)
        two = lax.ppermute(one, BOTH, pairs)
        two, wq_y, stay, wd = together(two, wq_y, stay, wd)
        wq_x = swap(wq_y, xx)
        dy_y = swap(after(dy_y, two), yy)
        three = lax.ppermute(two, BOTH, pairs)
        three, wq_x, dy_y = together(three, wq_x, dy_y)
        relay = swap(after(relay, two), yy)
        kv = jnp.stack([part for v in (kv_own, one, two, three) for part in (v, swap(v, xx))])
        slots = ring_slots(r, reps)
        kv, relay = together(kv, relay)
    else:
        wq_y, dy_y, relay = swap(wq_y, yy), swap(dy_y, yy), swap(relay, yy)
        wq_x = swap(wq_y, xx)
        kv = lax.all_gather(kv_own, "rep", axis=0, tiled=False)
        slots = jnp.arange(reps, dtype=jnp.int32)

    h_group = jnp.stack([h_one, swap(h_one, core), h_y, swap(h_y, core)])
    h_group = h_group.reshape(4 * rows, width)
    upper_half = x_bit == 1
    wq_y = jnp.concatenate(
        [jnp.where(upper_half, wq_x, wq_y), jnp.where(upper_half, wq_y, wq_x)], axis=1
    )
    wq_parts = [
        lax.dynamic_slice_in_dim(w_query, g * share, share, 1),
        swap(lax.dynamic_slice_in_dim(w_query, (g ^ 1) * share, share, 1), core),
        wq_y[0],
        swap(wq_y[1], core),
    ]
    wq_cols = jnp.concatenate(absolute(wq_parts, g), axis=0)
    query = dot(h_group, wq_cols).astype(BF16).reshape(4, rows, share)

    from_y = swap(after(to_y, relay), yy)
    relay_x = swap(relay, xx)
    attn, lse = attend(info, slots, starts, query, kv)
    attn, lse, from_y = together(attn, lse, from_y)
    attn_rows = attn.reshape(4 * rows, share)
    branch = scatter_four_core(dot(attn_rows, w_out).reshape(4, rows, width), core)
    from_branch = swap(branch[1].astype(BF16), yy)
    from_branch, relay_x = together(from_branch, relay_x)
    from_y_x = swap(from_y, xx)
    dy_near = jnp.stack([cotangent, dy_y])
    dy_far = swap(after(dy_near, attn), zz)
    resid = x_full + branch[0] + from_branch.astype(F32)
    inv_two = lax.rsqrt(jnp.mean(resid * resid, axis=1, keepdims=True) + EPSILON)
    normed_two = resid * inv_two
    h_two = (normed_two * gain_ffn).astype(BF16)

    h_y, h_z = swap(h_two, yy), swap(h_two, zz)
    h_y, h_z, dy_far = together(h_y, h_z, dy_far)
    low, upp = swap(h_y[: rows // 2], zz), swap(h_z[rows // 2 :], yy)
    low, upp, from_y_x = together(low, upp, from_y_x)
    h_a = jnp.concatenate([h_two, h_y, h_z, low, upp])
    h_b = swap(h_a, core)
    dy_a = jnp.stack([dy_near, dy_far]).reshape(4 * rows, width)
    dy_b = swap(dy_a, core)
    diagonal, diagonal_x = swap(relay, core), swap(relay_x, core)
    w_gu = jnp.concatenate(
        absolute(
            [
                stay,
                swap(to_core, core),
                jnp.concatenate(
                    [
                        jnp.where(upper_half, from_y_x, from_y),
                        jnp.where(upper_half, from_y, from_y_x),
                    ]
                ),
                jnp.concatenate(
                    [
                        jnp.where(upper_half, diagonal_x, diagonal),
                        jnp.where(upper_half, diagonal, diagonal_x),
                    ]
                ),
            ],
            g,
        ),
        axis=0,
    )

    def feed_forward(h, dy):
        both = dot(h, w_gu)
        gate, upper = both[:, :mine], both[:, mine:]
        d_hidden = dot_t(dy, wd)
        sigma = jax.nn.sigmoid(gate)
        swish = gate * sigma
        hidden = (swish * upper).astype(BF16)
        d_gate = (d_hidden * upper * sigma * (1.0 + gate * (1.0 - sigma))).astype(BF16)
        d_upper = (d_hidden * swish).astype(BF16)
        return hidden, jnp.concatenate([d_gate, d_upper], axis=1)

    hidden_a, d_both_a = feed_forward(h_a, dy_a)
    hidden_b, d_both_b = feed_forward(h_b, dy_b)
    from_core = swap(dot_t(d_both_b, w_gu).astype(BF16), core)
    d_h_parts = dot_t(d_both_a, w_gu) + from_core.astype(F32)
    d_h_parts = d_h_parts.reshape(4, rows, width)

    send_d, keep_d = rows_grad(info, hidden_a, hidden_b, dy_a, dy_b)
    send_g, send_u, keep_g, keep_u = columns_grad(info, h_a, h_b, d_both_a, d_both_b, out_rows)
    got_d = swap(send_d, xx)
    to_z, to_y = corner_step(d_h_parts, yy, zz)
    to_z, to_y, send_d, keep_d = together(to_z, to_y, send_d, keep_d)
    from_z, from_y = side_step(d_h_parts, to_z, to_y, yy, zz)
    from_z, from_y, send_g, send_u, got_d = together(from_z, from_y, send_g, send_u, got_d)
    got_g = swap(send_g, xx)
    d_h_two = d_h_parts[0] + from_z.astype(F32) + from_y.astype(F32)
    scaled_two = d_h_two * gain_ffn
    d_resid = cotangent.astype(F32) + inv_two * (
        scaled_two - normed_two * jnp.mean(scaled_two * normed_two, axis=1, keepdims=True)
    )
    da_own = d_resid.astype(BF16)
    da_y, da_c = swap(da_own, yy), swap(da_own, core)
    out_core = swap(dot(hidden_b, wd).astype(BF16), core)
    da_y, da_c, out_core = together(da_y, da_c, out_core)
    d_group = jnp.stack([da_own, da_c, da_y, swap(da_y, core)]).reshape(4 * rows, width)
    d_group, got_g = together(d_group, got_g)
    got_u = swap(send_u, xx)
    out_parts = (dot(hidden_a, wd) + out_core.astype(F32)).reshape(4, rows, width)
    out_z, out_y = corner_step(after(out_parts, d_group), yy, zz)

    d_attn = dot_t(d_group, w_out).astype(BF16).reshape(4, rows, share)
    grad_d = (keep_d + got_d.astype(F32)).reshape(outer, wide, width)
    d_query, d_kv = attend_back(info, slots, starts, query, d_attn, attn, lse, kv)
    d_query, d_kv, got_u, out_z, out_y = together(d_query, d_kv, got_u, out_z, out_y)
    d_query = d_query.reshape(4 * rows, share)
    out_z, out_y = side_step(out_parts, out_z, out_y, yy, zz)
    grad_d = scatter_high(grad_d, r, high, 0)

    d_h_one = scatter_four_core(dot_t(d_query, wq_cols).reshape(4, rows, width), core)
    from_h = swap(d_h_one[1].astype(BF16), yy)
    from_h, out_z, out_y, grad_d = together(from_h, out_z, out_y, grad_d)
    d_wdown = grad_d[:chunk]
    output = (resid + out_parts[0] + out_z.astype(F32) + out_y.astype(F32)).astype(BF16)
    d_h_one = d_h_one[0] + from_h.astype(F32)
    scaled_one = d_h_one * gain_attn
    d_tokens = (
        d_resid
        + inv_one
        * (scaled_one - normed_one * jnp.mean(scaled_one * normed_one, axis=1, keepdims=True))
    ).astype(BF16)

    def on(got, keep):
        grad = (keep + got.astype(F32)).reshape(4, outer, 2, out_rows, mine)
        grad = scatter_high(grad, r, high, 1).astype(BF16)
        other = swap(pick(grad, 1 - z_bit, 1), zz)
        grad = jnp.stack([pick(grad, z_bit, 1), other])
        return jnp.stack(exchange_four([pick(grad, g ^ j, 1) for j in range(4)], core, yy))

    grad_g = on(got_g, keep_g)
    grad_u = on(got_u, keep_u)
    gate_rows = lax.dynamic_slice_in_dim(w_gate, r * out_rows, out_rows, 0)
    up_rows = lax.dynamic_slice_in_dim(w_up, r * out_rows, out_rows, 0)
    gain_at = (g * reps + r) * out_rows
    gain_rows = lax.dynamic_slice_in_dim(gain_ffn, gain_at, out_rows, 0)
    d_wgate, d_wup, d_gain_two = unpack(
        info, grad_g, grad_u, gate_rows, up_rows, gain_rows[:, None], outer, chunk, wide
    )

    d_wout = t_dot(attn_rows, d_group).reshape(reps, out_rows, width)
    d_wout = scatter_rep(d_wout, r, high)
    d_kv = d_kv.reshape((outer, 2, 2) + d_kv.shape[1:])
    d_kv = d_kv[:, 0].astype(F32) + swap(d_kv[:, 1], zz).astype(F32)
    d_kv = d_kv[:, 0] + swap(d_kv[:, 1].astype(BF16), xx).astype(F32)
    for mask in reversed(high):
        d_kv = d_kv.reshape((2, d_kv.shape[0] // 2) + d_kv.shape[1:])
        d_kv = d_kv[0] + swap(d_kv[1].astype(BF16), mask).astype(F32)
    d_kv = d_kv[0].astype(BF16)
    d_kv = absolute(exchange_four([d_kv[j] for j in range(4)], core, yy), g)
    d_keys = jnp.concatenate([piece[:, :HD] for piece in d_kv], axis=1)
    d_values = jnp.concatenate([piece[:, HD:] for piece in d_kv], axis=1)
    d_wq = t_dot(h_group, d_query).reshape(4, reps, out_rows, share)
    d_wq = scatter_rep(jnp.swapaxes(d_wq, 0, 1), r, high).astype(BF16)
    d_wq = absolute(exchange_four([pick(d_wq, g ^ j, 0) for j in range(4)], core, yy), g)
    d_wquery = jnp.concatenate(d_wq, axis=1).astype(F32)
    query_rows = lax.dynamic_slice_in_dim(w_query, r * out_rows, out_rows, 0)
    gain_rows = lax.dynamic_slice_in_dim(gain_attn, gain_at, out_rows, 0)
    d_gain_one = jnp.sum(d_wquery * query_rows.astype(F32), axis=1) / gain_rows
    return (
        output,
        d_tokens,
        d_gain_one,
        d_gain_two[:, 0],
        d_wquery,
        d_wout,
        d_wgate,
        d_wup,
        d_wdown,
        d_keys,
        d_values,
    )


def solution(mesh):
    spread = P(BOTH, None)
    member = P("grp", None)
    in_specs = (
        spread,
        spread,
        P(),
        P(),
        member,
        member,
        member,
        member,
        member,
        spread,
        spread,
        P(),
    )
    out_specs = (
        spread,
        spread,
        P(BOTH),
        P(BOTH),
        spread,
        spread,
        spread,
        spread,
        spread,
        spread,
        spread,
    )
    return jax.shard_map(
        on_device, mesh=mesh, in_specs=in_specs, out_specs=out_specs, check_vma=False
    )
```

time: 748 us -> 496 us (0.66)
  waiting for transfers between devices: 339 us -> 216 us
  local copies, waits for them, and re-layouts: 144 us -> 45.8 us
  blocking collectives: 37 us -> 0 us
  Pallas kernels: 26.1 us -> 54.8 us
  starting transfers between devices: 40.3 us -> 68.9 us
  other arithmetic: 81.1 us -> 57.3 us
  between operations: 16.5 us -> 2.69 us
  matrix products: 54.2 us -> 45 us
    ppermute x52 -> x75, waiting for transfers between devices: 283 us -> 213 us  [swap(): return lax.ppermute(value, BOTH, [(i, i ^ mask) for i in range(count)])]
    reduce_scatter x2 -> x0, waiting for transfers between devices: 56.7 us -> none  [the longest x1 56.7 us: on_device(): lax.psum_scatter(t_dot(attn_rows, d_group).astype(BF16), 'rep', scatter_d...]
    unnamed x196 -> x176, local copies, waits for them, and re-layouts: 77.3 us -> 21.3 us
    unnamed x1 -> x0, blocking collectives: 37 us -> none
    pallas_call x0 -> x5, Pallas kernels: none -> 28.7 us  [the longest x1 11.3 us: columns_grad(): pl.pallas_call(functools.partial(columns_grad_kernel, rows, mine), grid=(...]
    slice x33 -> x10, local copies, waits for them, and re-layouts: 29.3 us -> 5.04 us  [the longest x2 1.93 us: on_device(): low, upp = (swap(h_y[:rows // 2], zz), swap(h_z[rows // 2:], yy))]
    ppermute x52 -> x75, starting transfers between devices: 39.7 us -> 61.4 us  [swap(): return lax.ppermute(value, BOTH, [(i, i ^ mask) for i in range(count)])]
    dot_general x5 -> x2, matrix products: 20.7 us -> 2.52 us  [t_dot(): lax.dot_general(a, b, (((0,), (0,)), ((), ())), preferred_element_type=F32)]
  transfers between devices with their start and end apart: 56 -> 78, of which waited for: 26 -> 31; matrix products, arithmetic and copies ran while one was open for 31% -> 24% of each run, Pallas kernels for 4% -> 11%
where the time goes in v2:
time: 496 us; the launch traced here: 491 us
  waiting for transfers between devices  216 us (44%)
  starting transfers between devices  68.9 us (14%)
  other arithmetic  57.3 us (12%)
  Pallas kernels  54.8 us (11%)
  local copies, waits for them, and re-layouts  45.8 us (9%)
  matrix products  45 us (9%)
    ppermute x75, waiting for transfers between devices, swap(): return lax.ppermute(value, BOTH, [(i, i ^ mask) for i in range(count)])  213 us
    ppermute x75, starting transfers between devices, swap(): return lax.ppermute(value, BOTH, [(i, i ^ mask) for i in range(count)])  61.4 us
    dot_general x6, matrix products, dot_t(): lax.dot_general(a, b, (((1,), (1,)), ((), ())), preferred_element_type=F32)  23.2 us
    unnamed x176, local copies, waits for them, and re-layouts  21.3 us
    dot_general x6, matrix products, dot(): return jnp.dot(a, b, preferred_element_type=F32)  19.3 us
    pallas_call x1, Pallas kernels, attend_back(): pl.pallas_call(functools.partial(attend_back_kernel, reps), grid=(4,), in...  16.2 us
    pallas_call x1, Pallas kernels, columns_grad(): pl.pallas_call(functools.partial(columns_grad_kernel, rows, mine), grid=(...  11.3 us
  transfers between devices with their start and end apart: 78, of which 31 were waited for; matrix products, arithmetic and copies ran while one was open for 24% of the time, Pallas kernels for 11%

profile of v2, /device:TPU:0, one launch (start us, length us, event | category | flops | bytes accessed | tf_op | source)
XLA Modules:
  0.0 490.9 jit_solution(11649690609163239777)
XLA Ops:
  15.4 6.6 %collective-permute-done.2 = bf16[2,128,256]{2,1,0:T(8,128)(2,1)S(1)} collective-permute-done((bf16[2,128,256]{2,1,0:T(8,128)(2,1)S(1)}, bf16[2,128,256]{2,1,0:T(8,128)(2,1)S(1)}, u32[]{:S(2)}, u32[]{:S(2)}) %collective-permute-start.2) | collective-permute-done | bytes 131104 | tf_op jit(solution)/shard_map/ppermute | solution.py:21
  36.2 5.6 %pack.1 = (bf16[512,1536]{1,0:T(8,128)(2,1)S(1)}, bf16[512,1536]{1,0:T(8,128)(2,1)}, bf16[256,1536]{1,0:T(8,128)(2,1)}, bf16[256,1536]{1,0:T(8,128)(2,1)S(1)}) custom-call(s32[2]{0:T(128)S(1)} %pad_add_fusion.info_ref, bf16[512,5504]{1,0:T(8,128)(2,1)S(1)} %bitcast.337, bf16[512,5504]{1,0:T(8,128)(2,1)S(1)} %copy-done.4), custom_call_target="tpu_custom_call" | custom-call | flops 1 | bytes 1 | tf_op jit(solution)/shard_map/pack/pallas_call | solution.py:177
  50.9 6.6 %collective-permute-done.8 = bf16[2,256,512]{2,1,0:T(8,128)(2,1)S(1)} collective-permute-done((bf16[2,256,512]{2,1,0:T(8,128)(2,1)S(1)}, bf16[2,256,512]{2,1,0:T(8,128)(2,1)S(1)}, u32[]{:S(2)}, u32[]{:S(2)}) %collective-permute-start.8) | collective-permute-done | bytes 524320 | tf_op jit(solution)/shard_map/ppermute | solution.py:21
  83.2 6.1 %collective-permute-done.18 = bf16[256,1536]{1,0:T(8,128)(2,1)} collective-permute-done((bf16[256,1536]{1,0:T(8,128)(2,1)S(1)}, bf16[256,1536]{1,0:T(8,128)(2,1)}, u32[]{:S(2)}, u32[]{:S(2)}) %collective-permute-start.18) | collective-permute-done | bytes 786464 | tf_op jit(solution)/shard_map/ppermute | solution.py:21
  93.0 9.9 %attend.1 = (bf16[4,128,512]{2,1,0:T(8,128)(2,1)S(1)}, f32[4,512,1]{2,1,0:T(8,128)S(1)}) custom-call(s32[2]{0:T(128)S(1)} %pad_add_fusion.info_ref, s32[8]{0:T(128)S(1)} %and_add_fusion.slots_ref, s32[8]{0:T(128)S(1)} %copy-done.22, bf16[4,128,512]{2,1,0:T(8,128)(2,1)S(1)} %bitcast.340, bf16[8,4,128,256]{3,2,1,0:T(8,128)(2,1)S(1)} %bitcast_dynamic-update-slice_fusion.kv_ref), custom_call_target="tpu_custom_call" | custom-call | flops 1 | bytes 1 | tf_op jit(solution)/shard_map/attend/pallas_call | solution.py:393
  102.9 5.5 %collective-permute-done.19 = bf16[256,1536]{1,0:T(8,128)(2,1)} collective-permute-done((bf16[256,1536]{1,0:T(8,128)(2,1)}, bf16[256,1536]{1,0:T(8,128)(2,1)}, u32[]{:S(2)}, u32[]{:S(2)}) %collective-permute-start.19) | collective-permute-done | bytes 786464 | tf_op jit(solution)/shard_map/ppermute | solution.py:21
  123.6 7.0 %collective-permute-done.22 = bf16[256,1536]{1,0:T(8,128)(2,1)} collective-permute-done((bf16[256,1536]{1,0:T(8,128)(2,1)}, bf16[256,1536]{1,0:T(8,128)(2,1)}, u32[]{:S(2)}, u32[]{:S(2)}) %collective-permute-start.22) | collective-permute-done | bytes 786464 | tf_op jit(solution)/shard_map/ppermute | solution.py:21
  139.8 6.6 %collective-permute-done.25 = bf16[2,128,2048]{2,1,0:T(8,128)(2,1)} collective-permute-done((bf16[2,128,2048]{2,1,0:T(8,128)(2,1)}, bf16[2,128,2048]{2,1,0:T(8,128)(2,1)}, u32[]{:S(2)}, u32[]{:S(2)}) %collective-permute-start.25) | collective-permute-done | bytes 1048608 | tf_op jit(solution)/shard_map/ppermute | solution.py:21
  146.7 10.8 %collective-permute-done.24 = bf16[128,2048]{1,0:T(8,128)(2,1)} collective-permute-done((bf16[128,2048]{1,0:T(8,128)(2,1)}, bf16[128,2048]{1,0:T(8,128)(2,1)}, u32[]{:S(2)}, u32[]{:S(2)}) %collective-permute-start.24) | collective-permute-done | bytes 524320 | tf_op jit(solution)/shard_map/ppermute | solution.py:21
  194.5 6.3 %fusion.79 = f32[512,1536]{1,0:T(8,128)S(1)} fusion(bf16[512,2048]{1,0:T(8,128)(2,1)} %copy-done.44, bf16[512,1536]{1,0:T(8,128)(2,1)} %copy-done.57, bf16[512,1536]{1,0:T(8,128)(2,1)} %copy-done.60, bf16[512,1536]{1,0:T(8,128)(2,1)} %copy-done.59, bf16[512,1536]{1,0:T(8,128)(2,1)} %copy-done.58), kind=kOutput, calls=%fused_computation.289 | convolution fusion | flops 3246391296 | bytes 11534336 | tf_op jit(solution)/shard_map/dot_general | solution.py:33
  205.4 7.2 %rows_grad.1 = (bf16[384,2048]{1,0:T(8,128)(2,1)}, f32[384,2048]{1,0:T(8,128)}) custom-call(s32[2]{0:T(128)S(1)} %pad_add_fusion.info_ref, bf16[512,768]{1,0:T(8,128)(2,1)S(1)} %get-tuple-element.170.ha, bf16[512,768]{1,0:T(8,128)(2,1)S(1)} %copy-done.16, bf16[512,2048]{1,0:T(8,128)(2,1)S(1)} %bitcast.335, bf16[512,2048]{1,0:T(8,128)(2,1)} %copy-done.52), custom_call_target="tpu_custom_call" | custom-call | flops 1 | bytes 1 | tf_op jit(solution)/shard_map/rows_grad/pallas_call | solution.py:284
  214.3 7.4 %fusion.92 = (bf16[512,2048]{1,0:T(8,128)(2,1)S(1)}, f32[512,2048]{1,0:T(8,128)S(1)}) fusion(bf16[512,2048]{1,0:T(8,128)(2,1)} %collective-permute-done.34, bf16[512,1536]{1,0:T(8,128)(2,1)} %copy-done.57, bf16[512,1536]{1,0:T(8,128)(2,1)} %copy-done.60, bf16[512,1536]{1,0:T(8,128)(2,1)} %copy-done.59, bf16[512,1536]{1,0:T(8,128)(2,1)} %copy-done.58, ...), kind=kOutput, calls=%fused_computation.300 | convolution fusion | flops 3252682752 | bytes 16252928 | tf_op jit(solution)/shard_map/dot_general | solution.py:37
  223.1 7.4 %collective-permute-done.35 = bf16[64,2048]{1,0:T(8,128)(2,1)S(1)} collective-permute-done((bf16[64,2048]{1,0:T(8,128)(2,1)S(1)}, bf16[64,2048]{1,0:T(8,128)(2,1)S(1)}, u32[]{:S(2)}, u32[]{:S(2)}) %collective-permute-start.35) | collective-permute-done | bytes 262176 | tf_op jit(solution)/shard_map/ppermute | solution.py:21
  240.1 11.3 %columns_grad.1 = (bf16[1024,768]{1,0:T(8,128)(2,1)}, bf16[1024,768]{1,0:T(8,128)(2,1)}, f32[1024,768]{1,0:T(8,128)}, f32[1024,768]{1,0:T(8,128)}) custom-call(s32[2]{0:T(128)} %copy-done.19, bf16[512,2048]{1,0:T(8,128)(2,1)} %copy-done.44, bf16[512,2048]{1,0:T(8,128)(2,1)} %copy-done.55, bf16[512,1536]{1,0:T(8,128)(2,1)} %pad_maximum_fusion.7.da, ...), custom_call_target="tpu_custom_call" | custom-call | flops 1 | bytes 1 | tf_op jit(solution)/shard_map/columns_grad/pallas_call | solution.py:255
  261.2 9.1 %collective-permute-done.40 = bf16[128,2048]{1,0:T(8,128)(2,1)S(1)} collective-permute-done((bf16[128,2048]{1,0:T(8,128)(2,1)S(1)}, bf16[128,2048]{1,0:T(8,128)(2,1)S(1)}, u32[]{:S(2)}, u32[]{:S(2)}) %collective-permute-start.40) | collective-permute-done | bytes 524320 | tf_op jit(solution)/shard_map/ppermute | solution.py:21
  275.1 22.7 %collective-permute-done.52 = bf16[1,192,2048]{2,1,0:T(8,128)(2,1)S(1)} collective-permute-done((bf16[1,192,2048]{2,1,0:T(8,128)(2,1)S(1)}, bf16[1,192,2048]{2,1,0:T(8,128)(2,1)S(1)}, u32[]{:S(2)}, u32[]{:S(2)}) %collective-permute-start.52) | collective-permute-done | bytes 786464 | tf_op jit(solution)/shard_map/ppermute | solution.py:21
  312.5 16.2 %attend_back.1 = (bf16[4,128,512]{2,1,0:T(8,128)(2,1)}, bf16[8,4,128,256]{3,2,1,0:T(8,128)(2,1)}) custom-call(s32[2]{0:T(128)} %copy-done.19, s32[8]{0:T(128)} %copy-done.21, s32[8]{0:T(128)} %starts_ref.3, bf16[4,128,512]{2,1,0:T(8,128)(2,1)} %bitcast.341, bf16[4,128,512]{2,1,0:T(8,128)(2,1)} %bitcast.371, bf16[4,128,512]{2,1,0:T(8,128)(2,1)} %copy-done.8, ...), custom_call_target="tpu_custom_call" | custom-call | flops 1 | bytes 1 | tf_op jit(solution)/shard_map/attend_back/pallas_call | solution.py:479
  343.5 6.0 %collective-permute-done.69 = bf16[2,2,64,2048]{3,2,1,0:T(8,128)(2,1)} collective-permute-done((bf16[2,2,64,2048]{3,2,1,0:T(8,128)(2,1)}, bf16[2,2,64,2048]{3,2,1,0:T(8,128)(2,1)}, u32[]{:S(2)}, u32[]{:S(2)}) %collective-permute-start.69) | collective-permute-done | bytes 1048608 | tf_op jit(solution)/shard_map/ppermute | solution.py:21
  352.7 20.9 %collective-permute-done.64 = bf16[4,1,2,64,768]{4,3,2,0,1:T(8,128)(2,1)S(1)} collective-permute-done((bf16[4,1,2,64,768]{4,3,2,0,1:T(8,128)(2,1)S(1)}, bf16[4,1,2,64,768]{4,3,2,0,1:T(8,128)(2,1)S(1)}, u32[]{:S(2)}, u32[]{:S(2)}) %collective-permute-start.64) | collective-permute-done | bytes 786464 | tf_op jit(solution)/shard_map/ppermute | solution.py:21
  375.3 23.5 %collective-permute-done.60 = bf16[4,64,768]{2,1,0:T(8,128)(2,1)S(1)} collective-permute-done((bf16[4,64,768]{2,1,0:T(8,128)(2,1)S(1)}, bf16[4,64,768]{2,1,0:T(8,128)(2,1)S(1)}, u32[]{:S(2)}, u32[]{:S(2)}) %collective-permute-start.60) | collective-permute-done | bytes 393248 | tf_op jit(solution)/shard_map/ppermute | solution.py:21
  402.3 21.6 %collective-permute-done.53 = bf16[2,2,4,64,512]{4,3,1,0,2:T(8,128)(2,1)S(1)} collective-permute-done((bf16[2,2,4,64,512]{4,3,1,0,2:T(8,128)(2,1)S(1)}, bf16[2,2,4,64,512]{4,3,1,0,2:T(8,128)(2,1)S(1)}, u32[]{:S(2)}, u32[]{:S(2)}) %collective-permute-start.53) | collective-permute-done | bytes 1048608 | tf_op jit(solution)/shard_map/ppermute | solution.py:21
  426.8 9.1 %collective-permute-done.62 = bf16[2,2,64,768]{3,2,1,0:T(8,128)(2,1)S(1)} collective-permute-done((bf16[2,2,64,768]{3,2,1,0:T(8,128)(2,1)S(1)}, bf16[2,2,64,768]{3,2,1,0:T(8,128)(2,1)S(1)}, u32[]{:S(2)}, u32[]{:S(2)}) %collective-permute-start.62) | collective-permute-done | bytes 393248 | tf_op jit(solution)/shard_map/ppermute | solution.py:21
  439.4 7.8 %collective-permute-done.49 = bf16[128,2048]{1,0:T(8,128)(2,1)S(1)} collective-permute-done((bf16[128,2048]{1,0:T(8,128)(2,1)S(1)}, bf16[128,2048]{1,0:T(8,128)(2,1)S(1)}, u32[]{:S(2)}, u32[]{:S(2)}) %collective-permute-start.49) | collective-permute-done | bytes 524320 | tf_op jit(solution)/shard_map/ppermute | solution.py:21
  457.7 12.5 %collective-permute-done.71 = bf16[1,64,2048]{2,1,0:T(8,128)(2,1)S(1)} collective-permute-done((bf16[1,64,2048]{2,1,0:T(8,128)(2,1)S(1)}, bf16[1,64,2048]{2,1,0:T(8,128)(2,1)S(1)}, u32[]{:S(2)}, u32[]{:S(2)}) %collective-permute-start.71) | collective-permute-done | bytes 262176 | tf_op jit(solution)/shard_map/ppermute | solution.py:21
  (459 shorter events, 234.4 us)
Async XLA Ops:
  4.1 41.6 %collective-permute-start.5 = (bf16[128,2048]{1,0:T(8,128)(2,1)}, bf16[128,2048]{1,0:T(8,128)(2,1)}, u32[]{:S(2)}, u32[]{:S(2)}) collective-permute-start(bf16[128,2048]{1,0:T(8,128)(2,1)} %fusion.16), channel_id=1, source_target_pairs={{0,16},{1,17},{2,18},{3,19},{4,20},{5,21},{6,22},{7,23},{8,24},{9,... | collective-permute-start | bytes 1572872 | tf_op jit(solution)/shard_map/ppermute | solution.py:21
  7.1 52.6 %collective-permute-start = (bf16[128,2048]{1,0:T(8,128)(2,1)}, bf16[128,2048]{1,0:T(8,128)(2,1)}, u32[]{:S(2)}, u32[]{:S(2)}) collective-permute-start(bf16[128,2048]{1,0:T(8,128)(2,1)} %fusion.16), channel_id=1, source_target_pairs={{0,8},{1,9},{2,10},{3,11},{4,12},{5,13},{6,14},{7,15},{8,0},{9,1},... | collective-permute-start | bytes 1572872 | tf_op jit(solution)/shard_map/ppermute | solution.py:21
  57.5 33.2 %collective-permute-start.13 = (bf16[512,512]{1,0:T(8,128)(2,1)S(1)}, bf16[512,512]{1,0:T(8,128)(2,1)S(1)}, u32[]{:S(2)}, u32[]{:S(2)}) collective-permute-start(bf16[512,512]{1,0:T(8,128)(2,1)S(1)} %copy-done.69), channel_id=1, source_target_pairs={{0,8},{1,9},{2,10},{3,11},{4,12},{5,13},{6,14},{7,15},{8,0},{9,1},... | collective-permute-start | bytes 1572872 | tf_op jit(solution)/shard_map/ppermute | solution.py:21
  116.6 54.8 %collective-permute-start.31 = (bf16[512,1536]{1,0:T(8,128)(2,1)}, bf16[512,1536]{1,0:T(8,128)(2,1)}, u32[]{:S(2)}, u32[]{:S(2)}) collective-permute-start(bf16[512,1536]{1,0:T(8,128)(2,1)} %get-tuple-element.106), channel_id=1, source_target_pairs={{0,8},{1,9},{2,10},{3,11},{4,12},{5,13},{6,14},{7,15},{8,0},{9,1},... | collective-permute-start | bytes 4718600 | tf_op jit(solution)/shard_map/ppermute | solution.py:21
  119.4 27.0 %collective-permute-start.25 = (bf16[2,128,2048]{2,1,0:T(8,128)(2,1)}, bf16[2,128,2048]{2,1,0:T(8,128)(2,1)}, u32[]{:S(2)}, u32[]{:S(2)}) collective-permute-start(bf16[2,128,2048]{2,1,0:T(8,128)(2,1)} %get-tuple-element.98), channel_id=1, source_target_pairs={{0,2},{1,3},{2,0},{3,1},{4,6},{5,7},{6,4},{7,5},{8,10},{9,11},{10,... | collective-permute-start | bytes 3145736 | tf_op jit(solution)/shard_map/ppermute | solution.py:21
  122.1 44.5 %collective-permute-start.28 = (bf16[256,1536]{1,0:T(8,128)(2,1)}, bf16[256,1536]{1,0:T(8,128)(2,1)}, u32[]{:S(2)}, u32[]{:S(2)}) collective-permute-start(bf16[256,1536]{1,0:T(8,128)(2,1)} %collective-permute-done.19), channel_id=1, source_target_pairs={{0,1},{1,0},{2,3},{3,2},{4,5},{5,4},{6,7},{7,6},{8,9},{9,8},{10,11... | collective-permute-start | bytes 2359304 | tf_op jit(solution)/shard_map/ppermute | solution.py:21
  212.7 38.7 %collective-permute-start.39 = (bf16[384,2048]{1,0:T(8,128)(2,1)}, bf16[384,2048]{1,0:T(8,128)(2,1)}, u32[]{:S(2)}, u32[]{:S(2)}) collective-permute-start(bf16[384,2048]{1,0:T(8,128)(2,1)} %get-tuple-element.110), channel_id=1, source_target_pairs={{0,1},{1,0},{2,3},{3,2},{4,5},{5,4},{6,7},{7,6},{8,9},{9,8},{10,11... | collective-permute-start | bytes 4718600 | tf_op jit(solution)/shard_map/ppermute | solution.py:21
  256.6 42.9 %collective-permute-start.44 = (bf16[1024,768]{1,0:T(8,128)(2,1)S(1)}, bf16[1024,768]{1,0:T(8,128)(2,1)S(1)}, u32[]{:S(2)}, u32[]{:S(2)}) collective-permute-start(bf16[1024,768]{1,0:T(8,128)(2,1)S(1)} %copy-done.80), channel_id=1, source_target_pairs={{0,1},{1,0},{2,3},{3,2},{4,5},{5,4},{6,7},{7,6},{8,9},{9,8},{10,11... | collective-permute-start | bytes 4718600 | tf_op jit(solution)/shard_map/ppermute | solution.py:21
  257.1 71.6 %collective-permute-start.45 = (bf16[1024,768]{1,0:T(8,128)(2,1)}, bf16[1024,768]{1,0:T(8,128)(2,1)}, u32[]{:S(2)}, u32[]{:S(2)}) collective-permute-start(bf16[1024,768]{1,0:T(8,128)(2,1)} %get-tuple-element.126), channel_id=1, source_target_pairs={{0,1},{1,0},{2,3},{3,2},{4,5},{5,4},{6,7},{7,6},{8,9},{9,8},{10,11... | collective-permute-start | bytes 4718600 | tf_op jit(solution)/shard_map/ppermute | solution.py:21
  260.8 37.0 %collective-permute-start.52 = (bf16[1,192,2048]{2,1,0:T(8,128)(2,1)S(1)}, bf16[1,192,2048]{2,1,0:T(8,128)(2,1)S(1)}, u32[]{:S(2)}, u32[]{:S(2)}) collective-permute-start(bf16[1,192,2048]{2,1,0:T(8,128)(2,1)S(1)} %fusion.36), channel_id=1, source_target_pairs={{0,4},{1,5},{2,6},{3,7},{4,0},{5,1},{6,2},{7,3},{8,12},{9,13},{10,... | collective-permute-start | bytes 2359304 | tf_op jit(solution)/shard_map/ppermute | solution.py:21
  270.2 29.0 %collective-permute-start.43 = (bf16[128,2048]{1,0:T(8,128)(2,1)S(1)}, bf16[128,2048]{1,0:T(8,128)(2,1)S(1)}, u32[]{:S(2)}, u32[]{:S(2)}) collective-permute-start(bf16[128,2048]{1,0:T(8,128)(2,1)S(1)} %collective-permute-done.40), channel_id=1, source_target_pairs={{0,8},{1,9},{2,10},{3,11},{4,12},{5,13},{6,14},{7,15},{8,0},{9,1},... | collective-permute-start | bytes 1572872 | tf_op jit(solution)/shard_map/ppermute | solution.py:21
  300.7 28.0 %collective-permute-start.46 = (bf16[64,2048]{1,0:T(8,128)(2,1)}, bf16[64,2048]{1,0:T(8,128)(2,1)}, u32[]{:S(2)}, u32[]{:S(2)}) collective-permute-start(bf16[64,2048]{1,0:T(8,128)(2,1)} %get-tuple-element.176), channel_id=1, source_target_pairs={{0,16},{1,17},{2,18},{3,19},{4,20},{5,21},{6,22},{7,23},{8,24},{9,... | collective-permute-start | bytes 786440 | tf_op jit(solution)/shard_map/ppermute | solution.py:21
  302.2 26.5 %collective-permute-start.47 = (bf16[64,2048]{1,0:T(8,128)(2,1)}, bf16[64,2048]{1,0:T(8,128)(2,1)}, u32[]{:S(2)}, u32[]{:S(2)}) collective-permute-start(bf16[64,2048]{1,0:T(8,128)(2,1)} %get-tuple-element.175), channel_id=1, source_target_pairs={{0,2},{1,3},{2,0},{3,1},{4,6},{5,7},{6,4},{7,5},{8,10},{9,11},{10,... | collective-permute-start | bytes 786440 | tf_op jit(solution)/shard_map/ppermute | solution.py:21
  303.6 36.5 %collective-permute-start.59 = (bf16[4,1,2,64,768]{4,3,2,0,1:T(8,128)(2,1)}, bf16[4,1,2,64,768]{4,3,2,0,1:T(8,128)(2,1)}, u32[]{:S(2)}, u32[]{:S(2)}) collective-permute-start(bf16[4,1,2,64,768]{4,3,2,0,1:T(8,128)(2,1)} %fusion.37), channel_id=1, source_target_pairs={{0,4},{1,5},{2,6},{3,7},{4,0},{5,1},{6,2},{7,3},{8,12},{9,13},{10,... | collective-permute-start | bytes 2359304 | tf_op jit(solution)/shard_map/ppermute | solution.py:21
  309.9 39.6 %collective-permute-start.69 = (bf16[2,2,64,2048]{3,2,1,0:T(8,128)(2,1)}, bf16[2,2,64,2048]{3,2,1,0:T(8,128)(2,1)}, u32[]{:S(2)}, u32[]{:S(2)}) collective-permute-start(bf16[2,2,64,2048]{3,2,1,0:T(8,128)(2,1)} %fusion.25), channel_id=1, source_target_pairs={{0,1},{1,0},{2,3},{3,2},{4,5},{5,4},{6,7},{7,6},{8,9},{9,8},{10,11... | collective-permute-start | bytes 3145736 | tf_op jit(solution)/shard_map/ppermute | solution.py:21
  332.0 67.7 %collective-permute-start.48 = (bf16[2,128,2048]{2,1,0:T(8,128)(2,1)S(1)}, bf16[2,128,2048]{2,1,0:T(8,128)(2,1)S(1)}, u32[]{:S(2)}, u32[]{:S(2)}) collective-permute-start(bf16[2,128,2048]{2,1,0:T(8,128)(2,1)S(1)} %fusion.27), channel_id=1, source_target_pairs={{0,8},{1,9},{2,10},{3,11},{4,12},{5,13},{6,14},{7,15},{8,0},{9,1},... | collective-permute-start | bytes 3145736 | tf_op jit(solution)/shard_map/ppermute | solution.py:21
  333.5 104.6 %collective-permute-start.50 = (bf16[128,2048]{1,0:T(8,128)(2,1)S(1)}, bf16[128,2048]{1,0:T(8,128)(2,1)S(1)}, u32[]{:S(2)}, u32[]{:S(2)}) collective-permute-start(bf16[128,2048]{1,0:T(8,128)(2,1)S(1)} %pad_maximum_fusion.16), channel_id=1, source_target_pairs={{0,2},{1,3},{2,0},{3,1},{4,6},{5,7},{6,4},{7,5},{8,10},{9,11},{10,... | collective-permute-start | bytes 1572872 | tf_op jit(solution)/shard_map/ppermute | solution.py:21
  336.2 37.5 %collective-permute-start.64 = (bf16[4,1,2,64,768]{4,3,2,0,1:T(8,128)(2,1)S(1)}, bf16[4,1,2,64,768]{4,3,2,0,1:T(8,128)(2,1)S(1)}, u32[]{:S(2)}, u32[]{:S(2)}) collective-permute-start(bf16[4,1,2,64,768]{4,3,2,0,1:T(8,128)(2,1)S(1)} %fusion.38), channel_id=1, source_target_pairs={{0,4},{1,5},{2,6},{3,7},{4,0},{5,1},{6,2},{7,3},{8,12},{9,13},{10,... | collective-permute-start | bytes 2359304 | tf_op jit(solution)/shard_map/ppermute | solution.py:21
  340.2 59.2 %collective-permute-start.72 = (bf16[2,2,4,128,256]{4,3,2,0,1:T(8,128)(2,1)S(1)}, bf16[2,2,4,128,256]{4,3,2,0,1:T(8,128)(2,1)S(1)}, u32[]{:S(2)}, u32[]{:S(2)}) collective-permute-start(bf16[2,2,4,128,256]{4,3,2,0,1:T(8,128)(2,1)S(1)} %bitcast.364), channel_id=1, source_target_pairs={{0,2},{1,3},{2,0},{3,1},{4,6},{5,7},{6,4},{7,5},{8,10},{9,11},{10,... | collective-permute-start | bytes 3145736 | tf_op jit(solution)/shard_map/ppermute | solution.py:21
  349.5 49.3 %collective-permute-start.60 = (bf16[4,64,768]{2,1,0:T(8,128)(2,1)S(1)}, bf16[4,64,768]{2,1,0:T(8,128)(2,1)S(1)}, u32[]{:S(2)}, u32[]{:S(2)}) collective-permute-start(bf16[4,64,768]{2,1,0:T(8,128)(2,1)S(1)} %get-tuple-element.201), channel_id=1, source_target_pairs={{0,2},{1,3},{2,0},{3,1},{4,6},{5,7},{6,4},{7,5},{8,10},{9,11},{10,... | collective-permute-start | bytes 1179656 | tf_op jit(solution)/shard_map/ppermute | solution.py:21
  373.7 65.7 %collective-permute-start.51 = (bf16[128,2048]{1,0:T(8,128)(2,1)S(1)}, bf16[128,2048]{1,0:T(8,128)(2,1)S(1)}, u32[]{:S(2)}, u32[]{:S(2)}) collective-permute-start(bf16[128,2048]{1,0:T(8,128)(2,1)S(1)} %pad_maximum_fusion.17), channel_id=1, source_target_pairs={{0,16},{1,17},{2,18},{3,19},{4,20},{5,21},{6,22},{7,23},{8,24},{9,... | collective-permute-start | bytes 1572872 | tf_op jit(solution)/shard_map/ppermute | solution.py:21
  439.4 32.9 %collective-permute-start.66 = (bf16[2,64,768]{2,1,0:T(8,128)(2,1)S(1)}, bf16[2,64,768]{2,1,0:T(8,128)(2,1)S(1)}, u32[]{:S(2)}, u32[]{:S(2)}) collective-permute-start(bf16[2,64,768]{2,1,0:T(8,128)(2,1)S(1)} %get-tuple-element.192), channel_id=1, source_target_pairs={{0,8},{1,9},{2,10},{3,11},{4,12},{5,13},{6,14},{7,15},{8,0},{9,1},... | collective-permute-start | bytes 589832 | tf_op jit(solution)/shard_map/ppermute | solution.py:21
  448.5 27.4 %collective-permute-start.55 = (bf16[1,4,64,512]{3,2,0,1:T(8,128)(2,1)}, bf16[1,4,64,512]{3,2,0,1:T(8,128)(2,1)}, u32[]{:S(2)}, u32[]{:S(2)}) collective-permute-start(bf16[1,4,64,512]{3,2,0,1:T(8,128)(2,1)} %dynamic-slice_convert_fusion.8), channel_id=1, source_target_pairs={{0,4},{1,5},{2,6},{3,7},{4,0},{5,1},{6,2},{7,3},{8,12},{9,13},{10,... | collective-permute-start | bytes 786440 | tf_op jit(solution)/shard_map/ppermute | solution.py:21
  452.4 28.1 %collective-permute-start.74 = (bf16[1,4,128,256]{3,2,1,0:T(8,128)(2,1)}, bf16[1,4,128,256]{3,2,1,0:T(8,128)(2,1)}, u32[]{:S(2)}, u32[]{:S(2)}) collective-permute-start(bf16[1,4,128,256]{3,2,1,0:T(8,128)(2,1)} %slice.472), channel_id=1, source_target_pairs={{0,4},{1,5},{2,6},{3,7},{4,0},{5,1},{6,2},{7,3},{8,12},{9,13},{10,... | collective-permute-start | bytes 786440 | tf_op jit(solution)/shard_map/ppermute | solution.py:21
  (137 other events, 1787.0 us)

commit v3 on v2

--- a/solution.py
+++ b/solution.py
@@ -51,16 +51,11 @@
     return parts[:, 0] + got.astype(F32)
 
 
-def corner_step(parts, yy, zz):
-    half = parts.shape[1] // 2
-    corner = parts[3].astype(BF16)
-    return swap(corner[:half], yy), swap(corner[half:], zz)
-
-
-def side_step(parts, to_z, to_y, yy, zz):
-    half = parts.shape[1] // 2
-    for_z = jnp.concatenate([parts[2, :half] + to_z.astype(F32), parts[2, half:]])
-    for_y = jnp.concatenate([parts[1, :half], parts[1, half:] + to_y.astype(F32)])
+def side_step(parts, to_z, to_y, rows, yy, zz):
+    half = rows // 2
+    for_z = [parts[2 * rows : 2 * rows + half] + to_z.astype(F32), parts[2 * rows + half :]]
+    for_y = [parts[rows : rows + half], parts[rows + half : 2 * rows] + to_y.astype(F32)]
+    for_z, for_y = jnp.concatenate(for_z), jnp.concatenate(for_y)
     return swap(for_z.astype(BF16), zz), swap(for_y.astype(BF16), yy)
 
 
@@ -84,27 +79,22 @@
     ]
 
 
-def halve(value, bit, mask, axis, hold=None):
-    got = swap(pick(value, 1 - bit, axis).astype(BF16), mask)
-    if hold is not None:
-        got = after(got, hold)
-    return pick(value, bit, axis).astype(F32) + got.astype(F32)
-
-
-def scatter_high(value, r, high, axis, hold=None):
-    for mask in reversed(high):
-        shape = value.shape
-        value = value.reshape(shape[:axis] + (2, shape[axis] // 2) + shape[axis + 1 :])
-        value = halve(value, (r & mask) // mask, mask, axis, hold)
+def part(value, bit, mask, axis):
+    return pick(value, bit, axis).astype(F32), swap(pick(value, 1 - bit, axis).astype(BF16), mask)
+
+
+def high_part(value, r, mask, axis):
+    shape = value.shape
+    value = value.reshape(shape[:axis] + (2, shape[axis] // 2) + shape[axis + 1 :])
+    return part(value, (r & mask) // mask, mask, axis)
+
+
+def high_rest(kept, got, r, high, axis):
+    value = kept + got.astype(F32)
+    for mask in reversed(high[:-1]):
+        kept, got = high_part(value, r, mask, axis)
+        value = kept + got.astype(F32)
     return jnp.squeeze(value, axis)
-
-
-def scatter_rep(value, r, high, hold=None):
-    reps = value.shape[0]
-    rest = value.shape[1:]
-    value = halve(value.reshape((reps // 4, 2, 2) + rest), r & 1, 1, 2, hold)
-    value = halve(value, (r >> 1) & 1, 2, 1)
-    return scatter_high(value, r, high, 0)
 
 
 def ring_of(reps):
@@ -231,38 +221,121 @@
     )(info, w_down)
 
 
-def columns_grad_kernel(rows, mine, info_ref, ha, hb, da, db, send_g, send_u, keep_g, keep_u):
+def feed_forward_kernel(h_ref, dy_ref, gate_ref, up_ref, down_ref, hid_ref, d_gate_ref, d_up_ref):
+    h = h_ref[...]
+    gate = dot(h, gate_ref[...])
+    upper = dot(h, up_ref[...])
+    d_hidden = dot_t(dy_ref[...], down_ref[...])
+    sigma = 1.0 / (1.0 + jnp.exp(-gate))
+    swish = gate * sigma
+    hid_ref[...] = (swish * upper).astype(BF16)
+    d_up_ref[...] = (d_hidden * swish).astype(BF16)
+    d_gate_ref[...] = (d_hidden * upper * (sigma + swish * (1.0 - sigma))).astype(BF16)
+
+
+def feed_forward(h, dy, w_gu, wd):
+    tokens, width = h.shape
+    mine = wd.shape[0]
+    piece = 256
+    steps = mine // piece
+    whole = pl.BlockSpec((tokens, width), lambda j: (0, 0))
+    out = pl.BlockSpec((tokens, piece), lambda j: (0, j))
+    return pl.pallas_call(
+        feed_forward_kernel,
+        grid=(steps,),
+        in_specs=[
+            whole,
+            whole,
+            pl.BlockSpec((width, piece), lambda j: (0, j)),
+            pl.BlockSpec((width, piece), lambda j: (0, j + steps)),
+            pl.BlockSpec((piece, width), lambda j: (j, 0)),
+        ],
+        out_specs=[out] * 3,
+        out_shape=[jax.ShapeDtypeStruct((tokens, mine), BF16)] * 3,
+        compiler_params=pltpu.CompilerParams(vmem_limit_bytes=48 << 20),
+        name="feed_forward",
+    )(h, dy, w_gu, w_gu, wd)
+
+
+def inputs_grad_kernel(mine, d_gate_ref, d_up_ref, w_ref, out_ref):
+    w = w_ref[...]
+    out = dot_t(d_gate_ref[...], w[:, :mine]) + dot_t(d_up_ref[...], w[:, mine:])
+    out_ref[...] = out.astype(BF16)
+
+
+def inputs_grad_sum_kernel(
+    mine, rows, d_gate_ref, d_up_ref, w_ref, other_ref, parts_ref, low_ref, upp_ref
+):
+    w = w_ref[...]
+    out = dot_t(d_gate_ref[...], w[:, :mine]) + dot_t(d_up_ref[...], w[:, mine:])
+    out = out + other_ref[...].astype(F32)
+    parts_ref[...] = out[: 3 * rows]
+    low_ref[...] = out[3 * rows : 3 * rows + rows // 2].astype(BF16)
+    upp_ref[...] = out[3 * rows + rows // 2 :].astype(BF16)
+
+
+def inputs_grad(d_gate, d_up, w_gu, other=None):
+    tokens, mine = d_gate.shape
+    width = w_gu.shape[0]
+    piece = min(512, width)
+    rows = tokens // 4
+    lhs = pl.BlockSpec((tokens, mine), lambda j: (0, 0))
+    in_specs = [lhs, lhs, pl.BlockSpec((piece, 2 * mine), lambda j: (j, 0))]
+    out = pl.BlockSpec((tokens, piece), lambda j: (0, j))
+    params = pltpu.CompilerParams(vmem_limit_bytes=48 << 20)
+    if other is None:
+        return pl.pallas_call(
+            functools.partial(inputs_grad_kernel, mine),
+            grid=(width // piece,),
+            in_specs=in_specs,
+            out_specs=out,
+            out_shape=jax.ShapeDtypeStruct((tokens, width), BF16),
+            compiler_params=params,
+            name="inputs_grad",
+        )(d_gate, d_up, w_gu)
+    half = pl.BlockSpec((rows // 2, piece), lambda j: (0, j))
+    return pl.pallas_call(
+        functools.partial(inputs_grad_sum_kernel, mine, rows),
+        grid=(width // piece,),
+        in_specs=in_specs + [out],
+        out_specs=[pl.BlockSpec((3 * rows, piece), lambda j: (0, j)), half, half],
+        out_shape=[jax.ShapeDtypeStruct((3 * rows, width), F32)]
+        + [jax.ShapeDtypeStruct((rows // 2, width), BF16)] * 2,
+        compiler_params=params,
+        name="inputs_grad_sum",
+    )(d_gate, d_up, w_gu, other)
+
+
+def columns_grad_kernel(
+    rows, info_ref, ha, hb, ga, gb, ua, ub, send_g, send_u, keep_g, keep_u
+):
     odd = (info_ref[1] & 1) == 1
-    grad = t_dot(ha[...], da[...]) + t_dot(hb[...], db[...])
-    count, width = grad.shape
-    grad = grad.reshape(count // (2 * rows), 2, rows, width)
-    low, upp = grad[:, 0], grad[:, 1]
-    send = jnp.where(odd, low, upp).astype(BF16).reshape(count // 2, width)
-    keep = jnp.where(odd, upp, low).reshape(count // 2, width)
-    send_g[...] = send[:, :mine]
-    send_u[...] = send[:, mine:]
-    keep_g[...] = keep[:, :mine]
-    keep_u[...] = keep[:, mine:]
-
-
-def columns_grad(info, ha, hb, da, db, rows):
+    for da, db, send, keep in ((ga, gb, send_g, keep_g), (ua, ub, send_u, keep_u)):
+        grad = t_dot(ha[...], da[...]) + t_dot(hb[...], db[...])
+        count, width = grad.shape
+        grad = grad.reshape(count // (2 * rows), 2, rows, width)
+        low, upp = grad[:, 0], grad[:, 1]
+        send[...] = jnp.where(odd, low, upp).astype(BF16).reshape(count // 2, width)
+        keep[...] = jnp.where(odd, upp, low).reshape(count // 2, width)
+
+
+def columns_grad(info, ha, hb, ga, gb, ua, ub, rows):
     tokens, width = ha.shape
-    mine = da.shape[1] // 2
+    mine = ga.shape[1]
     part = min(512, width)
     half = pl.BlockSpec((part // 2, mine), lambda i: (i, 0))
     lhs = pl.BlockSpec((tokens, part), lambda i: (0, i))
-    rhs = pl.BlockSpec(da.shape, lambda i: (0, 0))
+    rhs = pl.BlockSpec(ga.shape, lambda i: (0, 0))
     return pl.pallas_call(
-        functools.partial(columns_grad_kernel, rows, mine),
+        functools.partial(columns_grad_kernel, rows),
         grid=(width // part,),
-        in_specs=[pl.BlockSpec(memory_space=pltpu.SMEM), lhs, lhs, rhs, rhs],
+        in_specs=[pl.BlockSpec(memory_space=pltpu.SMEM), lhs, lhs, rhs, rhs, rhs, rhs],
         out_specs=[half] * 4,
         out_shape=[jax.ShapeDtypeStruct((width // 2, mine), BF16)] * 2
         + [jax.ShapeDtypeStruct((width // 2, mine), F32)] * 2,
         compiler_params=pltpu.CompilerParams(vmem_limit_bytes=56 << 20),
-        cost_estimate=BRIEF,
         name="columns_grad",
-    )(info, ha, hb, da, db)
+    )(info, ha, hb, ga, gb, ua, ub)
 
 
 def rows_grad_kernel(info_ref, ha, hb, da, db, send_ref, keep_ref):
@@ -425,7 +498,8 @@
     lse_ref,
     kv_ref,
     dq_ref,
-    dkv_ref,
+    keep_ref,
+    send_ref,
     sums,
 ):
     j = pl.program_id(0)
@@ -469,13 +543,16 @@
 
     @pl.when(j == 3)
     def _():
-        dkv_ref[...] = sums[...].astype(BF16)
+        for slot in range(reps // 2):
+            keep_ref[slot] = sums[2 * slot].astype(BF16)
+            send_ref[slot] = sums[2 * slot + 1].astype(BF16)
 
 
 def attend_back(info, slots, starts, query, d_out, out, lse, kv):
     reps = kv.shape[0]
     rows = pl.BlockSpec((1, HD, 4 * HD), lambda j: (j, 0, 0))
     whole = pl.BlockSpec(kv.shape, lambda j: (0, 0, 0, 0))
+    half = pl.BlockSpec((reps // 2,) + kv.shape[1:], lambda j: (0, 0, 0, 0))
     return pl.pallas_call(
         functools.partial(attend_back_kernel, reps),
         grid=(4,),
@@ -489,11 +566,9 @@
             pl.BlockSpec((1, 4 * HD, 1), lambda j: (j, 0, 0)),
             whole,
         ],
-        out_specs=[rows, whole],
-        out_shape=[
-            jax.ShapeDtypeStruct((4, HD, 4 * HD), BF16),
-            jax.ShapeDtypeStruct(kv.shape, BF16),
-        ],
+        out_specs=[rows, half, half],
+        out_shape=[jax.ShapeDtypeStruct((4, HD, 4 * HD), BF16)]
+        + [jax.ShapeDtypeStruct((reps // 2,) + kv.shape[1:], BF16)] * 2,
         scratch_shapes=[pltpu.VMEM(kv.shape, F32)],
         compiler_params=pltpu.CompilerParams(vmem_limit_bytes=60 << 20),
         cost_estimate=BRIEF,
@@ -541,14 +616,15 @@
         )
         for j in range(4)
     ]
-    kv_own = jnp.stack(exchange_four(kv_parts, core, yy))
+    kv_y = swap(jnp.stack([kv_parts[2], kv_parts[3]]), yy)
+    kv_own = jnp.stack([kv_parts[0], swap(kv_parts[1], core), kv_y[0], swap(kv_y[1], core)])
 
     x_full = tokens.astype(F32)
     inv_one = lax.rsqrt(jnp.mean(x_full * x_full, axis=1, keepdims=True) + EPSILON)
     normed_one = x_full * inv_one
     h_one = (normed_one * gain_attn).astype(BF16)
 
-    h_y = swap(h_one, yy)
+    h_y = swap(after(h_one, kv_y), yy)
     wq_half = share // 2
     wq_y = jnp.stack(
         [
@@ -556,26 +632,30 @@
             for j in (2, 3)
         ]
     )
-    stay, to_core, to_y, relay = pack(info, w_gate, w_up, outer, chunk, wide)
     wd = pack_down(info, w_down, outer, chunk, wide)
-    dy_y = cotangent
     if reps == 8:
         pairs = ring_of(reps)
+        one = lax.ppermute(kv_own, BOTH, pairs)
+        zero_x = swap(kv_own, xx)
         wq_y = swap(after(wq_y, kv_own), yy)
-        one = lax.ppermute(kv_own, BOTH, pairs)
-        one, h_y = together(one, h_y)
+        one, h_y, wd, zero_x = together(one, h_y, wd, zero_x)
+        stay, to_core, to_y, relay = pack(after(info, one), w_gate, w_up, outer, chunk, wide)
         two = lax.ppermute(one, BOTH, pairs)
-        two, wq_y, stay, wd = together(two, wq_y, stay, wd)
+        one_x = swap(one, xx)
+        two, wq_y, stay, one_x = together(two, wq_y, stay, one_x)
+        three = lax.ppermute(two, BOTH, pairs)
         wq_x = swap(wq_y, xx)
-        dy_y = swap(after(dy_y, two), yy)
-        three = lax.ppermute(two, BOTH, pairs)
-        three, wq_x, dy_y = together(three, wq_x, dy_y)
-        relay = swap(after(relay, two), yy)
-        kv = jnp.stack([part for v in (kv_own, one, two, three) for part in (v, swap(v, xx))])
+        two_x = swap(two, xx)
+        dy_y = swap(after(cotangent, two), yy)
+        three, two_x = together(three, two_x)
+        three_x = swap(three, xx)
+        three_x, wq_x, dy_y = together(three_x, wq_x, dy_y)
+        kv = jnp.stack([kv_own, zero_x, one, one_x, two, two_x, three, three_x])
         slots = ring_slots(r, reps)
-        kv, relay = together(kv, relay)
+        relay = swap(after(relay, wq_y), yy)
     else:
-        wq_y, dy_y, relay = swap(wq_y, yy), swap(dy_y, yy), swap(relay, yy)
+        stay, to_core, to_y, relay = pack(info, w_gate, w_up, outer, chunk, wide)
+        wq_y, dy_y, relay = swap(wq_y, yy), swap(cotangent, yy), swap(relay, yy)
         wq_x = swap(wq_y, xx)
         kv = lax.all_gather(kv_own, "rep", axis=0, tiled=False)
         slots = jnp.arange(reps, dtype=jnp.int32)
@@ -595,26 +675,26 @@
     wq_cols = jnp.concatenate(absolute(wq_parts, g), axis=0)
     query = dot(h_group, wq_cols).astype(BF16).reshape(4, rows, share)
 
+    dy_near = jnp.stack([cotangent, dy_y])
+    dy_far = swap(dy_near, zz)
+    attn, lse = attend(info, slots, starts, query, kv)
+    attn, lse, relay = together(attn, lse, relay)
     from_y = swap(after(to_y, relay), yy)
     relay_x = swap(relay, xx)
-    attn, lse = attend(info, slots, starts, query, kv)
-    attn, lse, from_y = together(attn, lse, from_y)
     attn_rows = attn.reshape(4 * rows, share)
     branch = scatter_four_core(dot(attn_rows, w_out).reshape(4, rows, width), core)
     from_branch = swap(branch[1].astype(BF16), yy)
-    from_branch, relay_x = together(from_branch, relay_x)
-    from_y_x = swap(from_y, xx)
-    dy_near = jnp.stack([cotangent, dy_y])
-    dy_far = swap(after(dy_near, attn), zz)
+    from_branch, from_y = together(from_branch, from_y)
     resid = x_full + branch[0] + from_branch.astype(F32)
     inv_two = lax.rsqrt(jnp.mean(resid * resid, axis=1, keepdims=True) + EPSILON)
     normed_two = resid * inv_two
     h_two = (normed_two * gain_ffn).astype(BF16)
 
     h_y, h_z = swap(h_two, yy), swap(h_two, zz)
-    h_y, h_z, dy_far = together(h_y, h_z, dy_far)
+    from_y_x = swap(from_y, xx)
+    h_y, h_z, relay_x = together(h_y, h_z, relay_x)
     low, upp = swap(h_y[: rows // 2], zz), swap(h_z[rows // 2 :], yy)
-    low, upp, from_y_x = together(low, upp, from_y_x)
+    low, upp, from_y_x, dy_far = together(low, upp, from_y_x, dy_far)
     h_a = jnp.concatenate([h_two, h_y, h_z, low, upp])
     h_b = swap(h_a, core)
     dy_a = jnp.stack([dy_near, dy_far]).reshape(4 * rows, width)
@@ -643,59 +723,65 @@
         axis=0,
     )
 
-    def feed_forward(h, dy):
-        both = dot(h, w_gu)
-        gate, upper = both[:, :mine], both[:, mine:]
-        d_hidden = dot_t(dy, wd)
-        sigma = jax.nn.sigmoid(gate)
-        swish = gate * sigma
-        hidden = (swish * upper).astype(BF16)
-        d_gate = (d_hidden * upper * sigma * (1.0 + gate * (1.0 - sigma))).astype(BF16)
-        d_upper = (d_hidden * swish).astype(BF16)
-        return hidden, jnp.concatenate([d_gate, d_upper], axis=1)
-
-    hidden_a, d_both_a = feed_forward(h_a, dy_a)
-    hidden_b, d_both_b = feed_forward(h_b, dy_b)
-    from_core = swap(dot_t(d_both_b, w_gu).astype(BF16), core)
-    d_h_parts = dot_t(d_both_a, w_gu) + from_core.astype(F32)
-    d_h_parts = d_h_parts.reshape(4, rows, width)
-
-    send_d, keep_d = rows_grad(info, hidden_a, hidden_b, dy_a, dy_b)
-    send_g, send_u, keep_g, keep_u = columns_grad(info, h_a, h_b, d_both_a, d_both_b, out_rows)
-    got_d = swap(send_d, xx)
-    to_z, to_y = corner_step(d_h_parts, yy, zz)
-    to_z, to_y, send_d, keep_d = together(to_z, to_y, send_d, keep_d)
-    from_z, from_y = side_step(d_h_parts, to_z, to_y, yy, zz)
-    from_z, from_y, send_g, send_u, got_d = together(from_z, from_y, send_g, send_u, got_d)
+    hidden_b, d_gate_b, d_up_b = feed_forward(h_b, dy_b, w_gu, wd)
+    from_core = swap(inputs_grad(d_gate_b, d_up_b, w_gu), core)
+    hidden_a, d_gate_a, d_up_a = feed_forward(h_a, after(dy_a, d_up_b), w_gu, wd)
+    d_h_parts, corner_low, corner_upp = inputs_grad(d_gate_a, d_up_a, w_gu, from_core)
+
+    to_z, to_y = swap(corner_low, yy), swap(corner_upp, zz)
+    send_g, send_u, keep_g, keep_u = columns_grad(
+        after(info, d_h_parts), h_a, h_b, d_gate_a, d_gate_b, d_up_a, d_up_b, out_rows
+    )
+    to_z, to_y, send_g = together(to_z, to_y, send_g)
     got_g = swap(send_g, xx)
-    d_h_two = d_h_parts[0] + from_z.astype(F32) + from_y.astype(F32)
+    from_z, from_y = side_step(d_h_parts, to_z, to_y, rows, yy, zz)
+    out_core = swap(dot(after(hidden_b, to_z), wd).astype(BF16), core)
+    send_d, keep_d = rows_grad(after(info, to_z), hidden_a, hidden_b, dy_a, dy_b)
+    out_parts = dot(after(hidden_a, to_z), wd)
+    from_z, from_y, out_core, send_d, out_parts = together(
+        from_z, from_y, out_core, send_d, out_parts
+    )
+    d_h_two = d_h_parts[:rows] + from_z.astype(F32) + from_y.astype(F32)
     scaled_two = d_h_two * gain_ffn
     d_resid = cotangent.astype(F32) + inv_two * (
         scaled_two - normed_two * jnp.mean(scaled_two * normed_two, axis=1, keepdims=True)
     )
     da_own = d_resid.astype(BF16)
     da_y, da_c = swap(da_own, yy), swap(da_own, core)
-    out_core = swap(dot(hidden_b, wd).astype(BF16), core)
-    da_y, da_c, out_core = together(da_y, da_c, out_core)
+    out_parts = (out_parts + out_core.astype(F32)).reshape(4, rows, width)
+    out_z = swap(out_parts[2:].astype(BF16), zz)
+    da_y, da_c = together(da_y, da_c)
     d_group = jnp.stack([da_own, da_c, da_y, swap(da_y, core)]).reshape(4 * rows, width)
-    d_group, got_g = together(d_group, got_g)
-    got_u = swap(send_u, xx)
-    out_parts = (dot(hidden_a, wd) + out_core.astype(F32)).reshape(4, rows, width)
-    out_z, out_y = corner_step(after(out_parts, d_group), yy, zz)
-
+    d_group, got_g, out_z = together(d_group, got_g, out_z)
+
+    got_u = swap(after(send_u, got_g), xx)
+    grad_g = (keep_g + got_g.astype(F32)).reshape(4, outer, 2, out_rows, mine)
+    keep_g, got_g = high_part(grad_g, r, high[-1], 1)
     d_attn = dot_t(d_group, w_out).astype(BF16).reshape(4, rows, share)
+    grad_o = t_dot(attn_rows, d_group).reshape(outer, 2, 2, out_rows, width)
+    keep_o, got_o = part(grad_o, z_bit, zz, 1)
+    d_query, keep_kv, send_kv = attend_back(info, slots, starts, query, d_attn, attn, lse, kv)
+    d_query, send_kv, got_u, out_z = together(d_query, send_kv, got_u, out_z)
+    out_parts = out_parts[:2] + out_z.astype(F32)
+
+    got_d = swap(after(send_d, got_u), xx)
+    grad_u = (keep_u + got_u.astype(F32)).reshape(4, outer, 2, out_rows, mine)
+    keep_u, got_u = high_part(grad_u, r, high[-1], 1)
+    d_query = d_query.reshape(4 * rows, share)
+    d_h_one = dot_t(d_query, wq_cols).reshape(2, 2, rows, width)
+    got_h = swap(d_h_one[:, 1].astype(BF16), core)
+    d_wq = t_dot(h_group, d_query).reshape(4, outer, 2, 2, out_rows, share)
+    got_h, got_g, got_o, d_wq = together(got_h, got_g, got_o, d_wq)
+
+    d_h_one = d_h_one[:, 0] + got_h.astype(F32)
+    from_h = swap(d_h_one[1].astype(BF16), yy)
+    grad_g = high_rest(keep_g, got_g, r, high, 1).astype(BF16)
+    near_g, far_g = pick(grad_g, z_bit, 1), swap(pick(grad_g, 1 - z_bit, 1), zz)
+    from_h, far_g, got_d, send_kv, d_wq = together(from_h, far_g, got_d, send_kv, d_wq)
+
+    got_kv = swap(send_kv, xx)
     grad_d = (keep_d + got_d.astype(F32)).reshape(outer, wide, width)
-    d_query, d_kv = attend_back(info, slots, starts, query, d_attn, attn, lse, kv)
-    d_query, d_kv, got_u, out_z, out_y = together(d_query, d_kv, got_u, out_z, out_y)
-    d_query = d_query.reshape(4 * rows, share)
-    out_z, out_y = side_step(out_parts, out_z, out_y, yy, zz)
-    grad_d = scatter_high(grad_d, r, high, 0)
-
-    d_h_one = scatter_four_core(dot_t(d_query, wq_cols).reshape(4, rows, width), core)
-    from_h = swap(d_h_one[1].astype(BF16), yy)
-    from_h, out_z, out_y, grad_d = together(from_h, out_z, out_y, grad_d)
-    d_wdown = grad_d[:chunk]
-    output = (resid + out_parts[0] + out_z.astype(F32) + out_y.astype(F32)).astype(BF16)
+    keep_d, got_d = high_part(grad_d, r, high[-1], 0)
     d_h_one = d_h_one[0] + from_h.astype(F32)
     scaled_one = d_h_one * gain_attn
     d_tokens = (
@@ -703,43 +789,63 @@
         + inv_one
         * (scaled_one - normed_one * jnp.mean(scaled_one * normed_one, axis=1, keepdims=True))
     ).astype(BF16)
-
-    def on(got, keep):
-        grad = (keep + got.astype(F32)).reshape(4, outer, 2, out_rows, mine)
-        grad = scatter_high(grad, r, high, 1).astype(BF16)
-        other = swap(pick(grad, 1 - z_bit, 1), zz)
-        grad = jnp.stack([pick(grad, z_bit, 1), other])
-        return jnp.stack(exchange_four([pick(grad, g ^ j, 1) for j in range(4)], core, yy))
-
-    grad_g = on(got_g, keep_g)
-    grad_u = on(got_u, keep_u)
-    gate_rows = lax.dynamic_slice_in_dim(w_gate, r * out_rows, out_rows, 0)
-    up_rows = lax.dynamic_slice_in_dim(w_up, r * out_rows, out_rows, 0)
-    gain_at = (g * reps + r) * out_rows
-    gain_rows = lax.dynamic_slice_in_dim(gain_ffn, gain_at, out_rows, 0)
-    d_wgate, d_wup, d_gain_two = unpack(
-        info, grad_g, grad_u, gate_rows, up_rows, gain_rows[:, None], outer, chunk, wide
-    )
-
-    d_wout = t_dot(attn_rows, d_group).reshape(reps, out_rows, width)
-    d_wout = scatter_rep(d_wout, r, high)
-    d_kv = d_kv.reshape((outer, 2, 2) + d_kv.shape[1:])
-    d_kv = d_kv[:, 0].astype(F32) + swap(d_kv[:, 1], zz).astype(F32)
-    d_kv = d_kv[:, 0] + swap(d_kv[:, 1].astype(BF16), xx).astype(F32)
+    grad_g = jnp.stack([near_g, far_g])
+    grad_g = [pick(grad_g, g ^ j, 1) for j in range(4)]
+    y_g = swap(jnp.stack([grad_g[2], grad_g[3]]), yy)
+    got_u, y_g, got_o = together(got_u, y_g, got_o)
+
+    grad_u = high_rest(keep_u, got_u, r, high, 1).astype(BF16)
+    near_u, far_u = pick(grad_u, z_bit, 1), swap(pick(grad_u, 1 - z_bit, 1), zz)
+    grad_g = jnp.stack(
+        [grad_g[0], swap(after(grad_g[1], y_g), core), y_g[0], swap(y_g[1], core)]
+    )
+    far_u, grad_g, got_kv, got_o, d_wq = together(far_u, grad_g, got_kv, got_o, d_wq)
+
+    keep_q, got_q = part(d_wq, x_bit, xx, 3)
+    grad_kv = keep_kv.astype(F32) + got_kv.astype(F32)
+    grad_kv = grad_kv.reshape((outer, 2) + grad_kv.shape[1:])
+    keep_kv, got_kv = grad_kv[:, 0], swap(grad_kv[:, 1].astype(BF16), zz)
+    grad_u = jnp.stack([near_u, far_u])
+    grad_u = [pick(grad_u, g ^ j, 1) for j in range(4)]
+    y_u = swap(jnp.stack([grad_u[2], grad_u[3]]), yy)
+    got_kv, y_u, got_d = together(got_kv, y_u, got_d)
+
+    d_wdown = high_rest(keep_d, got_d, r, high, 0)[:chunk]
+    grad_kv = keep_kv + got_kv.astype(F32)
     for mask in reversed(high):
-        d_kv = d_kv.reshape((2, d_kv.shape[0] // 2) + d_kv.shape[1:])
-        d_kv = d_kv[0] + swap(d_kv[1].astype(BF16), mask).astype(F32)
-    d_kv = d_kv[0].astype(BF16)
-    d_kv = absolute(exchange_four([d_kv[j] for j in range(4)], core, yy), g)
-    d_keys = jnp.concatenate([piece[:, :HD] for piece in d_kv], axis=1)
-    d_values = jnp.concatenate([piece[:, HD:] for piece in d_kv], axis=1)
-    d_wq = t_dot(h_group, d_query).reshape(4, reps, out_rows, share)
-    d_wq = scatter_rep(jnp.swapaxes(d_wq, 0, 1), r, high).astype(BF16)
+        grad_kv = grad_kv.reshape((2, grad_kv.shape[0] // 2) + grad_kv.shape[1:])
+        grad_kv = grad_kv[0] + swap(grad_kv[1].astype(BF16), mask).astype(F32)
+    grad_u = jnp.stack(
+        [grad_u[0], swap(after(grad_u[1], y_u), core), y_u[0], swap(y_u[1], core)]
+    )
+    out_y = swap(after(out_parts[1], y_u).astype(BF16), yy)
+    got_q, grad_u, keep_o = together(got_q, grad_u, keep_o)
+    keep_q, got_q = part(keep_q + got_q.astype(F32), z_bit, zz, 2)
+    keep_o, got_o = part(keep_o + got_o.astype(F32), x_bit, xx, 1)
+    got_q, got_o, out_y, grad_kv = together(got_q, got_o, out_y, grad_kv)
+
+    output = (resid + out_parts[0] + out_y.astype(F32)).astype(BF16)
+    keep_q, got_q = high_part(keep_q + got_q.astype(F32), r, high[-1], 1)
+    keep_o, got_o = high_part(keep_o + got_o.astype(F32), r, high[-1], 0)
+    grad_kv = grad_kv[0].astype(BF16)
+    grad_kv = absolute(exchange_four([grad_kv[j] for j in range(4)], core, yy), g)
+    d_keys = jnp.concatenate([piece[:, :HD] for piece in grad_kv], axis=1)
+    d_values = jnp.concatenate([piece[:, HD:] for piece in grad_kv], axis=1)
+    d_wq = high_rest(keep_q, got_q, r, high, 1).astype(BF16)
     d_wq = absolute(exchange_four([pick(d_wq, g ^ j, 0) for j in range(4)], core, yy), g)
     d_wquery = jnp.concatenate(d_wq, axis=1).astype(F32)
-    query_rows = lax.dynamic_slice_in_dim(w_query, r * out_rows, out_rows, 0)
+    d_wout = high_rest(keep_o, got_o, r, high, 0)
+
+    def own_rows(value):
+        return lax.dynamic_slice_in_dim(value, r * out_rows, out_rows, 0)
+
+    gain_at = (g * reps + r) * out_rows
+    gain_rows = lax.dynamic_slice_in_dim(gain_ffn, gain_at, out_rows, 0)[:, None]
+    d_wgate, d_wup, d_gain_two = unpack(
+        info, grad_g, grad_u, own_rows(w_gate), own_rows(w_up), gain_rows, outer, chunk, wide
+    )
     gain_rows = lax.dynamic_slice_in_dim(gain_attn, gain_at, out_rows, 0)
-    d_gain_one = jnp.sum(d_wquery * query_rows.astype(F32), axis=1) / gain_rows
+    d_gain_one = jnp.sum(d_wquery * own_rows(w_query).astype(F32), axis=1) / gain_rows
     return (
         output,
         d_tokens,

time: 496 us -> 440 us (0.89)
  waiting for transfers between devices: 216 us -> 180 us
  matrix products: 45 us -> 13.4 us
  Pallas kernels: 54.8 us -> 84.9 us
  starting transfers between devices: 68.9 us -> 57.6 us
  other arithmetic: 57.3 us -> 50.9 us
    ppermute x75 -> x73, waiting for transfers between devices: 213 us -> 176 us  [swap(): return lax.ppermute(value, BOTH, [(i, i ^ mask) for i in range(count)])]
    pallas_call x1 -> x5, Pallas kernels: 11.3 us -> 43.3 us  [the longest x2 17.3 us: feed_forward(): pl.pallas_call(feed_forward_kernel, grid=(steps,), in_specs=[whole, whole...]
    dot_general x6 -> x2, matrix products: 23.2 us -> 3.45 us  [dot_t(): lax.dot_general(a, b, (((1,), (1,)), ((), ())), preferred_element_type=F32)]
    dot_general x6 -> x4, matrix products: 19.3 us -> 7.44 us  [dot(): return jnp.dot(a, b, preferred_element_type=F32)]
    ppermute x75 -> x73, starting transfers between devices: 61.4 us -> 51.5 us  [swap(): return lax.ppermute(value, BOTH, [(i, i ^ mask) for i in range(count)])]
    add x8 -> x12, other arithmetic: 4.85 us -> 11.7 us  [the longest x1 2.18 us: on_device(): out_parts = (out_parts + out_core.astype(F32)).reshape(4, rows, width)]
    unnamed x176 -> x155, local copies, waits for them, and re-layouts: 21.3 us -> 22.1 us
  transfers between devices with their start and end apart: 78 -> 76, of which waited for: 31 -> 35; matrix products, arithmetic and copies ran while one was open for 24% -> 18% of each run, Pallas kernels for 11% -> 14%
where the time goes in v3:
time: 440 us; the launch traced here: 434 us
  waiting for transfers between devices  180 us (41%)
  Pallas kernels  84.9 us (19%)
  starting transfers between devices  57.6 us (13%)
  other arithmetic  50.9 us (12%)
  local copies, waits for them, and re-layouts  44.1 us (10%)
  matrix products  13.4 us (3%)
    ppermute x73, waiting for transfers between devices, swap(): return lax.ppermute(value, BOTH, [(i, i ^ mask) for i in range(count)])  176 us
    ppermute x73, starting transfers between devices, swap(): return lax.ppermute(value, BOTH, [(i, i ^ mask) for i in range(count)])  51.5 us
    unnamed x155, local copies, waits for them, and re-layouts  22.1 us
    pallas_call x2, Pallas kernels, feed_forward(): pl.pallas_call(feed_forward_kernel, grid=(steps,), in_specs=[whole, whole...  17.3 us
    pallas_call x1, Pallas kernels, attend_back(): pl.pallas_call(functools.partial(attend_back_kernel, reps), grid=(4,), in...  16.2 us
    pallas_call x1, Pallas kernels, columns_grad(): pl.pallas_call(functools.partial(columns_grad_kernel, rows), grid=(width...  11.4 us
    pallas_call x1, Pallas kernels, attend(): pl.pallas_call(functools.partial(attend_kernel, reps), grid=(4,), in_spec...  10 us
  transfers between devices with their start and end apart: 76, of which 35 were waited for; matrix products, arithmetic and copies ran while one was open for 18% of the time, Pallas kernels for 14%

profile of v3, /device:TPU:0, one launch (start us, length us, event | category | flops | bytes accessed | tf_op | source)
XLA Modules:
  0.0 433.9 jit_solution(3206264094253444642)
XLA Ops:
  45.7 4.0 collective-permute-done.11
  56.0 13.2 %collective-permute-done.13 = bf16[4,128,256]{2,1,0:T(8,128)(2,1)S(1)} collective-permute-done((bf16[4,128,256]{2,1,0:T(8,128)(2,1)S(1)}, bf16[4,128,256]{2,1,0:T(8,128)(2,1)S(1)}, u32[]{:S(2)}, u32[]{:S(2)}) %collective-permute-start.13) | collective-permute-done | bytes 262176 | tf_op jit(solution)/shard_map/ppermute | solution.py:21
  74.9 10.0 %attend.1 = (bf16[4,128,512]{2,1,0:T(8,128)(2,1)S(1)}, f32[4,512,1]{2,1,0:T(8,128)S(1)}) custom-call(s32[2]{0:T(128)S(1)} %pad_add_fusion.info_ref, s32[8]{0:T(128)S(1)} %and_add_fusion.slots_ref, s32[8]{0:T(128)S(1)} %copy-done.26, bf16[4,128,512]{2,1,0:T(8,128)(2,1)S(1)} %bitcast.293, bf16[8,4,128,256]{3,2,1,0:T(8,128)(2,1)S(1)} %bitcast_dynamic-update-slice_fusion.kv_ref), custom_call_target="tpu_custom_call" | custom-call | flops 1 | bytes 1 | tf_op jit(solution)/shard_map/attend/pallas_call | solution.py:466
  91.5 15.4 %collective-permute-done.21 = bf16[256,1536]{1,0:T(8,128)(2,1)S(1)} collective-permute-done((bf16[256,1536]{1,0:T(8,128)(2,1)S(1)}, bf16[256,1536]{1,0:T(8,128)(2,1)S(1)}, u32[]{:S(2)}, u32[]{:S(2)}) %collective-permute-start.21) | collective-permute-done | bytes 786464 | tf_op jit(solution)/shard_map/ppermute | solution.py:21
  106.9 10.8 %collective-permute-done.20 = bf16[128,2048]{1,0:T(8,128)(2,1)S(1)} collective-permute-done((bf16[128,2048]{1,0:T(8,128)(2,1)S(1)}, bf16[128,2048]{1,0:T(8,128)(2,1)S(1)}, u32[]{:S(2)}, u32[]{:S(2)}) %collective-permute-start.20) | collective-permute-done | bytes 524320 | tf_op jit(solution)/shard_map/ppermute | solution.py:21
  118.9 12.9 %collective-permute-done.22 = bf16[128,2048]{1,0:T(8,128)(2,1)S(1)} collective-permute-done((bf16[128,2048]{1,0:T(8,128)(2,1)S(1)}, bf16[128,2048]{1,0:T(8,128)(2,1)S(1)}, u32[]{:S(2)}, u32[]{:S(2)}) %collective-permute-start.22) | collective-permute-done | bytes 524320 | tf_op jit(solution)/shard_map/ppermute | solution.py:21
  134.2 4.7 %collective-permute-done.25 = bf16[64,2048]{1,0:T(8,128)(2,1)S(1)} collective-permute-done((bf16[64,2048]{1,0:T(8,128)(2,1)S(1)}, bf16[64,2048]{1,0:T(8,128)(2,1)S(1)}, u32[]{:S(2)}, u32[]{:S(2)}) %collective-permute-start.25) | collective-permute-done | bytes 262176 | tf_op jit(solution)/shard_map/ppermute | solution.py:21
  148.6 8.6 %feed_forward.2 = (bf16[512,768]{1,0:T(8,128)(2,1)S(1)}, bf16[512,768]{1,0:T(8,128)(2,1)S(1)}, bf16[512,768]{1,0:T(8,128)(2,1)S(1)}) custom-call(bf16[512,2048]{1,0:T(8,128)(2,1)S(1)} %collective-permute-done.29.h_ref.hb, bf16[512,2048]{1,0:T(8,128)(2,1)} %copy-done.40, bf16[2048,1536]{1,0:T(8,128)(2,1)} %pad_maximum_fusion.gate_ref.up_ref.w_ref, ...), custom_call_target="tpu_custom_call" | custom-call | tf_op jit(solution)/shard_map/feed_forward/pallas_call | solution.py:243
  157.3 6.6 %inputs_grad.1 = bf16[512,2048]{1,0:T(8,128)(2,1)S(1)} custom-call(bf16[512,768]{1,0:T(8,128)(2,1)S(1)} %get-tuple-element.163.d_gate_ref.gb, bf16[512,768]{1,0:T(8,128)(2,1)S(1)} %get-tuple-element.159.d_up_ref.ub, bf16[2048,1536]{1,0:T(8,128)(2,1)} %pad_maximum_fusion.gate_ref.up_ref.w_ref), custom_call_target="tpu_custom_call" | custom-call | tf_op jit(solution)/shard_map/inputs_grad/pallas_call | solution.py:287
  164.1 8.6 %feed_forward.3 = (bf16[512,768]{1,0:T(8,128)(2,1)S(1)}, bf16[512,768]{1,0:T(8,128)(2,1)S(1)}, bf16[512,768]{1,0:T(8,128)(2,1)S(1)}) custom-call(bf16[512,2048]{1,0:T(8,128)(2,1)S(1)} %constant_dynamic-update-slice_fusion.h_ref.ha, bf16[512,2048]{1,0:T(8,128)(2,1)} %bitcast.289, bf16[2048,1536]{1,0:T(8,128)(2,1)} %pad_maximum_fusion.gate_ref.up_ref.w_ref, ...), custom_call_target="tpu_custom_call" | custom-call | tf_op jit(solution)/shard_map/feed_forward/pallas_call | solution.py:243
  172.8 8.1 %inputs_grad_sum.1 = (f32[384,2048]{1,0:T(8,128)}, bf16[64,2048]{1,0:T(8,128)(2,1)}, bf16[64,2048]{1,0:T(8,128)(2,1)}) custom-call(bf16[512,768]{1,0:T(8,128)(2,1)S(1)} %get-tuple-element.161.d_gate_ref.ga, bf16[512,768]{1,0:T(8,128)(2,1)S(1)} %get-tuple-element.162.d_up_ref.ua, bf16[2048,1536]{1,0:T(8,128)(2,1)} %pad_maximum_fusion.gate_ref.up_ref.w_ref, ...), custom_call_target="tpu_custom_call" | custom-call | tf_op jit(solution)/shard_map/inputs_grad_sum/pallas_call | solution.py:297
  183.8 11.4 %columns_grad.1 = (bf16[1024,768]{1,0:T(8,128)(2,1)}, bf16[1024,768]{1,0:T(8,128)(2,1)}, f32[1024,768]{1,0:T(8,128)}, f32[1024,768]{1,0:T(8,128)}) custom-call(s32[2]{0:T(128)} %copy-done.22, bf16[512,2048]{1,0:T(8,128)(2,1)} %copy-done.6, bf16[512,2048]{1,0:T(8,128)(2,1)} %copy-done.8, bf16[512,768]{1,0:T(8,128)(2,1)} %copy-done.15, ...), custom_call_target="tpu_custom_call" | custom-call | tf_op jit(solution)/shard_map/columns_grad/pallas_call | solution.py:329
  204.4 6.8 %rows_grad.1 = (bf16[384,2048]{1,0:T(8,128)(2,1)S(1)}, f32[384,2048]{1,0:T(8,128)}) custom-call(s32[2]{0:T(128)S(1)} %copy-done.23, bf16[512,768]{1,0:T(8,128)(2,1)S(1)} %copy-done.21, bf16[512,768]{1,0:T(8,128)(2,1)S(1)} %get-tuple-element.172.hb, bf16[512,2048]{1,0:T(8,128)(2,1)S(1)} %bitcast.290, bf16[512,2048]{1,0:T(8,128)(2,1)} %copy-done.40), custom_call_target="tpu_custom_call" | custom-call | flops 1 | bytes 1 | tf_op jit(solution)/shard_map/rows_grad/pallas_call | solution.py:357
  225.4 7.7 %collective-permute-done.40 = bf16[128,2048]{1,0:T(8,128)(2,1)} collective-permute-done((bf16[128,2048]{1,0:T(8,128)(2,1)S(1)}, bf16[128,2048]{1,0:T(8,128)(2,1)}, u32[]{:S(2)}, u32[]{:S(2)}) %collective-permute-start.40) | collective-permute-done | bytes 524320 | tf_op jit(solution)/shard_map/ppermute | solution.py:21
  243.2 6.6 %collective-permute-done.44 = bf16[2,128,2048]{2,1,0:T(8,128)(2,1)} collective-permute-done((bf16[2,128,2048]{2,1,0:T(8,128)(2,1)}, bf16[2,128,2048]{2,1,0:T(8,128)(2,1)}, u32[]{:S(2)}, u32[]{:S(2)}) %collective-permute-start.44) | collective-permute-done | bytes 1048608 | tf_op jit(solution)/shard_map/ppermute | solution.py:21
  262.2 16.2 %attend_back.1 = (bf16[4,128,512]{2,1,0:T(8,128)(2,1)}, bf16[4,4,128,256]{3,2,1,0:T(8,128)(2,1)}, bf16[4,4,128,256]{3,2,1,0:T(8,128)(2,1)}) custom-call(s32[2]{0:T(128)} %copy-done.22, s32[8]{0:T(128)} %copy-done.25, s32[8]{0:T(128)} %starts_ref.3, bf16[4,128,512]{2,1,0:T(8,128)(2,1)} %bitcast.294, bf16[4,128,512]{2,1,0:T(8,128)(2,1)} %bitcast.316, ...), custom_call_target="tpu_custom_call" | custom-call | flops 1 | bytes 1 | tf_op jit(solution)/shard_map/attend_back/pallas_call | solution.py:556
  280.5 5.6 %collective-permute-done.45 = bf16[1024,768]{1,0:T(8,128)(2,1)} collective-permute-done((bf16[1024,768]{1,0:T(8,128)(2,1)}, bf16[1024,768]{1,0:T(8,128)(2,1)}, u32[]{:S(2)}, u32[]{:S(2)}) %collective-permute-start.45) | collective-permute-done | bytes 1572896 | tf_op jit(solution)/shard_map/ppermute | solution.py:21
  294.8 8.3 %collective-permute-done.49 = bf16[2,2,64,2048]{3,2,1,0:T(8,128)(2,1)S(1)} collective-permute-done((bf16[2,2,64,2048]{3,2,1,0:T(8,128)(2,1)}, bf16[2,2,64,2048]{3,2,1,0:T(8,128)(2,1)S(1)}, u32[]{:S(2)}, u32[]{:S(2)}) %collective-permute-start.49) | collective-permute-done | bytes 1048608 | tf_op jit(solution)/shard_map/ppermute | solution.py:21
  306.0 21.7 %collective-permute-done.51 = bf16[4,64,768]{2,1,0:T(8,128)(2,1)S(1)} collective-permute-done((bf16[4,64,768]{2,1,0:T(8,128)(2,1)S(1)}, bf16[4,64,768]{2,1,0:T(8,128)(2,1)S(1)}, u32[]{:S(2)}, u32[]{:S(2)}) %collective-permute-start.51) | collective-permute-done | bytes 393248 | tf_op jit(solution)/shard_map/ppermute | solution.py:21
  340.8 15.2 %collective-permute-done.54 = bf16[4,64,768]{2,1,0:T(8,128)(2,1)S(1)} collective-permute-done((bf16[4,64,768]{2,1,0:T(8,128)(2,1)S(1)}, bf16[4,64,768]{2,1,0:T(8,128)(2,1)S(1)}, u32[]{:S(2)}, u32[]{:S(2)}) %collective-permute-start.54) | collective-permute-done | bytes 393248 | tf_op jit(solution)/shard_map/ppermute | solution.py:21
  368.8 7.9 %collective-permute-done.59 = bf16[2,4,128,256]{3,2,1,0:T(8,128)(2,1)S(1)} collective-permute-done((bf16[2,4,128,256]{3,2,1,0:T(8,128)(2,1)S(1)}, bf16[2,4,128,256]{3,2,1,0:T(8,128)(2,1)S(1)}, u32[]{:S(2)}, u32[]{:S(2)}) %collective-permute-start.59) | collective-permute-done | bytes 524320 | tf_op jit(solution)/shard_map/ppermute | solution.py:21
  388.8 4.9 %collective-permute-done.67 = bf16[1,4,128,256]{3,2,1,0:T(8,128)(2,1)S(1)} collective-permute-done((bf16[1,4,128,256]{3,2,1,0:T(8,128)(2,1)S(1)}, bf16[1,4,128,256]{3,2,1,0:T(8,128)(2,1)S(1)}, u32[]{:S(2)}, u32[]{:S(2)}) %collective-permute-start.67) | collective-permute-done | bytes 262176 | tf_op jit(solution)/shard_map/ppermute | solution.py:21
  397.2 4.0 collective-permute-done.64
  414.7 9.4 %collective-permute-done.68 = bf16[4,1,64,512]{3,2,1,0:T(8,128)(2,1)S(1)} collective-permute-done((bf16[4,1,64,512]{3,2,1,0:T(8,128)(2,1)S(1)}, bf16[4,1,64,512]{3,2,1,0:T(8,128)(2,1)S(1)}, u32[]{:S(2)}, u32[]{:S(2)}) %collective-permute-start.68) | collective-permute-done | bytes 262176 | tf_op jit(solution)/shard_map/ppermute | solution.py:21
  (428 shorter events, 202.5 us)
Async XLA Ops:
  7.9 45.1 %collective-permute-start = (bf16[128,2048]{1,0:T(8,128)(2,1)}, bf16[128,2048]{1,0:T(8,128)(2,1)}, u32[]{:S(2)}, u32[]{:S(2)}) collective-permute-start(bf16[128,2048]{1,0:T(8,128)(2,1)} %fusion.14), channel_id=1, source_target_pairs={{0,8},{1,9},{2,10},{3,11},{4,12},{5,13},{6,14},{7,15},{8,0},{9,1},... | collective-permute-start | bytes 1572872 | tf_op jit(solution)/shard_map/ppermute | solution.py:21
  16.5 23.3 %collective-permute-start.9 = (bf16[2,256,512]{2,1,0:T(8,128)(2,1)}, bf16[2,256,512]{2,1,0:T(8,128)(2,1)}, u32[]{:S(2)}, u32[]{:S(2)}) collective-permute-start(bf16[2,256,512]{2,1,0:T(8,128)(2,1)} %pad_maximum_fusion.11), channel_id=1, source_target_pairs={{0,16},{1,17},{2,18},{3,19},{4,20},{5,21},{6,22},{7,23},{8,24},{9,... | collective-permute-start | bytes 1572872 | tf_op jit(solution)/shard_map/ppermute | solution.py:21
  30.5 23.3 %collective-permute-start.7 = (bf16[128,2048]{1,0:T(8,128)(2,1)}, bf16[128,2048]{1,0:T(8,128)(2,1)S(1)}, u32[]{:S(2)}, u32[]{:S(2)}) collective-permute-start(bf16[128,2048]{1,0:T(8,128)(2,1)} %collective-permute-done.5), channel_id=1, source_target_pairs={{0,8},{1,9},{2,10},{3,11},{4,12},{5,13},{6,14},{7,15},{8,0},{9,1},... | collective-permute-start | bytes 1572872 | tf_op jit(solution)/shard_map/ppermute | solution.py:21
  44.2 24.9 %collective-permute-start.14 = (bf16[2,256,512]{2,1,0:T(8,128)(2,1)}, bf16[2,256,512]{2,1,0:T(8,128)(2,1)S(1)}, u32[]{:S(2)}, u32[]{:S(2)}) collective-permute-start(bf16[2,256,512]{2,1,0:T(8,128)(2,1)} %collective-permute-done.9), channel_id=1, source_target_pairs={{0,1},{1,0},{2,3},{3,2},{4,5},{5,4},{6,7},{7,6},{8,9},{9,8},{10,11... | collective-permute-start | bytes 1572872 | tf_op jit(solution)/shard_map/ppermute | solution.py:21
  53.0 32.0 %collective-permute-start.18 = (bf16[256,1536]{1,0:T(8,128)(2,1)S(1)}, bf16[256,1536]{1,0:T(8,128)(2,1)}, u32[]{:S(2)}, u32[]{:S(2)}) collective-permute-start(bf16[256,1536]{1,0:T(8,128)(2,1)S(1)} %get-tuple-element.141), channel_id=1, source_target_pairs={{0,16},{1,17},{2,18},{3,19},{4,20},{5,21},{6,22},{7,23},{8,24},{9,... | collective-permute-start | bytes 2359304 | tf_op jit(solution)/shard_map/ppermute | solution.py:21
  86.5 20.4 %collective-permute-start.21 = (bf16[256,1536]{1,0:T(8,128)(2,1)S(1)}, bf16[256,1536]{1,0:T(8,128)(2,1)S(1)}, u32[]{:S(2)}, u32[]{:S(2)}) collective-permute-start(bf16[256,1536]{1,0:T(8,128)(2,1)S(1)} %get-tuple-element.145), channel_id=1, source_target_pairs={{0,16},{1,17},{2,18},{3,19},{4,20},{5,21},{6,22},{7,23},{8,24},{9,... | collective-permute-start | bytes 2359304 | tf_op jit(solution)/shard_map/ppermute | solution.py:21
  89.6 28.1 %collective-permute-start.20 = (bf16[128,2048]{1,0:T(8,128)(2,1)S(1)}, bf16[128,2048]{1,0:T(8,128)(2,1)S(1)}, u32[]{:S(2)}, u32[]{:S(2)}) collective-permute-start(bf16[128,2048]{1,0:T(8,128)(2,1)S(1)} %fusion.39), channel_id=1, source_target_pairs={{0,16},{1,17},{2,18},{3,19},{4,20},{5,21},{6,22},{7,23},{8,24},{9,... | collective-permute-start | bytes 1572872 | tf_op jit(solution)/shard_map/ppermute | solution.py:21
  91.3 42.7 %collective-permute-start.28 = (bf16[2,128,2048]{2,1,0:T(8,128)(2,1)S(1)}, bf16[2,128,2048]{2,1,0:T(8,128)(2,1)S(1)}, u32[]{:S(2)}, u32[]{:S(2)}) collective-permute-start(bf16[2,128,2048]{2,1,0:T(8,128)(2,1)S(1)} %get-tuple-element.262), channel_id=1, source_target_pairs={{0,2},{1,3},{2,0},{3,1},{4,6},{5,7},{6,4},{7,5},{8,10},{9,11},{10,... | collective-permute-start | bytes 3145736 | tf_op jit(solution)/shard_map/ppermute | solution.py:21
  91.4 27.4 %collective-permute-start.24 = (bf16[256,1536]{1,0:T(8,128)(2,1)}, bf16[256,1536]{1,0:T(8,128)(2,1)S(1)}, u32[]{:S(2)}, u32[]{:S(2)}) collective-permute-start(bf16[256,1536]{1,0:T(8,128)(2,1)} %collective-permute-done.18), channel_id=1, source_target_pairs={{0,1},{1,0},{2,3},{3,2},{4,5},{5,4},{6,7},{7,6},{8,9},{9,8},{10,11... | collective-permute-start | bytes 2359304 | tf_op jit(solution)/shard_map/ppermute | solution.py:21
  118.8 20.4 %collective-permute-start.27 = (bf16[256,1536]{1,0:T(8,128)(2,1)S(1)}, bf16[256,1536]{1,0:T(8,128)(2,1)S(1)}, u32[]{:S(2)}, u32[]{:S(2)}) collective-permute-start(bf16[256,1536]{1,0:T(8,128)(2,1)S(1)} %collective-permute-done.21), channel_id=1, source_target_pairs={{0,1},{1,0},{2,3},{3,2},{4,5},{5,4},{6,7},{7,6},{8,9},{9,8},{10,11... | collective-permute-start | bytes 2359304 | tf_op jit(solution)/shard_map/ppermute | solution.py:21
  118.8 22.4 %collective-permute-start.33 = (bf16[512,1536]{1,0:T(8,128)(2,1)S(1)}, bf16[512,1536]{1,0:T(8,128)(2,1)S(1)}, u32[]{:S(2)}, u32[]{:S(2)}) collective-permute-start(bf16[512,1536]{1,0:T(8,128)(2,1)S(1)} %get-tuple-element.156), channel_id=1, source_target_pairs={{0,8},{1,9},{2,10},{3,11},{4,12},{5,13},{6,14},{7,15},{8,0},{9,1},... | collective-permute-start | bytes 4718600 | tf_op jit(solution)/shard_map/ppermute | solution.py:21
  201.7 41.5 %collective-permute-start.43 = (bf16[1024,768]{1,0:T(8,128)(2,1)}, bf16[1024,768]{1,0:T(8,128)(2,1)}, u32[]{:S(2)}, u32[]{:S(2)}) collective-permute-start(bf16[1024,768]{1,0:T(8,128)(2,1)} %get-tuple-element.183), channel_id=1, source_target_pairs={{0,1},{1,0},{2,3},{3,2},{4,5},{5,4},{6,7},{7,6},{8,9},{9,8},{10,11... | collective-permute-start | bytes 4718600 | tf_op jit(solution)/shard_map/ppermute | solution.py:21
  223.8 25.9 %collective-permute-start.44 = (bf16[2,128,2048]{2,1,0:T(8,128)(2,1)}, bf16[2,128,2048]{2,1,0:T(8,128)(2,1)}, u32[]{:S(2)}, u32[]{:S(2)}) collective-permute-start(bf16[2,128,2048]{2,1,0:T(8,128)(2,1)} %bitcast.45), channel_id=1, source_target_pairs={{0,2},{1,3},{2,0},{3,1},{4,6},{5,7},{6,4},{7,5},{8,10},{9,11},{10,... | collective-permute-start | bytes 3145736 | tf_op jit(solution)/shard_map/ppermute | solution.py:21
  249.7 36.3 %collective-permute-start.45 = (bf16[1024,768]{1,0:T(8,128)(2,1)}, bf16[1024,768]{1,0:T(8,128)(2,1)}, u32[]{:S(2)}, u32[]{:S(2)}) collective-permute-start(bf16[1024,768]{1,0:T(8,128)(2,1)} %get-tuple-element.190), channel_id=1, source_target_pairs={{0,1},{1,0},{2,3},{3,2},{4,5},{5,4},{6,7},{7,6},{8,9},{9,8},{10,11... | collective-permute-start | bytes 4718600 | tf_op jit(solution)/shard_map/ppermute | solution.py:21
  254.2 40.6 %collective-permute-start.48 = (bf16[4,1,2,64,768]{4,3,2,0,1:T(8,128)(2,1)}, bf16[4,1,2,64,768]{4,3,2,0,1:T(8,128)(2,1)}, u32[]{:S(2)}, u32[]{:S(2)}) collective-permute-start(bf16[4,1,2,64,768]{4,3,2,0,1:T(8,128)(2,1)} %fusion.33), channel_id=1, source_target_pairs={{0,4},{1,5},{2,6},{3,7},{4,0},{5,1},{6,2},{7,3},{8,12},{9,13},{10,... | collective-permute-start | bytes 2359304 | tf_op jit(solution)/shard_map/ppermute | solution.py:21
  258.7 44.5 %collective-permute-start.49 = (bf16[2,2,64,2048]{3,2,1,0:T(8,128)(2,1)}, bf16[2,2,64,2048]{3,2,1,0:T(8,128)(2,1)S(1)}, u32[]{:S(2)}, u32[]{:S(2)}) collective-permute-start(bf16[2,2,64,2048]{3,2,1,0:T(8,128)(2,1)} %fusion.22), channel_id=1, source_target_pairs={{0,2},{1,3},{2,0},{3,1},{4,6},{5,7},{6,4},{7,5},{8,10},{9,11},{10,... | collective-permute-start | bytes 3145736 | tf_op jit(solution)/shard_map/ppermute | solution.py:21
  290.1 43.8 %collective-permute-start.46 = (bf16[4,1,2,64,768]{4,3,2,0,1:T(8,128)(2,1)S(1)}, bf16[4,1,2,64,768]{4,3,2,0,1:T(8,128)(2,1)S(1)}, u32[]{:S(2)}, u32[]{:S(2)}) collective-permute-start(bf16[4,1,2,64,768]{4,3,2,0,1:T(8,128)(2,1)S(1)} %fusion.32), channel_id=1, source_target_pairs={{0,4},{1,5},{2,6},{3,7},{4,0},{5,1},{6,2},{7,3},{8,12},{9,13},{10,... | collective-permute-start | bytes 2359304 | tf_op jit(solution)/shard_map/ppermute | solution.py:21
  290.1 37.6 %collective-permute-start.52 = (bf16[384,2048]{1,0:T(8,128)(2,1)S(1)}, bf16[384,2048]{1,0:T(8,128)(2,1)S(1)}, u32[]{:S(2)}, u32[]{:S(2)}) collective-permute-start(bf16[384,2048]{1,0:T(8,128)(2,1)S(1)} %copy-done.28), channel_id=1, source_target_pairs={{0,1},{1,0},{2,3},{3,2},{4,5},{5,4},{6,7},{7,6},{8,9},{9,8},{10,11... | collective-permute-start | bytes 4718600 | tf_op jit(solution)/shard_map/ppermute | solution.py:21
  303.6 24.1 %collective-permute-start.50 = (bf16[128,2048]{1,0:T(8,128)(2,1)S(1)}, bf16[128,2048]{1,0:T(8,128)(2,1)S(1)}, u32[]{:S(2)}, u32[]{:S(2)}) collective-permute-start(bf16[128,2048]{1,0:T(8,128)(2,1)S(1)} %fusion.40), channel_id=1, source_target_pairs={{0,16},{1,17},{2,18},{3,19},{4,20},{5,21},{6,22},{7,23},{8,24},{9,... | collective-permute-start | bytes 1572872 | tf_op jit(solution)/shard_map/ppermute | solution.py:21
  305.1 22.6 %collective-permute-start.51 = (bf16[4,64,768]{2,1,0:T(8,128)(2,1)S(1)}, bf16[4,64,768]{2,1,0:T(8,128)(2,1)S(1)}, u32[]{:S(2)}, u32[]{:S(2)}) collective-permute-start(bf16[4,64,768]{2,1,0:T(8,128)(2,1)S(1)} %get-tuple-element.275), channel_id=1, source_target_pairs={{0,2},{1,3},{2,0},{3,1},{4,6},{5,7},{6,4},{7,5},{8,10},{9,11},{10,... | collective-permute-start | bytes 1179656 | tf_op jit(solution)/shard_map/ppermute | solution.py:21
  330.5 25.6 %collective-permute-start.57 = (bf16[4,4,128,256]{3,2,1,0:T(8,128)(2,1)S(1)}, bf16[4,4,128,256]{3,2,1,0:T(8,128)(2,1)S(1)}, u32[]{:S(2)}, u32[]{:S(2)}) collective-permute-start(bf16[4,4,128,256]{3,2,1,0:T(8,128)(2,1)S(1)} %copy-done.72), channel_id=1, source_target_pairs={{0,1},{1,0},{2,3},{3,2},{4,5},{5,4},{6,7},{7,6},{8,9},{9,8},{10,11... | collective-permute-start | bytes 3145736 | tf_op jit(solution)/shard_map/ppermute | solution.py:21
  331.4 34.3 %collective-permute-start.61 = (bf16[1,192,2048]{2,1,0:T(8,128)(2,1)S(1)}, bf16[1,192,2048]{2,1,0:T(8,128)(2,1)S(1)}, u32[]{:S(2)}, u32[]{:S(2)}) collective-permute-start(bf16[1,192,2048]{2,1,0:T(8,128)(2,1)S(1)} %fusion.34), channel_id=1, source_target_pairs={{0,4},{1,5},{2,6},{3,7},{4,0},{5,1},{6,2},{7,3},{8,12},{9,13},{10,... | collective-permute-start | bytes 2359304 | tf_op jit(solution)/shard_map/ppermute | solution.py:21
  356.2 24.2 %collective-permute-start.58 = (bf16[4,2,2,64,512]{4,3,2,1,0:T(8,128)(2,1)S(1)}, bf16[4,2,2,64,512]{4,3,2,1,0:T(8,128)(2,1)S(1)}, u32[]{:S(2)}, u32[]{:S(2)}) collective-permute-start(bf16[4,2,2,64,512]{4,3,2,1,0:T(8,128)(2,1)S(1)} %fusion.23), channel_id=1, source_target_pairs={{0,1},{1,0},{2,3},{3,2},{4,5},{5,4},{6,7},{7,6},{8,9},{9,8},{10,11... | collective-permute-start | bytes 3145736 | tf_op jit(solution)/shard_map/ppermute | solution.py:21
  377.4 19.8 %collective-permute-start.66 = (bf16[128,2048]{1,0:T(8,128)(2,1)}, bf16[128,2048]{1,0:T(8,128)(2,1)}, u32[]{:S(2)}, u32[]{:S(2)}) collective-permute-start(bf16[128,2048]{1,0:T(8,128)(2,1)} %slice_bitcast_fusion.3), channel_id=1, source_target_pairs={{0,16},{1,17},{2,18},{3,19},{4,20},{5,21},{6,22},{7,23},{8,24},{9,... | collective-permute-start | bytes 1572872 | tf_op jit(solution)/shard_map/ppermute | solution.py:21
  (126 other events, 1323.9 us)

commit v4 on v3

--- a/solution.py
+++ b/solution.py
@@ -338,35 +338,74 @@
     )(info, ha, hb, ga, gb, ua, ub)
 
 
-def rows_grad_kernel(info_ref, ha, hb, da, db, send_ref, keep_ref):
+def rows_grad_kernel(info_ref, ha, hb, da, db, send_one, send_two, keep_one, keep_two):
     odd = (info_ref[1] & 1) == 1
+    step = pl.program_id(0)
+    first = step < pl.num_programs(0) // 2
     grad = t_dot(ha[...], da[...]) + t_dot(hb[...], db[...])
     half = grad.shape[0] // 2
     low, upp = grad[:half], grad[half:]
-    send_ref[...] = jnp.where(odd, low, upp).astype(BF16)
-    keep_ref[...] = jnp.where(odd, upp, low)
+    send = jnp.where(odd, low, upp).astype(BF16)
+    keep = jnp.where(odd, upp, low)
+
+    @pl.when(first)
+    def _():
+        send_one[...] = send
+        keep_one[...] = keep
+
+    @pl.when(jnp.logical_not(first))
+    def _():
+        send_two[...] = send
+        keep_two[...] = keep
 
 
 def rows_grad(info, ha, hb, da, db):
     tokens, mine = ha.shape
     width = da.shape[1]
-    part = min(512, width)
-    half = pl.BlockSpec((mine // 2, part), lambda i: (0, i))
+    part = min(512, width // 2)
+    steps = width // part
+    one = pl.BlockSpec((mine // 2, part), lambda i: (0, jnp.minimum(i, steps // 2 - 1)))
+    two = pl.BlockSpec((mine // 2, part), lambda i: (0, jnp.maximum(i - steps // 2, 0)))
     lhs = pl.BlockSpec(ha.shape, lambda i: (0, 0))
     rhs = pl.BlockSpec((tokens, part), lambda i: (0, i))
     return pl.pallas_call(
         rows_grad_kernel,
-        grid=(width // part,),
+        grid=(steps,),
         in_specs=[pl.BlockSpec(memory_space=pltpu.SMEM), lhs, lhs, rhs, rhs],
-        out_specs=[half] * 2,
-        out_shape=[
-            jax.ShapeDtypeStruct((mine // 2, width), BF16),
-            jax.ShapeDtypeStruct((mine // 2, width), F32),
-        ],
+        out_specs=[one, two, one, two],
+        out_shape=[jax.ShapeDtypeStruct((mine // 2, width // 2), BF16)] * 2
+        + [jax.ShapeDtypeStruct((mine // 2, width // 2), F32)] * 2,
         compiler_params=pltpu.CompilerParams(vmem_limit_bytes=48 << 20),
-        cost_estimate=BRIEF,
         name="rows_grad",
     )(info, ha, hb, da, db)
+
+
+def query_back_kernel(rows, d_ref, w_ref, keep_ref, send_ref):
+    out = dot_t(d_ref[...], w_ref[...])
+    for k in range(2):
+        keep_ref[k] = out[2 * k * rows : (2 * k + 1) * rows]
+        send_ref[k] = out[(2 * k + 1) * rows : (2 * k + 2) * rows].astype(BF16)
+
+
+def query_back(d_query, wq, rows):
+    width, share = wq.shape
+    part = min(512, width)
+    out = pl.BlockSpec((2, rows, part), lambda j: (0, 0, j))
+    return pl.pallas_call(
+        functools.partial(query_back_kernel, rows),
+        grid=(width // part,),
+        in_specs=[
+            pl.BlockSpec(d_query.shape, lambda j: (0, 0)),
+            pl.BlockSpec((part, share), lambda j: (j, 0)),
+        ],
+        out_specs=[out, out],
+        out_shape=[
+            jax.ShapeDtypeStruct((2, rows, width), F32),
+            jax.ShapeDtypeStruct((2, rows, width), BF16),
+        ],
+        compiler_params=pltpu.CompilerParams(vmem_limit_bytes=32 << 20),
+        name="query_back",
+    )(d_query, wq)
 
 
 def unpack_kernel(
@@ -391,15 +430,22 @@
 
 def unpack(info, got_g, got_u, w_gate, w_up, gain, outer, chunk, wide):
     rows = got_g.shape[2]
+    weight = pl.BlockSpec((rows, w_gate.shape[1]), lambda i, info: (info[1], 0))
     shape = jax.ShapeDtypeStruct((rows, 16 * outer * chunk), F32)
-    vmem = pl.BlockSpec(memory_space=pltpu.VMEM)
+    def whole(value):
+        return pl.BlockSpec(value.shape, lambda i, info: (0,) * len(value.shape))
+
+    outs = [shape, shape, jax.ShapeDtypeStruct((rows, 1), F32)]
     return pl.pallas_call(
         functools.partial(unpack_kernel, outer, chunk, wide),
-        in_specs=[pl.BlockSpec(memory_space=pltpu.SMEM)] + [vmem] * 5,
-        out_specs=[vmem] * 3,
-        out_shape=[shape, shape, jax.ShapeDtypeStruct((rows, 1), F32)],
+        grid_spec=pltpu.PrefetchScalarGridSpec(
+            num_scalar_prefetch=1,
+            grid=(1,),
+            in_specs=[whole(got_g), whole(got_u), weight, weight, whole(gain)],
+            out_specs=[whole(out) for out in outs],
+        ),
+        out_shape=outs,
         compiler_params=pltpu.CompilerParams(vmem_limit_bytes=32 << 20),
-        cost_estimate=BRIEF,
         name="unpack",
     )(info, got_g, got_u, w_gate, w_up, gain)
 
@@ -736,7 +782,9 @@
     got_g = swap(send_g, xx)
     from_z, from_y = side_step(d_h_parts, to_z, to_y, rows, yy, zz)
     out_core = swap(dot(after(hidden_b, to_z), wd).astype(BF16), core)
-    send_d, keep_d = rows_grad(after(info, to_z), hidden_a, hidden_b, dy_a, dy_b)
+    send_d, send_e, keep_d, keep_e = rows_grad(
+        after(info, to_z), hidden_a, hidden_b, dy_a, dy_b
+    )
     out_parts = dot(after(hidden_a, to_z), wd)
     from_z, from_y, out_core, send_d, out_parts = together(
         from_z, from_y, out_core, send_d, out_parts
@@ -748,11 +796,10 @@
     )
     da_own = d_resid.astype(BF16)
     da_y, da_c = swap(da_own, yy), swap(da_own, core)
-    out_parts = (out_parts + out_core.astype(F32)).reshape(4, rows, width)
-    out_z = swap(out_parts[2:].astype(BF16), zz)
+    out_parts = (out_parts + out_core.astype(F32)).reshape(2, 2, rows, width)
     da_y, da_c = together(da_y, da_c)
     d_group = jnp.stack([da_own, da_c, da_y, swap(da_y, core)]).reshape(4 * rows, width)
-    d_group, got_g, out_z = together(d_group, got_g, out_z)
+    d_group, got_g = together(d_group, got_g)
 
     got_u = swap(after(send_u, got_g), xx)
     grad_g = (keep_g + got_g.astype(F32)).reshape(4, outer, 2, out_rows, mine)
@@ -760,28 +807,32 @@
     d_attn = dot_t(d_group, w_out).astype(BF16).reshape(4, rows, share)
     grad_o = t_dot(attn_rows, d_group).reshape(outer, 2, 2, out_rows, width)
     keep_o, got_o = part(grad_o, z_bit, zz, 1)
+    out_y = swap(after(out_parts, d_group)[:, 1].astype(BF16), yy)
     d_query, keep_kv, send_kv = attend_back(info, slots, starts, query, d_attn, attn, lse, kv)
-    d_query, send_kv, got_u, out_z = together(d_query, send_kv, got_u, out_z)
-    out_parts = out_parts[:2] + out_z.astype(F32)
-
-    got_d = swap(after(send_d, got_u), xx)
+    d_query, send_kv, got_u, out_y = together(d_query, send_kv, got_u, out_y)
+
+    got_kv = swap(send_kv, xx)
     grad_u = (keep_u + got_u.astype(F32)).reshape(4, outer, 2, out_rows, mine)
     keep_u, got_u = high_part(grad_u, r, high[-1], 1)
     d_query = d_query.reshape(4 * rows, share)
-    d_h_one = dot_t(d_query, wq_cols).reshape(2, 2, rows, width)
-    got_h = swap(d_h_one[:, 1].astype(BF16), core)
+    d_h_one, send_h = query_back(d_query, wq_cols, rows)
+    got_h = swap(send_h, core)
     d_wq = t_dot(h_group, d_query).reshape(4, outer, 2, 2, out_rows, share)
-    got_h, got_g, got_o, d_wq = together(got_h, got_g, got_o, d_wq)
-
-    d_h_one = d_h_one[:, 0] + got_h.astype(F32)
+    out_parts = out_parts[:, 0] + out_y.astype(F32)
+    got_h, got_g, d_wq = together(got_h, got_g, d_wq)
+
+    d_h_one = d_h_one + got_h.astype(F32)
     from_h = swap(d_h_one[1].astype(BF16), yy)
     grad_g = high_rest(keep_g, got_g, r, high, 1).astype(BF16)
     near_g, far_g = pick(grad_g, z_bit, 1), swap(pick(grad_g, 1 - z_bit, 1), zz)
-    from_h, far_g, got_d, send_kv, d_wq = together(from_h, far_g, got_d, send_kv, d_wq)
-
-    got_kv = swap(send_kv, xx)
-    grad_d = (keep_d + got_d.astype(F32)).reshape(outer, wide, width)
-    keep_d, got_d = high_part(grad_d, r, high[-1], 0)
+    got_kv, d_wq = together(got_kv, d_wq)
+
+    keep_q, got_q = part(d_wq, x_bit, xx, 3)
+    grad_kv = keep_kv.astype(F32) + got_kv.astype(F32)
+    grad_kv = grad_kv.reshape((outer, 2) + grad_kv.shape[1:])
+    keep_kv, got_kv = grad_kv[:, 0], swap(grad_kv[:, 1].astype(BF16), zz)
+    from_h, far_g, got_u, got_o = together(from_h, far_g, got_u, got_o)
+
     d_h_one = d_h_one[0] + from_h.astype(F32)
     scaled_one = d_h_one * gain_attn
     d_tokens = (
@@ -792,49 +843,61 @@
     grad_g = jnp.stack([near_g, far_g])
     grad_g = [pick(grad_g, g ^ j, 1) for j in range(4)]
     y_g = swap(jnp.stack([grad_g[2], grad_g[3]]), yy)
-    got_u, y_g, got_o = together(got_u, y_g, got_o)
-
     grad_u = high_rest(keep_u, got_u, r, high, 1).astype(BF16)
     near_u, far_u = pick(grad_u, z_bit, 1), swap(pick(grad_u, 1 - z_bit, 1), zz)
-    grad_g = jnp.stack(
-        [grad_g[0], swap(after(grad_g[1], y_g), core), y_g[0], swap(y_g[1], core)]
-    )
-    far_u, grad_g, got_kv, got_o, d_wq = together(far_u, grad_g, got_kv, got_o, d_wq)
-
-    keep_q, got_q = part(d_wq, x_bit, xx, 3)
-    grad_kv = keep_kv.astype(F32) + got_kv.astype(F32)
-    grad_kv = grad_kv.reshape((outer, 2) + grad_kv.shape[1:])
-    keep_kv, got_kv = grad_kv[:, 0], swap(grad_kv[:, 1].astype(BF16), zz)
-    grad_u = jnp.stack([near_u, far_u])
-    grad_u = [pick(grad_u, g ^ j, 1) for j in range(4)]
-    y_u = swap(jnp.stack([grad_u[2], grad_u[3]]), yy)
-    got_kv, y_u, got_d = together(got_kv, y_u, got_d)
-
-    d_wdown = high_rest(keep_d, got_d, r, high, 0)[:chunk]
+    y_g, got_kv, got_q, send_d, send_e = together(y_g, got_kv, got_q, send_d, send_e)
+
+    got_d = swap(send_d, xx)
+    keep_q, got_q = part(keep_q + got_q.astype(F32), z_bit, zz, 2)
     grad_kv = keep_kv + got_kv.astype(F32)
     for mask in reversed(high):
         grad_kv = grad_kv.reshape((2, grad_kv.shape[0] // 2) + grad_kv.shape[1:])
         grad_kv = grad_kv[0] + swap(grad_kv[1].astype(BF16), mask).astype(F32)
+    grad_g = jnp.stack(
+        [grad_g[0], swap(after(grad_g[1], y_g), core), y_g[0], swap(y_g[1], core)]
+    )
+    far_u, got_d, got_q, send_e, out_parts = together(far_u, got_d, got_q, send_e, out_parts)
+    out_z = swap(out_parts[1].astype(BF16), zz)
+
+    got_e = swap(send_e, xx)
+    keep_q, got_q = high_part(keep_q + got_q.astype(F32), r, high[-1], 1)
+    grad_d = (keep_d + got_d.astype(F32)).reshape(outer, wide, width // 2)
+    keep_d, got_d = high_part(grad_d, r, high[-1], 0)
+    grad_u = jnp.stack([near_u, far_u])
+    grad_u = [pick(grad_u, g ^ j, 1) for j in range(4)]
+    y_u = swap(jnp.stack([grad_u[2], grad_u[3]]), yy)
+    y_u, got_e, got_q, grad_g, grad_kv, keep_o = together(
+        y_u, got_e, got_q, grad_g, grad_kv, keep_o
+    )
+
+    grad_e = (keep_e + got_e.astype(F32)).reshape(outer, wide, width // 2)
+    keep_e, got_e = high_part(grad_e, r, high[-1], 0)
+    keep_o, got_o = part(keep_o + got_o.astype(F32), x_bit, xx, 1)
+    grad_kv = grad_kv[0].astype(BF16)
+    y_kv = swap(jnp.stack([grad_kv[2], grad_kv[3]]), yy)
     grad_u = jnp.stack(
         [grad_u[0], swap(after(grad_u[1], y_u), core), y_u[0], swap(y_u[1], core)]
     )
-    out_y = swap(after(out_parts[1], y_u).astype(BF16), yy)
-    got_q, grad_u, keep_o = together(got_q, grad_u, keep_o)
-    keep_q, got_q = part(keep_q + got_q.astype(F32), z_bit, zz, 2)
-    keep_o, got_o = part(keep_o + got_o.astype(F32), x_bit, xx, 1)
-    got_q, got_o, out_y, grad_kv = together(got_q, got_o, out_y, grad_kv)
-
-    output = (resid + out_parts[0] + out_y.astype(F32)).astype(BF16)
-    keep_q, got_q = high_part(keep_q + got_q.astype(F32), r, high[-1], 1)
+    d_wq = high_rest(keep_q, got_q, r, high, 1).astype(BF16)
+    d_wq = [pick(d_wq, g ^ j, 0) for j in range(4)]
+    y_q = swap(jnp.stack([d_wq[2], d_wq[3]]), yy)
+    y_q, y_kv, grad_u, got_o, got_d, got_e, out_z = together(
+        y_q, y_kv, grad_u, got_o, got_d, got_e, out_z
+    )
+
     keep_o, got_o = high_part(keep_o + got_o.astype(F32), r, high[-1], 0)
-    grad_kv = grad_kv[0].astype(BF16)
-    grad_kv = absolute(exchange_four([grad_kv[j] for j in range(4)], core, yy), g)
+    c_q, cy_q = swap(after(d_wq[1], y_q), core), swap(y_q[1], core)
+    d_wq = absolute([d_wq[0], c_q, y_q[0], cy_q], g)
+    d_wquery = jnp.concatenate(d_wq, axis=1).astype(F32)
+    grad_kv = [grad_kv[0], swap(after(grad_kv[1], y_kv), core), y_kv[0], swap(y_kv[1], core)]
+    grad_kv = absolute(grad_kv, g)
     d_keys = jnp.concatenate([piece[:, :HD] for piece in grad_kv], axis=1)
     d_values = jnp.concatenate([piece[:, HD:] for piece in grad_kv], axis=1)
-    d_wq = high_rest(keep_q, got_q, r, high, 1).astype(BF16)
-    d_wq = absolute(exchange_four([pick(d_wq, g ^ j, 0) for j in range(4)], core, yy), g)
-    d_wquery = jnp.concatenate(d_wq, axis=1).astype(F32)
+    output = (resid + out_parts[0] + out_z.astype(F32)).astype(BF16)
     d_wout = high_rest(keep_o, got_o, r, high, 0)
+    d_wdown = jnp.concatenate(
+        [high_rest(keep_d, got_d, r, high, 0), high_rest(keep_e, got_e, r, high, 0)], axis=1
+    )[:chunk]
 
     def own_rows(value):
         return lax.dynamic_slice_in_dim(value, r * out_rows, out_rows, 0)
@@ -842,7 +905,7 @@
     gain_at = (g * reps + r) * out_rows
     gain_rows = lax.dynamic_slice_in_dim(gain_ffn, gain_at, out_rows, 0)[:, None]
     d_wgate, d_wup, d_gain_two = unpack(
-        info, grad_g, grad_u, own_rows(w_gate), own_rows(w_up), gain_rows, outer, chunk, wide
+        info, grad_g, grad_u, w_gate, w_up, gain_rows, outer, chunk, wide
     )
     gain_rows = lax.dynamic_slice_in_dim(gain_attn, gain_at, out_rows, 0)
     d_gain_one = jnp.sum(d_wquery * own_rows(w_query).astype(F32), axis=1) / gain_rows

time: 440 us -> 426 us (0.968)
  local copies, waits for them, and re-layouts: 44.1 us -> 36.5 us
  Pallas kernels: 84.9 us -> 80.1 us
    ppermute x73 -> x75, waiting for transfers between devices: 176 us -> 171 us  [swap(): return lax.ppermute(value, BOTH, [(i, i ^ mask) for i in range(count)])]
    ppermute x73 -> x75, starting transfers between devices: 51.5 us -> 54.1 us  [swap(): return lax.ppermute(value, BOTH, [(i, i ^ mask) for i in range(count)])]
    pallas_call x2 -> x3, Pallas kernels: 9.57 us -> 11.8 us  [the longest x1 7.04 us: rows_grad(): pl.pallas_call(rows_grad_kernel, grid=(steps,), in_specs=[pl.BlockSpec(me...]
  transfers between devices with their start and end apart: 76 -> 78, of which waited for: 35 -> 32; matrix products, arithmetic and copies ran while one was open for 18% -> 18% of each run, Pallas kernels for 14% -> 14%
where the time goes in v4:
time: 426 us; the launch traced here: 420 us
  waiting for transfers between devices  176 us (41%)
  Pallas kernels  80.1 us (19%)
  starting transfers between devices  60.1 us (14%)
  other arithmetic  50.1 us (12%)
  local copies, waits for them, and re-layouts  36.5 us (9%)
  matrix products  14.3 us (3%)
    ppermute x75, waiting for transfers between devices, swap(): return lax.ppermute(value, BOTH, [(i, i ^ mask) for i in range(count)])  171 us
    ppermute x75, starting transfers between devices, swap(): return lax.ppermute(value, BOTH, [(i, i ^ mask) for i in range(count)])  54.1 us
    unnamed x155, local copies, waits for them, and re-layouts  17.8 us
    pallas_call x2, Pallas kernels, feed_forward(): pl.pallas_call(feed_forward_kernel, grid=(steps,), in_specs=[whole, whole...  17.3 us
    pallas_call x1, Pallas kernels, attend_back(): pl.pallas_call(functools.partial(attend_back_kernel, reps), grid=(4,), in...  12.1 us
    pallas_call x1, Pallas kernels, columns_grad(): pl.pallas_call(functools.partial(columns_grad_kernel, rows), grid=(width...  11.3 us
    dot_general x4, matrix products, dot(): return jnp.dot(a, b, preferred_element_type=F32)  9.53 us
  transfers between devices with their start and end apart: 78, of which 32 were waited for; matrix products, arithmetic and copies ran while one was open for 18% of the time, Pallas kernels for 14%

profile of v4, /device:TPU:0, one launch (start us, length us, event | category | flops | bytes accessed | tf_op | source)
XLA Modules:
  0.0 419.7 jit_solution(11579296596144287143)
XLA Ops:
  44.7 4.9 %collective-permute-done.11 = bf16[4,128,256]{2,1,0:T(8,128)(2,1)S(1)} collective-permute-done((bf16[4,128,256]{2,1,0:T(8,128)(2,1)}, bf16[4,128,256]{2,1,0:T(8,128)(2,1)S(1)}, u32[]{:S(2)}, u32[]{:S(2)}) %collective-permute-start.11) | collective-permute-done | bytes 262176 | tf_op jit(solution)/shard_map/ppermute | solution.py:692
  55.8 12.4 %collective-permute-done.13 = bf16[4,128,256]{2,1,0:T(8,128)(2,1)S(1)} collective-permute-done((bf16[4,128,256]{2,1,0:T(8,128)(2,1)S(1)}, bf16[4,128,256]{2,1,0:T(8,128)(2,1)S(1)}, u32[]{:S(2)}, u32[]{:S(2)}) %collective-permute-start.13) | collective-permute-done | bytes 262176 | tf_op jit(solution)/shard_map/ppermute | solution.py:21
  73.8 7.1 %attend.1 = (bf16[4,128,512]{2,1,0:T(8,128)(2,1)S(1)}, f32[4,512,1]{2,1,0:T(8,128)S(1)}) custom-call(s32[2]{0:T(128)S(1)} %pad_add_fusion.info_ref, s32[8]{0:T(128)S(1)} %and_add_fusion.slots_ref, s32[8]{0:T(128)S(1)} %copy-done.26, bf16[4,128,512]{2,1,0:T(8,128)(2,1)S(1)} %bitcast.298, bf16[8,4,128,256]{3,2,1,0:T(8,128)(2,1)S(1)} %bitcast_dynamic-update-slice_fusion.kv_ref), custom_call_target="tpu_custom_call" | custom-call | flops 1 | bytes 1 | tf_op jit(solution)/shard_map/attend/pallas_call | solution.py:512
  89.0 14.0 %collective-permute-done.21 = bf16[256,1536]{1,0:T(8,128)(2,1)S(1)} collective-permute-done((bf16[256,1536]{1,0:T(8,128)(2,1)S(1)}, bf16[256,1536]{1,0:T(8,128)(2,1)S(1)}, u32[]{:S(2)}, u32[]{:S(2)}) %collective-permute-start.21) | collective-permute-done | bytes 786464 | tf_op jit(solution)/shard_map/ppermute | solution.py:21
  102.9 10.8 %collective-permute-done.20 = bf16[128,2048]{1,0:T(8,128)(2,1)S(1)} collective-permute-done((bf16[128,2048]{1,0:T(8,128)(2,1)S(1)}, bf16[128,2048]{1,0:T(8,128)(2,1)S(1)}, u32[]{:S(2)}, u32[]{:S(2)}) %collective-permute-start.20) | collective-permute-done | bytes 524320 | tf_op jit(solution)/shard_map/ppermute | solution.py:21
  116.4 11.5 %collective-permute-done.22 = bf16[128,2048]{1,0:T(8,128)(2,1)S(1)} collective-permute-done((bf16[128,2048]{1,0:T(8,128)(2,1)S(1)}, bf16[128,2048]{1,0:T(8,128)(2,1)S(1)}, u32[]{:S(2)}, u32[]{:S(2)}) %collective-permute-start.22) | collective-permute-done | bytes 524320 | tf_op jit(solution)/shard_map/ppermute | solution.py:21
  144.9 8.6 %feed_forward.2 = (bf16[512,768]{1,0:T(8,128)(2,1)S(1)}, bf16[512,768]{1,0:T(8,128)(2,1)S(1)}, bf16[512,768]{1,0:T(8,128)(2,1)S(1)}) custom-call(bf16[512,2048]{1,0:T(8,128)(2,1)S(1)} %collective-permute-done.29.h_ref.hb, bf16[512,2048]{1,0:T(8,128)(2,1)} %copy-done.45, bf16[2048,1536]{1,0:T(8,128)(2,1)} %pad_maximum_fusion.gate_ref.up_ref.w_ref, ...), custom_call_target="tpu_custom_call" | custom-call | tf_op jit(solution)/shard_map/feed_forward/pallas_call | solution.py:243
  153.5 6.6 %inputs_grad.1 = bf16[512,2048]{1,0:T(8,128)(2,1)S(1)} custom-call(bf16[512,768]{1,0:T(8,128)(2,1)S(1)} %get-tuple-element.172.d_gate_ref.gb, bf16[512,768]{1,0:T(8,128)(2,1)S(1)} %get-tuple-element.168.d_up_ref.ub, bf16[2048,1536]{1,0:T(8,128)(2,1)} %pad_maximum_fusion.gate_ref.up_ref.w_ref), custom_call_target="tpu_custom_call" | custom-call | tf_op jit(solution)/shard_map/inputs_grad/pallas_call | solution.py:287
  160.5 8.6 %feed_forward.3 = (bf16[512,768]{1,0:T(8,128)(2,1)S(1)}, bf16[512,768]{1,0:T(8,128)(2,1)S(1)}, bf16[512,768]{1,0:T(8,128)(2,1)S(1)}) custom-call(bf16[512,2048]{1,0:T(8,128)(2,1)S(1)} %constant_dynamic-update-slice_fusion.h_ref.ha, bf16[512,2048]{1,0:T(8,128)(2,1)} %bitcast.301, bf16[2048,1536]{1,0:T(8,128)(2,1)} %pad_maximum_fusion.gate_ref.up_ref.w_ref, ...), custom_call_target="tpu_custom_call" | custom-call | tf_op jit(solution)/shard_map/feed_forward/pallas_call | solution.py:243
  169.2 8.1 %inputs_grad_sum.1 = (f32[384,2048]{1,0:T(8,128)}, bf16[64,2048]{1,0:T(8,128)(2,1)}, bf16[64,2048]{1,0:T(8,128)(2,1)}) custom-call(bf16[512,768]{1,0:T(8,128)(2,1)S(1)} %get-tuple-element.170.d_gate_ref.ga, bf16[512,768]{1,0:T(8,128)(2,1)S(1)} %get-tuple-element.171.d_up_ref.ua, bf16[2048,1536]{1,0:T(8,128)(2,1)} %pad_maximum_fusion.gate_ref.up_ref.w_ref, ...), custom_call_target="tpu_custom_call" | custom-call | tf_op jit(solution)/shard_map/inputs_grad_sum/pallas_call | solution.py:297
  179.9 11.3 %columns_grad.1 = (bf16[1024,768]{1,0:T(8,128)(2,1)}, bf16[1024,768]{1,0:T(8,128)(2,1)}, f32[1024,768]{1,0:T(8,128)}, f32[1024,768]{1,0:T(8,128)}) custom-call(s32[2]{0:T(128)} %copy-done.22, bf16[512,2048]{1,0:T(8,128)(2,1)} %copy-done.5, bf16[512,2048]{1,0:T(8,128)(2,1)} %copy-done.8, bf16[512,768]{1,0:T(8,128)(2,1)} %copy-done.13, ...), custom_call_target="tpu_custom_call" | custom-call | tf_op jit(solution)/shard_map/columns_grad/pallas_call | solution.py:329
  198.6 7.0 %rows_grad.1 = (bf16[384,1024]{1,0:T(8,128)(2,1)S(1)}, bf16[384,1024]{1,0:T(8,128)(2,1)S(1)}, f32[384,1024]{1,0:T(8,128)S(1)}, f32[384,1024]{1,0:T(8,128)}) custom-call(s32[2]{0:T(128)S(1)} %copy-done.23, bf16[512,768]{1,0:T(8,128)(2,1)S(1)} %copy-done.21, bf16[512,768]{1,0:T(8,128)(2,1)S(1)} %get-tuple-element.182.hb, bf16[512,2048]{1,0:T(8,128)(2,1)} %bitcast.302, ...), custom_call_target="tpu_custom_call" | custom-call | tf_op jit(solution)/shard_map/rows_grad/pallas_call | solution.py:371
  221.8 5.6 %collective-permute-done.40 = bf16[128,2048]{1,0:T(8,128)(2,1)} collective-permute-done((bf16[128,2048]{1,0:T(8,128)(2,1)}, bf16[128,2048]{1,0:T(8,128)(2,1)}, u32[]{:S(2)}, u32[]{:S(2)}) %collective-permute-start.40) | collective-permute-done | bytes 524320 | tf_op jit(solution)/shard_map/ppermute | solution.py:21
  250.7 12.1 %attend_back.1 = (bf16[4,128,512]{2,1,0:T(8,128)(2,1)}, bf16[4,4,128,256]{3,2,1,0:T(8,128)(2,1)}, bf16[4,4,128,256]{3,2,1,0:T(8,128)(2,1)}) custom-call(s32[2]{0:T(128)} %copy-done.22, s32[8]{0:T(128)} %copy-done.25, s32[8]{0:T(128)} %starts_ref.3, bf16[4,128,512]{2,1,0:T(8,128)(2,1)} %bitcast.299, bf16[4,128,512]{2,1,0:T(8,128)(2,1)} %bitcast.325, ...), custom_call_target="tpu_custom_call" | custom-call | flops 1 | bytes 1 | tf_op jit(solution)/shard_map/attend_back/pallas_call | solution.py:602
  264.9 5.4 %collective-permute-done.44 = bf16[1024,768]{1,0:T(8,128)(2,1)} collective-permute-done((bf16[1024,768]{1,0:T(8,128)(2,1)}, bf16[1024,768]{1,0:T(8,128)(2,1)}, u32[]{:S(2)}, u32[]{:S(2)}) %collective-permute-start.44) | collective-permute-done | bytes 1572896 | tf_op jit(solution)/shard_map/ppermute | solution.py:21
  285.7 16.0 %collective-permute-done.54 = bf16[4,4,128,256]{3,2,1,0:T(8,128)(2,1)S(1)} collective-permute-done((bf16[4,4,128,256]{3,2,1,0:T(8,128)(2,1)S(1)}, bf16[4,4,128,256]{3,2,1,0:T(8,128)(2,1)S(1)}, u32[]{:S(2)}, u32[]{:S(2)}) %collective-permute-start.54) | collective-permute-done | bytes 1048608 | tf_op jit(solution)/shard_map/ppermute | solution.py:21
  304.4 8.0 %collective-permute-done.50 = bf16[4,1,2,64,768]{4,3,2,0,1:T(8,128)(2,1)S(1)} collective-permute-done((bf16[4,1,2,64,768]{4,3,2,0,1:T(8,128)(2,1)S(1)}, bf16[4,1,2,64,768]{4,3,2,0,1:T(8,128)(2,1)S(1)}, u32[]{:S(2)}, u32[]{:S(2)}) %collective-permute-start.50) | collective-permute-done | bytes 786464 | tf_op jit(solution)/shard_map/ppermute | solution.py:21
  314.7 8.9 %collective-permute-done.55 = bf16[2,4,128,256]{3,2,1,0:T(8,128)(2,1)S(1)} collective-permute-done((bf16[2,4,128,256]{3,2,1,0:T(8,128)(2,1)S(1)}, bf16[2,4,128,256]{3,2,1,0:T(8,128)(2,1)S(1)}, u32[]{:S(2)}, u32[]{:S(2)}) %collective-permute-start.55) | collective-permute-done | bytes 524320 | tf_op jit(solution)/shard_map/ppermute | solution.py:21
  323.6 4.4 %collective-permute-done.56 = bf16[4,2,2,64,512]{4,3,2,1,0:T(8,128)(2,1)S(1)} collective-permute-done((bf16[4,2,2,64,512]{4,3,2,1,0:T(8,128)(2,1)S(1)}, bf16[4,2,2,64,512]{4,3,2,1,0:T(8,128)(2,1)S(1)}, u32[]{:S(2)}, u32[]{:S(2)}) %collective-permute-start.56) | collective-permute-done | bytes 1048608 | tf_op jit(solution)/shard_map/ppermute | solution.py:21
  333.4 11.0 %collective-permute-done.64 = bf16[1,4,128,256]{3,2,1,0:T(8,128)(2,1)S(1)} collective-permute-done((bf16[1,4,128,256]{3,2,1,0:T(8,128)(2,1)S(1)}, bf16[1,4,128,256]{3,2,1,0:T(8,128)(2,1)S(1)}, u32[]{:S(2)}, u32[]{:S(2)}) %collective-permute-start.64) | collective-permute-done | bytes 262176 | tf_op jit(solution)/shard_map/ppermute | solution.py:21
  344.6 4.2 collective-permute-done.58
  355.2 19.0 %collective-permute-done.61 = bf16[4,1,64,512]{3,2,1,0:T(8,128)(2,1)S(1)} collective-permute-done((bf16[4,1,64,512]{3,2,1,0:T(8,128)(2,1)S(1)}, bf16[4,1,64,512]{3,2,1,0:T(8,128)(2,1)S(1)}, u32[]{:S(2)}, u32[]{:S(2)}) %collective-permute-start.61) | collective-permute-done | bytes 262176 | tf_op jit(solution)/shard_map/ppermute | solution.py:21
  377.4 13.6 %collective-permute-done.70 = bf16[1,192,1024]{2,1,0:T(8,128)(2,1)S(1)} collective-permute-done((bf16[1,192,1024]{2,1,0:T(8,128)(2,1)S(1)}, bf16[1,192,1024]{2,1,0:T(8,128)(2,1)S(1)}, u32[]{:S(2)}, u32[]{:S(2)}) %collective-permute-start.70) | collective-permute-done | bytes 393248 | tf_op jit(solution)/shard_map/ppermute | solution.py:21
  393.7 4.1 collective-permute-done.65
  (434 shorter events, 193.4 us)
Async XLA Ops:
  7.9 44.3 %collective-permute-start = (bf16[128,2048]{1,0:T(8,128)(2,1)}, bf16[128,2048]{1,0:T(8,128)(2,1)}, u32[]{:S(2)}, u32[]{:S(2)}) collective-permute-start(bf16[128,2048]{1,0:T(8,128)(2,1)} %fusion.11), channel_id=1, source_target_pairs={{0,8},{1,9},{2,10},{3,11},{4,12},{5,13},{6,14},{7,15},{8,0},{9,1},... | collective-permute-start | bytes 1572872 | tf_op jit(solution)/shard_map/ppermute | solution.py:21
  15.8 23.9 %collective-permute-start.9 = (bf16[2,256,512]{2,1,0:T(8,128)(2,1)}, bf16[2,256,512]{2,1,0:T(8,128)(2,1)}, u32[]{:S(2)}, u32[]{:S(2)}) collective-permute-start(bf16[2,256,512]{2,1,0:T(8,128)(2,1)} %pad_maximum_fusion.12), channel_id=1, source_target_pairs={{0,16},{1,17},{2,18},{3,19},{4,20},{5,21},{6,22},{7,23},{8,24},{9,... | collective-permute-start | bytes 1572872 | tf_op jit(solution)/shard_map/ppermute | solution.py:21
  30.5 23.3 %collective-permute-start.7 = (bf16[128,2048]{1,0:T(8,128)(2,1)}, bf16[128,2048]{1,0:T(8,128)(2,1)S(1)}, u32[]{:S(2)}, u32[]{:S(2)}) collective-permute-start(bf16[128,2048]{1,0:T(8,128)(2,1)} %collective-permute-done.5), channel_id=1, source_target_pairs={{0,8},{1,9},{2,10},{3,11},{4,12},{5,13},{6,14},{7,15},{8,0},{9,1},... | collective-permute-start | bytes 1572872 | tf_op jit(solution)/shard_map/ppermute | solution.py:21
  43.2 25.0 %collective-permute-start.14 = (bf16[2,256,512]{2,1,0:T(8,128)(2,1)}, bf16[2,256,512]{2,1,0:T(8,128)(2,1)S(1)}, u32[]{:S(2)}, u32[]{:S(2)}) collective-permute-start(bf16[2,256,512]{2,1,0:T(8,128)(2,1)} %collective-permute-done.9), channel_id=1, source_target_pairs={{0,1},{1,0},{2,3},{3,2},{4,5},{5,4},{6,7},{7,6},{8,9},{9,8},{10,11... | collective-permute-start | bytes 1572872 | tf_op jit(solution)/shard_map/ppermute | solution.py:21
  52.2 28.8 %collective-permute-start.18 = (bf16[256,1536]{1,0:T(8,128)(2,1)S(1)}, bf16[256,1536]{1,0:T(8,128)(2,1)}, u32[]{:S(2)}, u32[]{:S(2)}) collective-permute-start(bf16[256,1536]{1,0:T(8,128)(2,1)S(1)} %get-tuple-element.150), channel_id=1, source_target_pairs={{0,16},{1,17},{2,18},{3,19},{4,20},{5,21},{6,22},{7,23},{8,24},{9,... | collective-permute-start | bytes 2359304 | tf_op jit(solution)/shard_map/ppermute | solution.py:21
  85.6 28.1 %collective-permute-start.20 = (bf16[128,2048]{1,0:T(8,128)(2,1)S(1)}, bf16[128,2048]{1,0:T(8,128)(2,1)S(1)}, u32[]{:S(2)}, u32[]{:S(2)}) collective-permute-start(bf16[128,2048]{1,0:T(8,128)(2,1)S(1)} %fusion.36), channel_id=1, source_target_pairs={{0,16},{1,17},{2,18},{3,19},{4,20},{5,21},{6,22},{7,23},{8,24},{9,... | collective-permute-start | bytes 1572872 | tf_op jit(solution)/shard_map/ppermute | solution.py:21
  87.4 43.4 %collective-permute-start.28 = (bf16[2,128,2048]{2,1,0:T(8,128)(2,1)S(1)}, bf16[2,128,2048]{2,1,0:T(8,128)(2,1)S(1)}, u32[]{:S(2)}, u32[]{:S(2)}) collective-permute-start(bf16[2,128,2048]{2,1,0:T(8,128)(2,1)S(1)} %get-tuple-element.280), channel_id=1, source_target_pairs={{0,2},{1,3},{2,0},{3,1},{4,6},{5,7},{6,4},{7,5},{8,10},{9,11},{10,... | collective-permute-start | bytes 3145736 | tf_op jit(solution)/shard_map/ppermute | solution.py:21
  88.4 27.9 %collective-permute-start.24 = (bf16[256,1536]{1,0:T(8,128)(2,1)}, bf16[256,1536]{1,0:T(8,128)(2,1)S(1)}, u32[]{:S(2)}, u32[]{:S(2)}) collective-permute-start(bf16[256,1536]{1,0:T(8,128)(2,1)} %collective-permute-done.18), channel_id=1, source_target_pairs={{0,1},{1,0},{2,3},{3,2},{4,5},{5,4},{6,7},{7,6},{8,9},{9,8},{10,11... | collective-permute-start | bytes 2359304 | tf_op jit(solution)/shard_map/ppermute | solution.py:21
  198.1 36.6 %collective-permute-start.43 = (bf16[1024,768]{1,0:T(8,128)(2,1)}, bf16[1024,768]{1,0:T(8,128)(2,1)}, u32[]{:S(2)}, u32[]{:S(2)}) collective-permute-start(bf16[1024,768]{1,0:T(8,128)(2,1)} %get-tuple-element.191), channel_id=1, source_target_pairs={{0,1},{1,0},{2,3},{3,2},{4,5},{5,4},{6,7},{7,6},{8,9},{9,8},{10,11... | collective-permute-start | bytes 4718600 | tf_op jit(solution)/shard_map/ppermute | solution.py:21
  234.6 35.7 %collective-permute-start.44 = (bf16[1024,768]{1,0:T(8,128)(2,1)}, bf16[1024,768]{1,0:T(8,128)(2,1)}, u32[]{:S(2)}, u32[]{:S(2)}) collective-permute-start(bf16[1024,768]{1,0:T(8,128)(2,1)} %get-tuple-element.198), channel_id=1, source_target_pairs={{0,1},{1,0},{2,3},{3,2},{4,5},{5,4},{6,7},{7,6},{8,9},{9,8},{10,11... | collective-permute-start | bytes 4718600 | tf_op jit(solution)/shard_map/ppermute | solution.py:21
  236.3 28.6 %collective-permute-start.45 = (bf16[2,128,2048]{2,1,0:T(8,128)(2,1)}, bf16[2,128,2048]{2,1,0:T(8,128)(2,1)}, u32[]{:S(2)}, u32[]{:S(2)}) collective-permute-start(bf16[2,128,2048]{2,1,0:T(8,128)(2,1)} %fusion.22), channel_id=1, source_target_pairs={{0,16},{1,17},{2,18},{3,19},{4,20},{5,21},{6,22},{7,23},{8,24},{9,... | collective-permute-start | bytes 3145736 | tf_op jit(solution)/shard_map/ppermute | solution.py:21
  240.6 40.2 %collective-permute-start.47 = (bf16[4,1,2,64,768]{4,3,2,0,1:T(8,128)(2,1)}, bf16[4,1,2,64,768]{4,3,2,0,1:T(8,128)(2,1)}, u32[]{:S(2)}, u32[]{:S(2)}) collective-permute-start(bf16[4,1,2,64,768]{4,3,2,0,1:T(8,128)(2,1)} %fusion.28), channel_id=1, source_target_pairs={{0,4},{1,5},{2,6},{3,7},{4,0},{5,1},{6,2},{7,3},{8,12},{9,13},{10,... | collective-permute-start | bytes 2359304 | tf_op jit(solution)/shard_map/ppermute | solution.py:21
  247.1 56.7 %collective-permute-start.51 = (bf16[2,2,64,2048]{3,2,1,0:T(8,128)(2,1)}, bf16[2,2,64,2048]{3,2,1,0:T(8,128)(2,1)S(1)}, u32[]{:S(2)}, u32[]{:S(2)}) collective-permute-start(bf16[2,2,64,2048]{3,2,1,0:T(8,128)(2,1)} %fusion.19), channel_id=1, source_target_pairs={{0,2},{1,3},{2,0},{3,1},{4,6},{5,7},{6,4},{7,5},{8,10},{9,11},{10,... | collective-permute-start | bytes 3145736 | tf_op jit(solution)/shard_map/ppermute | solution.py:21
  274.5 37.9 %collective-permute-start.50 = (bf16[4,1,2,64,768]{4,3,2,0,1:T(8,128)(2,1)S(1)}, bf16[4,1,2,64,768]{4,3,2,0,1:T(8,128)(2,1)S(1)}, u32[]{:S(2)}, u32[]{:S(2)}) collective-permute-start(bf16[4,1,2,64,768]{4,3,2,0,1:T(8,128)(2,1)S(1)} %fusion.29), channel_id=1, source_target_pairs={{0,4},{1,5},{2,6},{3,7},{4,0},{5,1},{6,2},{7,3},{8,12},{9,13},{10,... | collective-permute-start | bytes 2359304 | tf_op jit(solution)/shard_map/ppermute | solution.py:21
  276.5 25.3 %collective-permute-start.54 = (bf16[4,4,128,256]{3,2,1,0:T(8,128)(2,1)S(1)}, bf16[4,4,128,256]{3,2,1,0:T(8,128)(2,1)S(1)}, u32[]{:S(2)}, u32[]{:S(2)}) collective-permute-start(bf16[4,4,128,256]{3,2,1,0:T(8,128)(2,1)S(1)} %copy-done.68), channel_id=1, source_target_pairs={{0,1},{1,0},{2,3},{3,2},{4,5},{5,4},{6,7},{7,6},{8,9},{9,8},{10,11... | collective-permute-start | bytes 3145736 | tf_op jit(solution)/shard_map/ppermute | solution.py:21
  281.2 31.1 %collective-permute-start.48 = (bf16[128,2048]{1,0:T(8,128)(2,1)S(1)}, bf16[128,2048]{1,0:T(8,128)(2,1)S(1)}, u32[]{:S(2)}, u32[]{:S(2)}) collective-permute-start(bf16[128,2048]{1,0:T(8,128)(2,1)S(1)} %fusion.37), channel_id=1, source_target_pairs={{0,16},{1,17},{2,18},{3,19},{4,20},{5,21},{6,22},{7,23},{8,24},{9,... | collective-permute-start | bytes 1572872 | tf_op jit(solution)/shard_map/ppermute | solution.py:21
  284.2 28.1 %collective-permute-start.49 = (bf16[4,64,768]{2,1,0:T(8,128)(2,1)S(1)}, bf16[4,64,768]{2,1,0:T(8,128)(2,1)S(1)}, u32[]{:S(2)}, u32[]{:S(2)}) collective-permute-start(bf16[4,64,768]{2,1,0:T(8,128)(2,1)S(1)} %get-tuple-element.292), channel_id=1, source_target_pairs={{0,2},{1,3},{2,0},{3,1},{4,6},{5,7},{6,4},{7,5},{8,10},{9,11},{10,... | collective-permute-start | bytes 1179656 | tf_op jit(solution)/shard_map/ppermute | solution.py:21
  303.8 24.2 %collective-permute-start.56 = (bf16[4,2,2,64,512]{4,3,2,1,0:T(8,128)(2,1)S(1)}, bf16[4,2,2,64,512]{4,3,2,1,0:T(8,128)(2,1)S(1)}, u32[]{:S(2)}, u32[]{:S(2)}) collective-permute-start(bf16[4,2,2,64,512]{4,3,2,1,0:T(8,128)(2,1)S(1)} %fusion.20), channel_id=1, source_target_pairs={{0,1},{1,0},{2,3},{3,2},{4,5},{5,4},{6,7},{7,6},{8,9},{9,8},{10,11... | collective-permute-start | bytes 3145736 | tf_op jit(solution)/shard_map/ppermute | solution.py:21
  312.6 31.9 %collective-permute-start.52 = (bf16[4,64,768]{2,1,0:T(8,128)(2,1)S(1)}, bf16[4,64,768]{2,1,0:T(8,128)(2,1)S(1)}, u32[]{:S(2)}, u32[]{:S(2)}) collective-permute-start(bf16[4,64,768]{2,1,0:T(8,128)(2,1)S(1)} %get-tuple-element.293), channel_id=1, source_target_pairs={{0,2},{1,3},{2,0},{3,1},{4,6},{5,7},{6,4},{7,5},{8,10},{9,11},{10,... | collective-permute-start | bytes 1179656 | tf_op jit(solution)/shard_map/ppermute | solution.py:21
  348.9 25.3 %collective-permute-start.59 = (bf16[2,2,64,768]{3,2,1,0:T(8,128)(2,1)S(1)}, bf16[2,2,64,768]{3,2,1,0:T(8,128)(2,1)S(1)}, u32[]{:S(2)}, u32[]{:S(2)}) collective-permute-start(bf16[2,2,64,768]{3,2,1,0:T(8,128)(2,1)S(1)} %pad_maximum_fusion.16), channel_id=1, source_target_pairs={{0,16},{1,17},{2,18},{3,19},{4,20},{5,21},{6,22},{7,23},{8,24},{9,... | collective-permute-start | bytes 1179656 | tf_op jit(solution)/shard_map/ppermute | solution.py:21
  350.4 23.9 %collective-permute-start.60 = (bf16[384,1024]{1,0:T(8,128)(2,1)S(1)}, bf16[384,1024]{1,0:T(8,128)(2,1)S(1)}, u32[]{:S(2)}, u32[]{:S(2)}) collective-permute-start(bf16[384,1024]{1,0:T(8,128)(2,1)S(1)} %copy-done.28), channel_id=1, source_target_pairs={{0,1},{1,0},{2,3},{3,2},{4,5},{5,4},{6,7},{7,6},{8,9},{9,8},{10,11... | collective-permute-start | bytes 2359304 | tf_op jit(solution)/shard_map/ppermute | solution.py:21
  352.5 38.5 %collective-permute-start.70 = (bf16[1,192,1024]{2,1,0:T(8,128)(2,1)S(1)}, bf16[1,192,1024]{2,1,0:T(8,128)(2,1)S(1)}, u32[]{:S(2)}, u32[]{:S(2)}) collective-permute-start(bf16[1,192,1024]{2,1,0:T(8,128)(2,1)S(1)} %fusion.42), channel_id=1, source_target_pairs={{0,4},{1,5},{2,6},{3,7},{4,0},{5,1},{6,2},{7,3},{8,12},{9,13},{10,... | collective-permute-start | bytes 1179656 | tf_op jit(solution)/shard_map/ppermute | solution.py:21
  354.6 39.1 %collective-permute-start.72 = (bf16[128,2048]{1,0:T(8,128)(2,1)S(1)}, bf16[128,2048]{1,0:T(8,128)(2,1)S(1)}, u32[]{:S(2)}, u32[]{:S(2)}) collective-permute-start(bf16[128,2048]{1,0:T(8,128)(2,1)S(1)} %fusion.38), channel_id=1, source_target_pairs={{0,2},{1,3},{2,0},{3,1},{4,6},{5,7},{6,4},{7,5},{8,10},{9,11},{10,... | collective-permute-start | bytes 1572872 | tf_op jit(solution)/shard_map/ppermute | solution.py:21
  374.8 25.5 %collective-permute-start.69 = (bf16[2,64,2048]{2,1,0:T(8,128)(2,1)S(1)}, bf16[2,64,2048]{2,1,0:T(8,128)(2,1)S(1)}, u32[]{:S(2)}, u32[]{:S(2)}) collective-permute-start(bf16[2,64,2048]{2,1,0:T(8,128)(2,1)S(1)} %fusion.33), channel_id=1, source_target_pairs={{0,1},{1,0},{2,3},{3,2},{4,5},{5,4},{6,7},{7,6},{8,9},{9,8},{10,11... | collective-permute-start | bytes 1572872 | tf_op jit(solution)/shard_map/ppermute | solution.py:21
  (127 other events, 1504.2 us)

commit v5 on v4

--- a/solution.py
+++ b/solution.py
@@ -226,7 +226,7 @@
     gate = dot(h, gate_ref[...])
     upper = dot(h, up_ref[...])
     d_hidden = dot_t(dy_ref[...], down_ref[...])
-    sigma = 1.0 / (1.0 + jnp.exp(-gate))
+    sigma = jax.nn.sigmoid(gate)
     swish = gate * sigma
     hid_ref[...] = (swish * upper).astype(BF16)
     d_up_ref[...] = (d_hidden * swish).astype(BF16)

time: 426 us -> 427 us (level)
  no operation moved by 1% of the time
where the time goes in v5:
time: 427 us; the launch traced here: 420 us
  waiting for transfers between devices  176 us (41%)
  Pallas kernels  80.1 us (19%)
  starting transfers between devices  59.8 us (14%)
  other arithmetic  50.1 us (12%)
  local copies, waits for them, and re-layouts  36.4 us (9%)
  matrix products  14.2 us (3%)
    ppermute x75, waiting for transfers between devices, swap(): return lax.ppermute(value, BOTH, [(i, i ^ mask) for i in range(count)])  171 us
    ppermute x75, starting transfers between devices, swap(): return lax.ppermute(value, BOTH, [(i, i ^ mask) for i in range(count)])  53.8 us
    unnamed x155, local copies, waits for them, and re-layouts  17.8 us
    pallas_call x2, Pallas kernels, feed_forward(): pl.pallas_call(feed_forward_kernel, grid=(steps,), in_specs=[whole, whole...  17.3 us
    pallas_call x1, Pallas kernels, attend_back(): pl.pallas_call(functools.partial(attend_back_kernel, reps), grid=(4,), in...  12.1 us
    pallas_call x1, Pallas kernels, columns_grad(): pl.pallas_call(functools.partial(columns_grad_kernel, rows), grid=(width...  11.3 us
    dot_general x4, matrix products, dot(): return jnp.dot(a, b, preferred_element_type=F32)  9.53 us
  transfers between devices with their start and end apart: 78, of which 32 were waited for; matrix products, arithmetic and copies ran while one was open for 18% of the time, Pallas kernels for 14%

profile of v5, /device:TPU:0, one launch (start us, length us, event | category | flops | bytes accessed | tf_op | source)
XLA Modules:
  0.0 419.7 jit_solution(15812093713021059329)
XLA Ops:
  44.7 4.9 %collective-permute-done.11 = bf16[4,128,256]{2,1,0:T(8,128)(2,1)S(1)} collective-permute-done((bf16[4,128,256]{2,1,0:T(8,128)(2,1)}, bf16[4,128,256]{2,1,0:T(8,128)(2,1)S(1)}, u32[]{:S(2)}, u32[]{:S(2)}) %collective-permute-start.11) | collective-permute-done | bytes 262176 | tf_op jit(solution)/shard_map/ppermute | solution.py:692
  55.8 12.4 %collective-permute-done.13 = bf16[4,128,256]{2,1,0:T(8,128)(2,1)S(1)} collective-permute-done((bf16[4,128,256]{2,1,0:T(8,128)(2,1)S(1)}, bf16[4,128,256]{2,1,0:T(8,128)(2,1)S(1)}, u32[]{:S(2)}, u32[]{:S(2)}) %collective-permute-start.13) | collective-permute-done | bytes 262176 | tf_op jit(solution)/shard_map/ppermute | solution.py:21
  73.8 7.1 %attend.1 = (bf16[4,128,512]{2,1,0:T(8,128)(2,1)S(1)}, f32[4,512,1]{2,1,0:T(8,128)S(1)}) custom-call(s32[2]{0:T(128)S(1)} %pad_add_fusion.info_ref, s32[8]{0:T(128)S(1)} %and_add_fusion.slots_ref, s32[8]{0:T(128)S(1)} %copy-done.26, bf16[4,128,512]{2,1,0:T(8,128)(2,1)S(1)} %bitcast.298, bf16[8,4,128,256]{3,2,1,0:T(8,128)(2,1)S(1)} %bitcast_dynamic-update-slice_fusion.kv_ref), custom_call_target="tpu_custom_call" | custom-call | flops 1 | bytes 1 | tf_op jit(solution)/shard_map/attend/pallas_call | solution.py:512
  89.0 14.0 %collective-permute-done.21 = bf16[256,1536]{1,0:T(8,128)(2,1)S(1)} collective-permute-done((bf16[256,1536]{1,0:T(8,128)(2,1)S(1)}, bf16[256,1536]{1,0:T(8,128)(2,1)S(1)}, u32[]{:S(2)}, u32[]{:S(2)}) %collective-permute-start.21) | collective-permute-done | bytes 786464 | tf_op jit(solution)/shard_map/ppermute | solution.py:21
  102.9 10.8 %collective-permute-done.20 = bf16[128,2048]{1,0:T(8,128)(2,1)S(1)} collective-permute-done((bf16[128,2048]{1,0:T(8,128)(2,1)S(1)}, bf16[128,2048]{1,0:T(8,128)(2,1)S(1)}, u32[]{:S(2)}, u32[]{:S(2)}) %collective-permute-start.20) | collective-permute-done | bytes 524320 | tf_op jit(solution)/shard_map/ppermute | solution.py:21
  116.4 11.5 %collective-permute-done.22 = bf16[128,2048]{1,0:T(8,128)(2,1)S(1)} collective-permute-done((bf16[128,2048]{1,0:T(8,128)(2,1)S(1)}, bf16[128,2048]{1,0:T(8,128)(2,1)S(1)}, u32[]{:S(2)}, u32[]{:S(2)}) %collective-permute-start.22) | collective-permute-done | bytes 524320 | tf_op jit(solution)/shard_map/ppermute | solution.py:21
  144.9 8.6 %feed_forward.2 = (bf16[512,768]{1,0:T(8,128)(2,1)S(1)}, bf16[512,768]{1,0:T(8,128)(2,1)S(1)}, bf16[512,768]{1,0:T(8,128)(2,1)S(1)}) custom-call(bf16[512,2048]{1,0:T(8,128)(2,1)S(1)} %collective-permute-done.29.h_ref.hb, bf16[512,2048]{1,0:T(8,128)(2,1)} %copy-done.45, bf16[2048,1536]{1,0:T(8,128)(2,1)} %pad_maximum_fusion.gate_ref.up_ref.w_ref, ...), custom_call_target="tpu_custom_call" | custom-call | tf_op jit(solution)/shard_map/feed_forward/pallas_call | solution.py:243
  153.5 6.6 %inputs_grad.1 = bf16[512,2048]{1,0:T(8,128)(2,1)S(1)} custom-call(bf16[512,768]{1,0:T(8,128)(2,1)S(1)} %get-tuple-element.172.d_gate_ref.gb, bf16[512,768]{1,0:T(8,128)(2,1)S(1)} %get-tuple-element.168.d_up_ref.ub, bf16[2048,1536]{1,0:T(8,128)(2,1)} %pad_maximum_fusion.gate_ref.up_ref.w_ref), custom_call_target="tpu_custom_call" | custom-call | tf_op jit(solution)/shard_map/inputs_grad/pallas_call | solution.py:287
  160.5 8.7 %feed_forward.3 = (bf16[512,768]{1,0:T(8,128)(2,1)S(1)}, bf16[512,768]{1,0:T(8,128)(2,1)S(1)}, bf16[512,768]{1,0:T(8,128)(2,1)S(1)}) custom-call(bf16[512,2048]{1,0:T(8,128)(2,1)S(1)} %constant_dynamic-update-slice_fusion.h_ref.ha, bf16[512,2048]{1,0:T(8,128)(2,1)} %bitcast.301, bf16[2048,1536]{1,0:T(8,128)(2,1)} %pad_maximum_fusion.gate_ref.up_ref.w_ref, ...), custom_call_target="tpu_custom_call" | custom-call | tf_op jit(solution)/shard_map/feed_forward/pallas_call | solution.py:243
  169.2 8.1 %inputs_grad_sum.1 = (f32[384,2048]{1,0:T(8,128)}, bf16[64,2048]{1,0:T(8,128)(2,1)}, bf16[64,2048]{1,0:T(8,128)(2,1)}) custom-call(bf16[512,768]{1,0:T(8,128)(2,1)S(1)} %get-tuple-element.170.d_gate_ref.ga, bf16[512,768]{1,0:T(8,128)(2,1)S(1)} %get-tuple-element.171.d_up_ref.ua, bf16[2048,1536]{1,0:T(8,128)(2,1)} %pad_maximum_fusion.gate_ref.up_ref.w_ref, ...), custom_call_target="tpu_custom_call" | custom-call | tf_op jit(solution)/shard_map/inputs_grad_sum/pallas_call | solution.py:297
  179.9 11.3 %columns_grad.1 = (bf16[1024,768]{1,0:T(8,128)(2,1)}, bf16[1024,768]{1,0:T(8,128)(2,1)}, f32[1024,768]{1,0:T(8,128)}, f32[1024,768]{1,0:T(8,128)}) custom-call(s32[2]{0:T(128)} %copy-done.22, bf16[512,2048]{1,0:T(8,128)(2,1)} %copy-done.5, bf16[512,2048]{1,0:T(8,128)(2,1)} %copy-done.8, bf16[512,768]{1,0:T(8,128)(2,1)} %copy-done.13, ...), custom_call_target="tpu_custom_call" | custom-call | tf_op jit(solution)/shard_map/columns_grad/pallas_call | solution.py:329
  198.6 7.0 %rows_grad.1 = (bf16[384,1024]{1,0:T(8,128)(2,1)S(1)}, bf16[384,1024]{1,0:T(8,128)(2,1)S(1)}, f32[384,1024]{1,0:T(8,128)S(1)}, f32[384,1024]{1,0:T(8,128)}) custom-call(s32[2]{0:T(128)S(1)} %copy-done.23, bf16[512,768]{1,0:T(8,128)(2,1)S(1)} %copy-done.21, bf16[512,768]{1,0:T(8,128)(2,1)S(1)} %get-tuple-element.182.hb, bf16[512,2048]{1,0:T(8,128)(2,1)} %bitcast.302, ...), custom_call_target="tpu_custom_call" | custom-call | tf_op jit(solution)/shard_map/rows_grad/pallas_call | solution.py:371
  221.8 5.6 %collective-permute-done.40 = bf16[128,2048]{1,0:T(8,128)(2,1)} collective-permute-done((bf16[128,2048]{1,0:T(8,128)(2,1)}, bf16[128,2048]{1,0:T(8,128)(2,1)}, u32[]{:S(2)}, u32[]{:S(2)}) %collective-permute-start.40) | collective-permute-done | bytes 524320 | tf_op jit(solution)/shard_map/ppermute | solution.py:21
  250.5 12.1 %attend_back.1 = (bf16[4,128,512]{2,1,0:T(8,128)(2,1)}, bf16[4,4,128,256]{3,2,1,0:T(8,128)(2,1)}, bf16[4,4,128,256]{3,2,1,0:T(8,128)(2,1)}) custom-call(s32[2]{0:T(128)} %copy-done.22, s32[8]{0:T(128)} %copy-done.25, s32[8]{0:T(128)} %starts_ref.3, bf16[4,128,512]{2,1,0:T(8,128)(2,1)} %bitcast.299, bf16[4,128,512]{2,1,0:T(8,128)(2,1)} %bitcast.325, ...), custom_call_target="tpu_custom_call" | custom-call | flops 1 | bytes 1 | tf_op jit(solution)/shard_map/attend_back/pallas_call | solution.py:602
  264.6 5.7 %collective-permute-done.44 = bf16[1024,768]{1,0:T(8,128)(2,1)} collective-permute-done((bf16[1024,768]{1,0:T(8,128)(2,1)}, bf16[1024,768]{1,0:T(8,128)(2,1)}, u32[]{:S(2)}, u32[]{:S(2)}) %collective-permute-start.44) | collective-permute-done | bytes 1572896 | tf_op jit(solution)/shard_map/ppermute | solution.py:21
  285.8 16.0 %collective-permute-done.54 = bf16[4,4,128,256]{3,2,1,0:T(8,128)(2,1)S(1)} collective-permute-done((bf16[4,4,128,256]{3,2,1,0:T(8,128)(2,1)S(1)}, bf16[4,4,128,256]{3,2,1,0:T(8,128)(2,1)S(1)}, u32[]{:S(2)}, u32[]{:S(2)}) %collective-permute-start.54) | collective-permute-done | bytes 1048608 | tf_op jit(solution)/shard_map/ppermute | solution.py:21
  304.4 7.9 %collective-permute-done.50 = bf16[4,1,2,64,768]{4,3,2,0,1:T(8,128)(2,1)S(1)} collective-permute-done((bf16[4,1,2,64,768]{4,3,2,0,1:T(8,128)(2,1)S(1)}, bf16[4,1,2,64,768]{4,3,2,0,1:T(8,128)(2,1)S(1)}, u32[]{:S(2)}, u32[]{:S(2)}) %collective-permute-start.50) | collective-permute-done | bytes 786464 | tf_op jit(solution)/shard_map/ppermute | solution.py:21
  314.7 8.9 %collective-permute-done.55 = bf16[2,4,128,256]{3,2,1,0:T(8,128)(2,1)S(1)} collective-permute-done((bf16[2,4,128,256]{3,2,1,0:T(8,128)(2,1)S(1)}, bf16[2,4,128,256]{3,2,1,0:T(8,128)(2,1)S(1)}, u32[]{:S(2)}, u32[]{:S(2)}) %collective-permute-start.55) | collective-permute-done | bytes 524320 | tf_op jit(solution)/shard_map/ppermute | solution.py:21
  323.6 4.4 %collective-permute-done.56 = bf16[4,2,2,64,512]{4,3,2,1,0:T(8,128)(2,1)S(1)} collective-permute-done((bf16[4,2,2,64,512]{4,3,2,1,0:T(8,128)(2,1)S(1)}, bf16[4,2,2,64,512]{4,3,2,1,0:T(8,128)(2,1)S(1)}, u32[]{:S(2)}, u32[]{:S(2)}) %collective-permute-start.56) | collective-permute-done | bytes 1048608 | tf_op jit(solution)/shard_map/ppermute | solution.py:21
  333.4 11.1 %collective-permute-done.64 = bf16[1,4,128,256]{3,2,1,0:T(8,128)(2,1)S(1)} collective-permute-done((bf16[1,4,128,256]{3,2,1,0:T(8,128)(2,1)S(1)}, bf16[1,4,128,256]{3,2,1,0:T(8,128)(2,1)S(1)}, u32[]{:S(2)}, u32[]{:S(2)}) %collective-permute-start.64) | collective-permute-done | bytes 262176 | tf_op jit(solution)/shard_map/ppermute | solution.py:21
  344.6 4.2 collective-permute-done.58
  355.2 19.0 %collective-permute-done.61 = bf16[4,1,64,512]{3,2,1,0:T(8,128)(2,1)S(1)} collective-permute-done((bf16[4,1,64,512]{3,2,1,0:T(8,128)(2,1)S(1)}, bf16[4,1,64,512]{3,2,1,0:T(8,128)(2,1)S(1)}, u32[]{:S(2)}, u32[]{:S(2)}) %collective-permute-start.61) | collective-permute-done | bytes 262176 | tf_op jit(solution)/shard_map/ppermute | solution.py:21
  377.4 13.7 %collective-permute-done.70 = bf16[1,192,1024]{2,1,0:T(8,128)(2,1)S(1)} collective-permute-done((bf16[1,192,1024]{2,1,0:T(8,128)(2,1)S(1)}, bf16[1,192,1024]{2,1,0:T(8,128)(2,1)S(1)}, u32[]{:S(2)}, u32[]{:S(2)}) %collective-permute-start.70) | collective-permute-done | bytes 393248 | tf_op jit(solution)/shard_map/ppermute | solution.py:21
  393.9 4.1 collective-permute-done.65
  (434 shorter events, 193.1 us)
Async XLA Ops:
  7.9 44.3 %collective-permute-start = (bf16[128,2048]{1,0:T(8,128)(2,1)}, bf16[128,2048]{1,0:T(8,128)(2,1)}, u32[]{:S(2)}, u32[]{:S(2)}) collective-permute-start(bf16[128,2048]{1,0:T(8,128)(2,1)} %fusion.11), channel_id=1, source_target_pairs={{0,8},{1,9},{2,10},{3,11},{4,12},{5,13},{6,14},{7,15},{8,0},{9,1},... | collective-permute-start | bytes 1572872 | tf_op jit(solution)/shard_map/ppermute | solution.py:21
  15.8 23.9 %collective-permute-start.9 = (bf16[2,256,512]{2,1,0:T(8,128)(2,1)}, bf16[2,256,512]{2,1,0:T(8,128)(2,1)}, u32[]{:S(2)}, u32[]{:S(2)}) collective-permute-start(bf16[2,256,512]{2,1,0:T(8,128)(2,1)} %pad_maximum_fusion.12), channel_id=1, source_target_pairs={{0,16},{1,17},{2,18},{3,19},{4,20},{5,21},{6,22},{7,23},{8,24},{9,... | collective-permute-start | bytes 1572872 | tf_op jit(solution)/shard_map/ppermute | solution.py:21
  30.5 23.3 %collective-permute-start.7 = (bf16[128,2048]{1,0:T(8,128)(2,1)}, bf16[128,2048]{1,0:T(8,128)(2,1)S(1)}, u32[]{:S(2)}, u32[]{:S(2)}) collective-permute-start(bf16[128,2048]{1,0:T(8,128)(2,1)} %collective-permute-done.5), channel_id=1, source_target_pairs={{0,8},{1,9},{2,10},{3,11},{4,12},{5,13},{6,14},{7,15},{8,0},{9,1},... | collective-permute-start | bytes 1572872 | tf_op jit(solution)/shard_map/ppermute | solution.py:21
  43.2 25.0 %collective-permute-start.14 = (bf16[2,256,512]{2,1,0:T(8,128)(2,1)}, bf16[2,256,512]{2,1,0:T(8,128)(2,1)S(1)}, u32[]{:S(2)}, u32[]{:S(2)}) collective-permute-start(bf16[2,256,512]{2,1,0:T(8,128)(2,1)} %collective-permute-done.9), channel_id=1, source_target_pairs={{0,1},{1,0},{2,3},{3,2},{4,5},{5,4},{6,7},{7,6},{8,9},{9,8},{10,11... | collective-permute-start | bytes 1572872 | tf_op jit(solution)/shard_map/ppermute | solution.py:21
  52.2 28.8 %collective-permute-start.18 = (bf16[256,1536]{1,0:T(8,128)(2,1)S(1)}, bf16[256,1536]{1,0:T(8,128)(2,1)}, u32[]{:S(2)}, u32[]{:S(2)}) collective-permute-start(bf16[256,1536]{1,0:T(8,128)(2,1)S(1)} %get-tuple-element.150), channel_id=1, source_target_pairs={{0,16},{1,17},{2,18},{3,19},{4,20},{5,21},{6,22},{7,23},{8,24},{9,... | collective-permute-start | bytes 2359304 | tf_op jit(solution)/shard_map/ppermute | solution.py:21
  85.6 28.1 %collective-permute-start.20 = (bf16[128,2048]{1,0:T(8,128)(2,1)S(1)}, bf16[128,2048]{1,0:T(8,128)(2,1)S(1)}, u32[]{:S(2)}, u32[]{:S(2)}) collective-permute-start(bf16[128,2048]{1,0:T(8,128)(2,1)S(1)} %fusion.36), channel_id=1, source_target_pairs={{0,16},{1,17},{2,18},{3,19},{4,20},{5,21},{6,22},{7,23},{8,24},{9,... | collective-permute-start | bytes 1572872 | tf_op jit(solution)/shard_map/ppermute | solution.py:21
  87.4 43.4 %collective-permute-start.28 = (bf16[2,128,2048]{2,1,0:T(8,128)(2,1)S(1)}, bf16[2,128,2048]{2,1,0:T(8,128)(2,1)S(1)}, u32[]{:S(2)}, u32[]{:S(2)}) collective-permute-start(bf16[2,128,2048]{2,1,0:T(8,128)(2,1)S(1)} %get-tuple-element.280), channel_id=1, source_target_pairs={{0,2},{1,3},{2,0},{3,1},{4,6},{5,7},{6,4},{7,5},{8,10},{9,11},{10,... | collective-permute-start | bytes 3145736 | tf_op jit(solution)/shard_map/ppermute | solution.py:21
  88.4 27.9 %collective-permute-start.24 = (bf16[256,1536]{1,0:T(8,128)(2,1)}, bf16[256,1536]{1,0:T(8,128)(2,1)S(1)}, u32[]{:S(2)}, u32[]{:S(2)}) collective-permute-start(bf16[256,1536]{1,0:T(8,128)(2,1)} %collective-permute-done.18), channel_id=1, source_target_pairs={{0,1},{1,0},{2,3},{3,2},{4,5},{5,4},{6,7},{7,6},{8,9},{9,8},{10,11... | collective-permute-start | bytes 2359304 | tf_op jit(solution)/shard_map/ppermute | solution.py:21
  198.1 36.6 %collective-permute-start.43 = (bf16[1024,768]{1,0:T(8,128)(2,1)}, bf16[1024,768]{1,0:T(8,128)(2,1)}, u32[]{:S(2)}, u32[]{:S(2)}) collective-permute-start(bf16[1024,768]{1,0:T(8,128)(2,1)} %get-tuple-element.191), channel_id=1, source_target_pairs={{0,1},{1,0},{2,3},{3,2},{4,5},{5,4},{6,7},{7,6},{8,9},{9,8},{10,11... | collective-permute-start | bytes 4718600 | tf_op jit(solution)/shard_map/ppermute | solution.py:21
  234.6 35.7 %collective-permute-start.44 = (bf16[1024,768]{1,0:T(8,128)(2,1)}, bf16[1024,768]{1,0:T(8,128)(2,1)}, u32[]{:S(2)}, u32[]{:S(2)}) collective-permute-start(bf16[1024,768]{1,0:T(8,128)(2,1)} %get-tuple-element.198), channel_id=1, source_target_pairs={{0,1},{1,0},{2,3},{3,2},{4,5},{5,4},{6,7},{7,6},{8,9},{9,8},{10,11... | collective-permute-start | bytes 4718600 | tf_op jit(solution)/shard_map/ppermute | solution.py:21
  236.3 28.4 %collective-permute-start.45 = (bf16[2,128,2048]{2,1,0:T(8,128)(2,1)}, bf16[2,128,2048]{2,1,0:T(8,128)(2,1)}, u32[]{:S(2)}, u32[]{:S(2)}) collective-permute-start(bf16[2,128,2048]{2,1,0:T(8,128)(2,1)} %fusion.22), channel_id=1, source_target_pairs={{0,16},{1,17},{2,18},{3,19},{4,20},{5,21},{6,22},{7,23},{8,24},{9,... | collective-permute-start | bytes 3145736 | tf_op jit(solution)/shard_map/ppermute | solution.py:21
  240.6 40.2 %collective-permute-start.47 = (bf16[4,1,2,64,768]{4,3,2,0,1:T(8,128)(2,1)}, bf16[4,1,2,64,768]{4,3,2,0,1:T(8,128)(2,1)}, u32[]{:S(2)}, u32[]{:S(2)}) collective-permute-start(bf16[4,1,2,64,768]{4,3,2,0,1:T(8,128)(2,1)} %fusion.28), channel_id=1, source_target_pairs={{0,4},{1,5},{2,6},{3,7},{4,0},{5,1},{6,2},{7,3},{8,12},{9,13},{10,... | collective-permute-start | bytes 2359304 | tf_op jit(solution)/shard_map/ppermute | solution.py:21
  246.9 56.9 %collective-permute-start.51 = (bf16[2,2,64,2048]{3,2,1,0:T(8,128)(2,1)}, bf16[2,2,64,2048]{3,2,1,0:T(8,128)(2,1)S(1)}, u32[]{:S(2)}, u32[]{:S(2)}) collective-permute-start(bf16[2,2,64,2048]{3,2,1,0:T(8,128)(2,1)} %fusion.19), channel_id=1, source_target_pairs={{0,2},{1,3},{2,0},{3,1},{4,6},{5,7},{6,4},{7,5},{8,10},{9,11},{10,... | collective-permute-start | bytes 3145736 | tf_op jit(solution)/shard_map/ppermute | solution.py:21
  274.5 37.9 %collective-permute-start.50 = (bf16[4,1,2,64,768]{4,3,2,0,1:T(8,128)(2,1)S(1)}, bf16[4,1,2,64,768]{4,3,2,0,1:T(8,128)(2,1)S(1)}, u32[]{:S(2)}, u32[]{:S(2)}) collective-permute-start(bf16[4,1,2,64,768]{4,3,2,0,1:T(8,128)(2,1)S(1)} %fusion.29), channel_id=1, source_target_pairs={{0,4},{1,5},{2,6},{3,7},{4,0},{5,1},{6,2},{7,3},{8,12},{9,13},{10,... | collective-permute-start | bytes 2359304 | tf_op jit(solution)/shard_map/ppermute | solution.py:21
  276.5 25.3 %collective-permute-start.54 = (bf16[4,4,128,256]{3,2,1,0:T(8,128)(2,1)S(1)}, bf16[4,4,128,256]{3,2,1,0:T(8,128)(2,1)S(1)}, u32[]{:S(2)}, u32[]{:S(2)}) collective-permute-start(bf16[4,4,128,256]{3,2,1,0:T(8,128)(2,1)S(1)} %copy-done.68), channel_id=1, source_target_pairs={{0,1},{1,0},{2,3},{3,2},{4,5},{5,4},{6,7},{7,6},{8,9},{9,8},{10,11... | collective-permute-start | bytes 3145736 | tf_op jit(solution)/shard_map/ppermute | solution.py:21
  281.3 31.1 %collective-permute-start.48 = (bf16[128,2048]{1,0:T(8,128)(2,1)S(1)}, bf16[128,2048]{1,0:T(8,128)(2,1)S(1)}, u32[]{:S(2)}, u32[]{:S(2)}) collective-permute-start(bf16[128,2048]{1,0:T(8,128)(2,1)S(1)} %fusion.37), channel_id=1, source_target_pairs={{0,16},{1,17},{2,18},{3,19},{4,20},{5,21},{6,22},{7,23},{8,24},{9,... | collective-permute-start | bytes 1572872 | tf_op jit(solution)/shard_map/ppermute | solution.py:21
  284.3 28.1 %collective-permute-start.49 = (bf16[4,64,768]{2,1,0:T(8,128)(2,1)S(1)}, bf16[4,64,768]{2,1,0:T(8,128)(2,1)S(1)}, u32[]{:S(2)}, u32[]{:S(2)}) collective-permute-start(bf16[4,64,768]{2,1,0:T(8,128)(2,1)S(1)} %get-tuple-element.292), channel_id=1, source_target_pairs={{0,2},{1,3},{2,0},{3,1},{4,6},{5,7},{6,4},{7,5},{8,10},{9,11},{10,... | collective-permute-start | bytes 1179656 | tf_op jit(solution)/shard_map/ppermute | solution.py:21
  303.8 24.2 %collective-permute-start.56 = (bf16[4,2,2,64,512]{4,3,2,1,0:T(8,128)(2,1)S(1)}, bf16[4,2,2,64,512]{4,3,2,1,0:T(8,128)(2,1)S(1)}, u32[]{:S(2)}, u32[]{:S(2)}) collective-permute-start(bf16[4,2,2,64,512]{4,3,2,1,0:T(8,128)(2,1)S(1)} %fusion.20), channel_id=1, source_target_pairs={{0,1},{1,0},{2,3},{3,2},{4,5},{5,4},{6,7},{7,6},{8,9},{9,8},{10,11... | collective-permute-start | bytes 3145736 | tf_op jit(solution)/shard_map/ppermute | solution.py:21
  312.6 32.0 %collective-permute-start.52 = (bf16[4,64,768]{2,1,0:T(8,128)(2,1)S(1)}, bf16[4,64,768]{2,1,0:T(8,128)(2,1)S(1)}, u32[]{:S(2)}, u32[]{:S(2)}) collective-permute-start(bf16[4,64,768]{2,1,0:T(8,128)(2,1)S(1)} %get-tuple-element.293), channel_id=1, source_target_pairs={{0,2},{1,3},{2,0},{3,1},{4,6},{5,7},{6,4},{7,5},{8,10},{9,11},{10,... | collective-permute-start | bytes 1179656 | tf_op jit(solution)/shard_map/ppermute | solution.py:21
  348.9 25.4 %collective-permute-start.59 = (bf16[2,2,64,768]{3,2,1,0:T(8,128)(2,1)S(1)}, bf16[2,2,64,768]{3,2,1,0:T(8,128)(2,1)S(1)}, u32[]{:S(2)}, u32[]{:S(2)}) collective-permute-start(bf16[2,2,64,768]{3,2,1,0:T(8,128)(2,1)S(1)} %pad_maximum_fusion.16), channel_id=1, source_target_pairs={{0,16},{1,17},{2,18},{3,19},{4,20},{5,21},{6,22},{7,23},{8,24},{9,... | collective-permute-start | bytes 1179656 | tf_op jit(solution)/shard_map/ppermute | solution.py:21
  350.4 23.9 %collective-permute-start.60 = (bf16[384,1024]{1,0:T(8,128)(2,1)S(1)}, bf16[384,1024]{1,0:T(8,128)(2,1)S(1)}, u32[]{:S(2)}, u32[]{:S(2)}) collective-permute-start(bf16[384,1024]{1,0:T(8,128)(2,1)S(1)} %copy-done.28), channel_id=1, source_target_pairs={{0,1},{1,0},{2,3},{3,2},{4,5},{5,4},{6,7},{7,6},{8,9},{9,8},{10,11... | collective-permute-start | bytes 2359304 | tf_op jit(solution)/shard_map/ppermute | solution.py:21
  352.5 38.6 %collective-permute-start.70 = (bf16[1,192,1024]{2,1,0:T(8,128)(2,1)S(1)}, bf16[1,192,1024]{2,1,0:T(8,128)(2,1)S(1)}, u32[]{:S(2)}, u32[]{:S(2)}) collective-permute-start(bf16[1,192,1024]{2,1,0:T(8,128)(2,1)S(1)} %fusion.42), channel_id=1, source_target_pairs={{0,4},{1,5},{2,6},{3,7},{4,0},{5,1},{6,2},{7,3},{8,12},{9,13},{10,... | collective-permute-start | bytes 1179656 | tf_op jit(solution)/shard_map/ppermute | solution.py:21
  354.6 39.3 %collective-permute-start.72 = (bf16[128,2048]{1,0:T(8,128)(2,1)S(1)}, bf16[128,2048]{1,0:T(8,128)(2,1)S(1)}, u32[]{:S(2)}, u32[]{:S(2)}) collective-permute-start(bf16[128,2048]{1,0:T(8,128)(2,1)S(1)} %fusion.38), channel_id=1, source_target_pairs={{0,2},{1,3},{2,0},{3,1},{4,6},{5,7},{6,4},{7,5},{8,10},{9,11},{10,... | collective-permute-start | bytes 1572872 | tf_op jit(solution)/shard_map/ppermute | solution.py:21
  374.8 25.7 %collective-permute-start.69 = (bf16[2,64,2048]{2,1,0:T(8,128)(2,1)S(1)}, bf16[2,64,2048]{2,1,0:T(8,128)(2,1)S(1)}, u32[]{:S(2)}, u32[]{:S(2)}) collective-permute-start(bf16[2,64,2048]{2,1,0:T(8,128)(2,1)S(1)} %fusion.33), channel_id=1, source_target_pairs={{0,1},{1,0},{2,3},{3,2},{4,5},{5,4},{6,7},{7,6},{8,9},{9,8},{10,11... | collective-permute-start | bytes 1572872 | tf_op jit(solution)/shard_map/ppermute | solution.py:21
  (127 other events, 1505.7 us)

commit v6 on v5

--- a/solution.py
+++ b/solution.py
@@ -13,7 +13,7 @@
 F32 = jnp.float32
 BF16 = jnp.bfloat16
 BOTH = ("grp", "rep")
-BRIEF = pl.CostEstimate(flops=1, transcendentals=0, bytes_accessed=1)
+TILE = 4
 
 
 def swap(value, mask):
@@ -180,7 +180,6 @@
         ),
         out_shape=[shape, shape, small, small],
         compiler_params=pltpu.CompilerParams(vmem_limit_bytes=32 << 20),
-        cost_estimate=BRIEF,
         name="pack",
     )(info, w_gate, w_up)
 
@@ -216,7 +215,6 @@
         out_specs=pl.BlockSpec((mine, part), lambda i: (0, i)),
         out_shape=jax.ShapeDtypeStruct((mine, width), BF16),
         compiler_params=pltpu.CompilerParams(vmem_limit_bytes=32 << 20),
-        cost_estimate=BRIEF,
         name="pack_down",
     )(info, w_down)
 
@@ -338,15 +336,20 @@
     )(info, ha, hb, ga, gb, ua, ub)
 
 
-def rows_grad_kernel(info_ref, ha, hb, da, db, send_one, send_two, keep_one, keep_two):
+def rows_grad_kernel(
+    outer, used, info_ref, ha, hb, da, db, send_one, send_two, keep_one, keep_two
+):
     odd = (info_ref[1] & 1) == 1
     step = pl.program_id(0)
     first = step < pl.num_programs(0) // 2
     grad = t_dot(ha[...], da[...]) + t_dot(hb[...], db[...])
-    half = grad.shape[0] // 2
-    low, upp = grad[:half], grad[half:]
-    send = jnp.where(odd, low, upp).astype(BF16)
-    keep = jnp.where(odd, upp, low)
+    wide = grad.shape[0] // (2 * outer)
+    halves = []
+    for x in range(2):
+        at = [(x * outer + o) * wide for o in range(outer)]
+        halves.append(jnp.concatenate([grad[a : a + used] for a in at], axis=0))
+    send = jnp.where(odd, halves[0], halves[1]).astype(BF16)
+    keep = jnp.where(odd, halves[1], halves[0])
 
     @pl.when(first)
     def _():
@@ -359,25 +362,48 @@
         keep_two[...] = keep
 
 
-def rows_grad(info, ha, hb, da, db):
+def rows_grad(info, ha, hb, da, db, outer, used):
+    count = outer * used
     tokens, mine = ha.shape
     width = da.shape[1]
     part = min(512, width // 2)
     steps = width // part
-    one = pl.BlockSpec((mine // 2, part), lambda i: (0, jnp.minimum(i, steps // 2 - 1)))
-    two = pl.BlockSpec((mine // 2, part), lambda i: (0, jnp.maximum(i - steps // 2, 0)))
+    one = pl.BlockSpec((count, part), lambda i: (0, jnp.minimum(i, steps // 2 - 1)))
+    two = pl.BlockSpec((count, part), lambda i: (0, jnp.maximum(i - steps // 2, 0)))
     lhs = pl.BlockSpec(ha.shape, lambda i: (0, 0))
     rhs = pl.BlockSpec((tokens, part), lambda i: (0, i))
     return pl.pallas_call(
-        rows_grad_kernel,
+        functools.partial(rows_grad_kernel, outer, used),
         grid=(steps,),
         in_specs=[pl.BlockSpec(memory_space=pltpu.SMEM), lhs, lhs, rhs, rhs],
         out_specs=[one, two, one, two],
-        out_shape=[jax.ShapeDtypeStruct((mine // 2, width // 2), BF16)] * 2
-        + [jax.ShapeDtypeStruct((mine // 2, width // 2), F32)] * 2,
+        out_shape=[jax.ShapeDtypeStruct((count, width // 2), BF16)] * 2
+        + [jax.ShapeDtypeStruct((count, width // 2), F32)] * 2,
         compiler_params=pltpu.CompilerParams(vmem_limit_bytes=48 << 20),
         name="rows_grad",
     )(info, ha, hb, da, db)
+
+
+def product_kernel(a_ref, b_ref, out_ref):
+    out_ref[...] = dot(a_ref[...], b_ref[...]).astype(out_ref.dtype)
+
+
+def product(a, b, kind):
+    count, depth = a.shape
+    width = b.shape[1]
+    part = min(512, width)
+    return pl.pallas_call(
+        product_kernel,
+        grid=(width // part,),
+        in_specs=[
+            pl.BlockSpec((count, depth), lambda j: (0, 0)),
+            pl.BlockSpec((depth, part), lambda j: (0, j)),
+        ],
+        out_specs=pl.BlockSpec((count, part), lambda j: (0, j)),
+        out_shape=jax.ShapeDtypeStruct((count, width), kind),
+        compiler_params=pltpu.CompilerParams(vmem_limit_bytes=32 << 20),
+        name="product",
+    )(a, b)
 
 
 def query_back_kernel(rows, d_ref, w_ref, keep_ref, send_ref):
@@ -464,10 +490,10 @@
 
 
 def key_tile(info_ref, slots_ref, kv_ref, tile, reps):
-    per = reps // 4
+    per = reps // TILE
     member = (tile // per) ^ info_ref[0]
-    base = 4 * (tile % per)
-    piece = jnp.concatenate([kv_ref[slots_ref[base + k], member] for k in range(4)], axis=0)
+    base = TILE * (tile % per)
+    piece = jnp.concatenate([kv_ref[slots_ref[base + k], member] for k in range(TILE)], axis=0)
     return piece[:, :HD], piece[:, HD:]
 
 
@@ -486,7 +512,7 @@
         best, total, accum = carry
         key, value = key_tile(info_ref, slots_ref, kv_ref, tile, reps)
         scores = dot_t(query, key) * scale
-        at = tile * 512 + lax.broadcasted_iota(jnp.int32, (1, 512), 1)
+        at = tile * TILE * HD + lax.broadcasted_iota(jnp.int32, (1, TILE * HD), 1)
         scores = jnp.where((at >= lowest) & (at <= position), scores, NEGATIVE)
         new_best = jnp.maximum(best, jnp.max(scores, axis=1, keepdims=True))
         weights = jnp.exp(scores - new_best)
@@ -500,7 +526,9 @@
         jnp.zeros((rows, 1), F32),
         jnp.zeros((rows, HD), F32),
     )
-    best, total, accum = lax.fori_loop(first // 512, place // 512 + 1, step, init)
+    best, total, accum = lax.fori_loop(
+        first // (TILE * HD), place // (TILE * HD) + 1, step, init
+    )
     out = accum / total
     for h in range(4):
         o_ref[0, :, h * HD : (h + 1) * HD] = out[h * HD : (h + 1) * HD].astype(BF16)
@@ -528,7 +556,6 @@
             jax.ShapeDtypeStruct((4, 4 * HD, 1), F32),
         ],
         compiler_params=pltpu.CompilerParams(vmem_limit_bytes=48 << 20),
-        cost_estimate=BRIEF,
         name="attend",
     )(info, slots, starts, query, kv)
 
@@ -561,12 +588,12 @@
     lse = lse_ref[0]
     delta = jnp.sum(d_out.astype(F32) * out.astype(F32), axis=1, keepdims=True)
     scale = HD ** (-0.5)
-    per = reps // 4
+    per = reps // TILE
 
     def step(tile, d_query):
         key, value = key_tile(info_ref, slots_ref, kv_ref, tile, reps)
         scores = dot_t(query, key) * scale
-        at = tile * 512 + lax.broadcasted_iota(jnp.int32, (1, 512), 1)
+        at = tile * TILE * HD + lax.broadcasted_iota(jnp.int32, (1, TILE * HD), 1)
         probs = jnp.where((at >= lowest) & (at <= position), jnp.exp(scores - lse), 0.0)
         d_probs = dot_t(d_out, value)
         d_scores = (probs * (d_probs - delta)).astype(BF16)
@@ -575,13 +602,16 @@
         d_value = t_dot(probs.astype(BF16), d_out)
         member = (tile // per) ^ info_ref[0]
         both = jnp.concatenate([d_key, d_value], axis=1)
-        for k in range(4):
-            slot = (4 * (tile % per) + k) ^ info_ref[1]
+        for k in range(TILE):
+            slot = (TILE * (tile % per) + k) ^ info_ref[1]
             sums[slot, member] = sums[slot, member] + both[k * HD : (k + 1) * HD]
         return d_query
 
     d_query = lax.fori_loop(
-        first // 512, place // 512 + 1, step, jnp.zeros((4 * HD, HD), F32)
+        first // (TILE * HD),
+        place // (TILE * HD) + 1,
+        step,
+        jnp.zeros((4 * HD, HD), F32),
     )
     d_query = (d_query * scale).astype(BF16)
     for h in range(4):
@@ -617,7 +647,6 @@
         + [jax.ShapeDtypeStruct((reps // 2,) + kv.shape[1:], BF16)] * 2,
         scratch_shapes=[pltpu.VMEM(kv.shape, F32)],
         compiler_params=pltpu.CompilerParams(vmem_limit_bytes=60 << 20),
-        cost_estimate=BRIEF,
         name="attend_back",
     )(info, slots, starts, query, d_out, out, lse, kv)
 
@@ -650,6 +679,7 @@
     chunk = hidden_all // (4 * reps)
     wide = -(-(2 * outer * chunk) // 256) * 256 // (2 * outer)
     mine = 2 * outer * wide
+    used = -(-chunk // 16) * 16
     info = jnp.stack([g, r]).astype(jnp.int32)
 
     kv_parts = [
@@ -781,9 +811,9 @@
     to_z, to_y, send_g = together(to_z, to_y, send_g)
     got_g = swap(send_g, xx)
     from_z, from_y = side_step(d_h_parts, to_z, to_y, rows, yy, zz)
-    out_core = swap(dot(after(hidden_b, to_z), wd).astype(BF16), core)
+    out_core = swap(product(after(hidden_b, to_z), wd, BF16), core)
     send_d, send_e, keep_d, keep_e = rows_grad(
-        after(info, to_z), hidden_a, hidden_b, dy_a, dy_b
+        after(info, to_z), hidden_a, hidden_b, dy_a, dy_b, outer, used
     )
     out_parts = dot(after(hidden_a, to_z), wd)
     from_z, from_y, out_core, send_d, out_parts = together(
@@ -861,7 +891,7 @@
 
     got_e = swap(send_e, xx)
     keep_q, got_q = high_part(keep_q + got_q.astype(F32), r, high[-1], 1)
-    grad_d = (keep_d + got_d.astype(F32)).reshape(outer, wide, width // 2)
+    grad_d = (keep_d + got_d.astype(F32)).reshape(outer, used, width // 2)
     keep_d, got_d = high_part(grad_d, r, high[-1], 0)
     grad_u = jnp.stack([near_u, far_u])
     grad_u = [pick(grad_u, g ^ j, 1) for j in range(4)]
@@ -870,7 +900,7 @@
         y_u, got_e, got_q, grad_g, grad_kv, keep_o
     )
 
-    grad_e = (keep_e + got_e.astype(F32)).reshape(outer, wide, width // 2)
+    grad_e = (keep_e + got_e.astype(F32)).reshape(outer, used, width // 2)
     keep_e, got_e = high_part(grad_e, r, high[-1], 0)
     keep_o, got_o = part(keep_o + got_o.astype(F32), x_bit, xx, 1)
     grad_kv = grad_kv[0].astype(BF16)

time: 427 us -> 427 us (level)
  Pallas kernels: 80.1 us -> 88.8 us
  starting transfers between devices: 59.8 us -> 52.5 us
    ppermute x75, starting transfers between devices: 53.8 us -> 46.6 us  [swap(): return lax.ppermute(value, BOTH, [(i, i ^ mask) for i in range(count)])]
    dot_general x4 -> x3, matrix products: 9.53 us -> 6.31 us  [dot(): return jnp.dot(a, b, preferred_element_type=F32)]
    pallas_call x1 -> x2, Pallas kernels: 7.04 us -> 8.83 us  [the longest x1 6.14 us: rows_grad(): pl.pallas_call(functools.partial(rows_grad_kernel, outer, used), grid=(st...]
    unnamed x155 -> x159, local copies, waits for them, and re-layouts: 17.8 us -> 18.4 us
  transfers between devices with their start and end apart: 78 -> 78, of which waited for: 32 -> 30; matrix products, arithmetic and copies ran while one was open for 18% -> 19% of each run, Pallas kernels for 14% -> 15%
where the time goes in v6:
time: 427 us; the launch traced here: 421 us
  waiting for transfers between devices  176 us (41%)
  Pallas kernels  88.8 us (21%)
  other arithmetic  52.8 us (12%)
  starting transfers between devices  52.5 us (12%)
  local copies, waits for them, and re-layouts  36.9 us (9%)
  matrix products  11 us (3%)
    ppermute x75, waiting for transfers between devices, swap(): return lax.ppermute(value, BOTH, [(i, i ^ mask) for i in range(count)])  171 us
    ppermute x75, starting transfers between devices, swap(): return lax.ppermute(value, BOTH, [(i, i ^ mask) for i in range(count)])  46.6 us
    unnamed x159, local copies, waits for them, and re-layouts  18.4 us
    pallas_call x2, Pallas kernels, feed_forward(): pl.pallas_call(feed_forward_kernel, grid=(steps,), in_specs=[whole, whole...  17.3 us
    pallas_call x1, Pallas kernels, attend_back(): pl.pallas_call(functools.partial(attend_back_kernel, reps), grid=(4,), in...  16.2 us
    pallas_call x1, Pallas kernels, columns_grad(): pl.pallas_call(functools.partial(columns_grad_kernel, rows), grid=(width...  11.3 us
    pallas_call x1, Pallas kernels, attend(): pl.pallas_call(functools.partial(attend_kernel, reps), grid=(4,), in_spec...  10 us
  transfers between devices with their start and end apart: 78, of which 30 were waited for; matrix products, arithmetic and copies ran while one was open for 19% of the time, Pallas kernels for 15%

profile of v6, /device:TPU:0, one launch (start us, length us, event | category | flops | bytes accessed | tf_op | source)
XLA Modules:
  0.0 420.7 jit_solution(9629815116858812351)
XLA Ops:
  44.7 4.9 %collective-permute-done.11 = bf16[4,128,256]{2,1,0:T(8,128)(2,1)S(1)} collective-permute-done((bf16[4,128,256]{2,1,0:T(8,128)(2,1)}, bf16[4,128,256]{2,1,0:T(8,128)(2,1)S(1)}, u32[]{:S(2)}, u32[]{:S(2)}) %collective-permute-start.11) | collective-permute-done | bytes 262176 | tf_op jit(solution)/shard_map/ppermute | solution.py:722
  55.8 12.4 %collective-permute-done.13 = bf16[4,128,256]{2,1,0:T(8,128)(2,1)S(1)} collective-permute-done((bf16[4,128,256]{2,1,0:T(8,128)(2,1)S(1)}, bf16[4,128,256]{2,1,0:T(8,128)(2,1)S(1)}, u32[]{:S(2)}, u32[]{:S(2)}) %collective-permute-start.13) | collective-permute-done | bytes 262176 | tf_op jit(solution)/shard_map/ppermute | solution.py:21
  73.8 10.0 %attend.1 = (bf16[4,128,512]{2,1,0:T(8,128)(2,1)S(1)}, f32[4,512,1]{2,1,0:T(8,128)S(1)}) custom-call(s32[2]{0:T(128)S(1)} %pad_add_fusion.info_ref, s32[8]{0:T(128)S(1)} %and_add_fusion.slots_ref, s32[8]{0:T(128)S(1)} %copy-done.28, bf16[4,128,512]{2,1,0:T(8,128)(2,1)S(1)} %bitcast.296, bf16[8,4,128,256]{3,2,1,0:T(8,128)(2,1)S(1)} %bitcast_dynamic-update-slice_fusion.kv_ref), custom_call_target="tpu_custom_call" | custom-call | tf_op jit(solution)/shard_map/attend/pallas_call | solution.py:540
  91.0 14.9 %collective-permute-done.21 = bf16[256,1536]{1,0:T(8,128)(2,1)S(1)} collective-permute-done((bf16[256,1536]{1,0:T(8,128)(2,1)S(1)}, bf16[256,1536]{1,0:T(8,128)(2,1)S(1)}, u32[]{:S(2)}, u32[]{:S(2)}) %collective-permute-start.21) | collective-permute-done | bytes 786464 | tf_op jit(solution)/shard_map/ppermute | solution.py:21
  105.9 10.8 %collective-permute-done.20 = bf16[128,2048]{1,0:T(8,128)(2,1)S(1)} collective-permute-done((bf16[128,2048]{1,0:T(8,128)(2,1)S(1)}, bf16[128,2048]{1,0:T(8,128)(2,1)S(1)}, u32[]{:S(2)}, u32[]{:S(2)}) %collective-permute-start.20) | collective-permute-done | bytes 524320 | tf_op jit(solution)/shard_map/ppermute | solution.py:21
  118.3 12.4 %collective-permute-done.22 = bf16[128,2048]{1,0:T(8,128)(2,1)S(1)} collective-permute-done((bf16[128,2048]{1,0:T(8,128)(2,1)S(1)}, bf16[128,2048]{1,0:T(8,128)(2,1)S(1)}, u32[]{:S(2)}, u32[]{:S(2)}) %collective-permute-start.22) | collective-permute-done | bytes 524320 | tf_op jit(solution)/shard_map/ppermute | solution.py:21
  133.3 4.5 %collective-permute-done.25 = bf16[64,2048]{1,0:T(8,128)(2,1)S(1)} collective-permute-done((bf16[64,2048]{1,0:T(8,128)(2,1)S(1)}, bf16[64,2048]{1,0:T(8,128)(2,1)S(1)}, u32[]{:S(2)}, u32[]{:S(2)}) %collective-permute-start.25) | collective-permute-done | bytes 262176 | tf_op jit(solution)/shard_map/ppermute | solution.py:21
  147.5 8.6 %feed_forward.2 = (bf16[512,768]{1,0:T(8,128)(2,1)S(1)}, bf16[512,768]{1,0:T(8,128)(2,1)S(1)}, bf16[512,768]{1,0:T(8,128)(2,1)S(1)}) custom-call(bf16[512,2048]{1,0:T(8,128)(2,1)S(1)} %collective-permute-done.29.h_ref.hb, bf16[512,2048]{1,0:T(8,128)(2,1)} %copy-done.48, bf16[2048,1536]{1,0:T(8,128)(2,1)} %pad_maximum_fusion.gate_ref.up_ref.w_ref, ...), custom_call_target="tpu_custom_call" | custom-call | tf_op jit(solution)/shard_map/feed_forward/pallas_call | solution.py:241
  156.1 6.6 %inputs_grad.1 = bf16[512,2048]{1,0:T(8,128)(2,1)S(1)} custom-call(bf16[512,768]{1,0:T(8,128)(2,1)S(1)} %get-tuple-element.172.d_gate_ref.gb, bf16[512,768]{1,0:T(8,128)(2,1)S(1)} %get-tuple-element.168.d_up_ref.ub, bf16[2048,1536]{1,0:T(8,128)(2,1)} %pad_maximum_fusion.gate_ref.up_ref.w_ref), custom_call_target="tpu_custom_call" | custom-call | tf_op jit(solution)/shard_map/inputs_grad/pallas_call | solution.py:285
  163.0 8.7 %feed_forward.3 = (bf16[512,768]{1,0:T(8,128)(2,1)S(1)}, bf16[512,768]{1,0:T(8,128)(2,1)S(1)}, bf16[512,768]{1,0:T(8,128)(2,1)S(1)}) custom-call(bf16[512,2048]{1,0:T(8,128)(2,1)S(1)} %constant_dynamic-update-slice_fusion.h_ref.ha, bf16[512,2048]{1,0:T(8,128)(2,1)} %bitcast.299, bf16[2048,1536]{1,0:T(8,128)(2,1)} %pad_maximum_fusion.gate_ref.up_ref.w_ref, ...), custom_call_target="tpu_custom_call" | custom-call | tf_op jit(solution)/shard_map/feed_forward/pallas_call | solution.py:241
  171.7 8.0 %inputs_grad_sum.1 = (f32[384,2048]{1,0:T(8,128)}, bf16[64,2048]{1,0:T(8,128)(2,1)}, bf16[64,2048]{1,0:T(8,128)(2,1)}) custom-call(bf16[512,768]{1,0:T(8,128)(2,1)S(1)} %get-tuple-element.170.d_gate_ref.ga, bf16[512,768]{1,0:T(8,128)(2,1)S(1)} %get-tuple-element.171.d_up_ref.ua, bf16[2048,1536]{1,0:T(8,128)(2,1)} %pad_maximum_fusion.gate_ref.up_ref.w_ref, ...), custom_call_target="tpu_custom_call" | custom-call | tf_op jit(solution)/shard_map/inputs_grad_sum/pallas_call | solution.py:295
  182.8 11.3 %columns_grad.1 = (bf16[1024,768]{1,0:T(8,128)(2,1)}, bf16[1024,768]{1,0:T(8,128)(2,1)}, f32[1024,768]{1,0:T(8,128)}, f32[1024,768]{1,0:T(8,128)}) custom-call(s32[2]{0:T(128)} %copy-done.24, bf16[512,2048]{1,0:T(8,128)(2,1)} %copy-done.5, bf16[512,2048]{1,0:T(8,128)(2,1)} %copy-done.8, bf16[512,768]{1,0:T(8,128)(2,1)} %copy-done.13, ...), custom_call_target="tpu_custom_call" | custom-call | tf_op jit(solution)/shard_map/columns_grad/pallas_call | solution.py:327
  201.4 6.1 %rows_grad.1 = (bf16[352,1024]{1,0:T(8,128)(2,1)S(1)}, bf16[352,1024]{1,0:T(8,128)(2,1)S(1)}, f32[352,1024]{1,0:T(8,128)S(1)}, f32[352,1024]{1,0:T(8,128)S(1)}) custom-call(s32[2]{0:T(128)S(1)} %copy-done.25, bf16[512,768]{1,0:T(8,128)(2,1)S(1)} %copy-done.23, bf16[512,768]{1,0:T(8,128)(2,1)S(1)} %get-tuple-element.182.a_ref.hb, ...), custom_call_target="tpu_custom_call" | custom-call | tf_op jit(solution)/shard_map/rows_grad/pallas_call | solution.py:375
  226.7 5.5 %collective-permute-done.40 = bf16[128,2048]{1,0:T(8,128)(2,1)} collective-permute-done((bf16[128,2048]{1,0:T(8,128)(2,1)}, bf16[128,2048]{1,0:T(8,128)(2,1)}, u32[]{:S(2)}, u32[]{:S(2)}) %collective-permute-start.40) | collective-permute-done | bytes 524320 | tf_op jit(solution)/shard_map/ppermute | solution.py:21
  251.5 16.2 %attend_back.1 = (bf16[4,128,512]{2,1,0:T(8,128)(2,1)}, bf16[4,4,128,256]{3,2,1,0:T(8,128)(2,1)}, bf16[4,4,128,256]{3,2,1,0:T(8,128)(2,1)}) custom-call(s32[2]{0:T(128)} %copy-done.24, s32[8]{0:T(128)} %copy-done.27, s32[8]{0:T(128)} %starts_ref.3, bf16[4,128,512]{2,1,0:T(8,128)(2,1)} %bitcast.297, bf16[4,128,512]{2,1,0:T(8,128)(2,1)} %bitcast.323, ...), custom_call_target="tpu_custom_call" | custom-call | tf_op jit(solution)/shard_map/attend_back/pallas_call | solution.py:632
  269.7 5.2 %collective-permute-done.44 = bf16[1024,768]{1,0:T(8,128)(2,1)} collective-permute-done((bf16[1024,768]{1,0:T(8,128)(2,1)}, bf16[1024,768]{1,0:T(8,128)(2,1)}, u32[]{:S(2)}, u32[]{:S(2)}) %collective-permute-start.44) | collective-permute-done | bytes 1572896 | tf_op jit(solution)/shard_map/ppermute | solution.py:21
  288.4 16.3 %collective-permute-done.54 = bf16[4,4,128,256]{3,2,1,0:T(8,128)(2,1)S(1)} collective-permute-done((bf16[4,4,128,256]{3,2,1,0:T(8,128)(2,1)S(1)}, bf16[4,4,128,256]{3,2,1,0:T(8,128)(2,1)S(1)}, u32[]{:S(2)}, u32[]{:S(2)}) %collective-permute-start.54) | collective-permute-done | bytes 1048608 | tf_op jit(solution)/shard_map/ppermute | solution.py:21
  307.4 9.6 %collective-permute-done.50 = bf16[4,1,2,64,768]{4,3,2,0,1:T(8,128)(2,1)S(1)} collective-permute-done((bf16[4,1,2,64,768]{4,3,2,0,1:T(8,128)(2,1)S(1)}, bf16[4,1,2,64,768]{4,3,2,0,1:T(8,128)(2,1)S(1)}, u32[]{:S(2)}, u32[]{:S(2)}) %collective-permute-start.50) | collective-permute-done | bytes 786464 | tf_op jit(solution)/shard_map/ppermute | solution.py:21
  318.5 9.6 %collective-permute-done.55 = bf16[2,4,128,256]{3,2,1,0:T(8,128)(2,1)S(1)} collective-permute-done((bf16[2,4,128,256]{3,2,1,0:T(8,128)(2,1)S(1)}, bf16[2,4,128,256]{3,2,1,0:T(8,128)(2,1)S(1)}, u32[]{:S(2)}, u32[]{:S(2)}) %collective-permute-start.55) | collective-permute-done | bytes 524320 | tf_op jit(solution)/shard_map/ppermute | solution.py:21
  338.1 10.1 %collective-permute-done.64 = bf16[1,4,128,256]{3,2,1,0:T(8,128)(2,1)S(1)} collective-permute-done((bf16[1,4,128,256]{3,2,1,0:T(8,128)(2,1)S(1)}, bf16[1,4,128,256]{3,2,1,0:T(8,128)(2,1)S(1)}, u32[]{:S(2)}, u32[]{:S(2)}) %collective-permute-start.64) | collective-permute-done | bytes 262176 | tf_op jit(solution)/shard_map/ppermute | solution.py:21
  348.3 5.1 %collective-permute-done.58 = bf16[4,2,64,512]{3,2,1,0:T(8,128)(2,1)S(1)} collective-permute-done((bf16[4,2,64,512]{3,2,1,0:T(8,128)(2,1)S(1)}, bf16[4,2,64,512]{3,2,1,0:T(8,128)(2,1)S(1)}, u32[]{:S(2)}, u32[]{:S(2)}) %collective-permute-start.58) | collective-permute-done | bytes 524320 | tf_op jit(solution)/shard_map/ppermute | solution.py:21
  359.2 17.1 %collective-permute-done.61 = bf16[4,1,64,512]{3,2,1,0:T(8,128)(2,1)S(1)} collective-permute-done((bf16[4,1,64,512]{3,2,1,0:T(8,128)(2,1)S(1)}, bf16[4,1,64,512]{3,2,1,0:T(8,128)(2,1)S(1)}, u32[]{:S(2)}, u32[]{:S(2)}) %collective-permute-start.61) | collective-permute-done | bytes 262176 | tf_op jit(solution)/shard_map/ppermute | solution.py:21
  379.2 12.5 %collective-permute-done.70 = bf16[1,176,1024]{2,1,0:T(8,128)(2,1)S(1)} collective-permute-done((bf16[1,176,1024]{2,1,0:T(8,128)(2,1)S(1)}, bf16[1,176,1024]{2,1,0:T(8,128)(2,1)S(1)}, u32[]{:S(2)}, u32[]{:S(2)}) %collective-permute-start.70) | collective-permute-done | bytes 360480 | tf_op jit(solution)/shard_map/ppermute | solution.py:21
  394.6 4.1 collective-permute-done.65
  (438 shorter events, 187.0 us)
Async XLA Ops:
  7.9 44.3 %collective-permute-start = (bf16[128,2048]{1,0:T(8,128)(2,1)}, bf16[128,2048]{1,0:T(8,128)(2,1)}, u32[]{:S(2)}, u32[]{:S(2)}) collective-permute-start(bf16[128,2048]{1,0:T(8,128)(2,1)} %fusion.11), channel_id=1, source_target_pairs={{0,8},{1,9},{2,10},{3,11},{4,12},{5,13},{6,14},{7,15},{8,0},{9,1},... | collective-permute-start | bytes 1572872 | tf_op jit(solution)/shard_map/ppermute | solution.py:21
  15.8 23.9 %collective-permute-start.9 = (bf16[2,256,512]{2,1,0:T(8,128)(2,1)}, bf16[2,256,512]{2,1,0:T(8,128)(2,1)}, u32[]{:S(2)}, u32[]{:S(2)}) collective-permute-start(bf16[2,256,512]{2,1,0:T(8,128)(2,1)} %pad_maximum_fusion.12), channel_id=1, source_target_pairs={{0,16},{1,17},{2,18},{3,19},{4,20},{5,21},{6,22},{7,23},{8,24},{9,... | collective-permute-start | bytes 1572872 | tf_op jit(solution)/shard_map/ppermute | solution.py:21
  30.5 23.3 %collective-permute-start.7 = (bf16[128,2048]{1,0:T(8,128)(2,1)}, bf16[128,2048]{1,0:T(8,128)(2,1)S(1)}, u32[]{:S(2)}, u32[]{:S(2)}) collective-permute-start(bf16[128,2048]{1,0:T(8,128)(2,1)} %collective-permute-done.5), channel_id=1, source_target_pairs={{0,8},{1,9},{2,10},{3,11},{4,12},{5,13},{6,14},{7,15},{8,0},{9,1},... | collective-permute-start | bytes 1572872 | tf_op jit(solution)/shard_map/ppermute | solution.py:21
  43.2 25.0 %collective-permute-start.14 = (bf16[2,256,512]{2,1,0:T(8,128)(2,1)}, bf16[2,256,512]{2,1,0:T(8,128)(2,1)S(1)}, u32[]{:S(2)}, u32[]{:S(2)}) collective-permute-start(bf16[2,256,512]{2,1,0:T(8,128)(2,1)} %collective-permute-done.9), channel_id=1, source_target_pairs={{0,1},{1,0},{2,3},{3,2},{4,5},{5,4},{6,7},{7,6},{8,9},{9,8},{10,11... | collective-permute-start | bytes 1572872 | tf_op jit(solution)/shard_map/ppermute | solution.py:21
  52.2 31.7 %collective-permute-start.18 = (bf16[256,1536]{1,0:T(8,128)(2,1)S(1)}, bf16[256,1536]{1,0:T(8,128)(2,1)}, u32[]{:S(2)}, u32[]{:S(2)}) collective-permute-start(bf16[256,1536]{1,0:T(8,128)(2,1)S(1)} %get-tuple-element.150), channel_id=1, source_target_pairs={{0,16},{1,17},{2,18},{3,19},{4,20},{5,21},{6,22},{7,23},{8,24},{9,... | collective-permute-start | bytes 2359304 | tf_op jit(solution)/shard_map/ppermute | solution.py:21
  88.5 28.1 %collective-permute-start.20 = (bf16[128,2048]{1,0:T(8,128)(2,1)S(1)}, bf16[128,2048]{1,0:T(8,128)(2,1)S(1)}, u32[]{:S(2)}, u32[]{:S(2)}) collective-permute-start(bf16[128,2048]{1,0:T(8,128)(2,1)S(1)} %fusion.36), channel_id=1, source_target_pairs={{0,16},{1,17},{2,18},{3,19},{4,20},{5,21},{6,22},{7,23},{8,24},{9,... | collective-permute-start | bytes 1572872 | tf_op jit(solution)/shard_map/ppermute | solution.py:21
  90.3 42.9 %collective-permute-start.28 = (bf16[2,128,2048]{2,1,0:T(8,128)(2,1)S(1)}, bf16[2,128,2048]{2,1,0:T(8,128)(2,1)S(1)}, u32[]{:S(2)}, u32[]{:S(2)}) collective-permute-start(bf16[2,128,2048]{2,1,0:T(8,128)(2,1)S(1)} %get-tuple-element.280), channel_id=1, source_target_pairs={{0,2},{1,3},{2,0},{3,1},{4,6},{5,7},{6,4},{7,5},{8,10},{9,11},{10,... | collective-permute-start | bytes 3145736 | tf_op jit(solution)/shard_map/ppermute | solution.py:21
  90.8 27.5 %collective-permute-start.24 = (bf16[256,1536]{1,0:T(8,128)(2,1)}, bf16[256,1536]{1,0:T(8,128)(2,1)S(1)}, u32[]{:S(2)}, u32[]{:S(2)}) collective-permute-start(bf16[256,1536]{1,0:T(8,128)(2,1)} %collective-permute-done.18), channel_id=1, source_target_pairs={{0,1},{1,0},{2,3},{3,2},{4,5},{5,4},{6,7},{7,6},{8,9},{9,8},{10,11... | collective-permute-start | bytes 2359304 | tf_op jit(solution)/shard_map/ppermute | solution.py:21
  200.8 36.9 %collective-permute-start.43 = (bf16[1024,768]{1,0:T(8,128)(2,1)}, bf16[1024,768]{1,0:T(8,128)(2,1)}, u32[]{:S(2)}, u32[]{:S(2)}) collective-permute-start(bf16[1024,768]{1,0:T(8,128)(2,1)} %get-tuple-element.191), channel_id=1, source_target_pairs={{0,1},{1,0},{2,3},{3,2},{4,5},{5,4},{6,7},{7,6},{8,9},{9,8},{10,11... | collective-permute-start | bytes 4718600 | tf_op jit(solution)/shard_map/ppermute | solution.py:21
  237.7 37.2 %collective-permute-start.44 = (bf16[1024,768]{1,0:T(8,128)(2,1)}, bf16[1024,768]{1,0:T(8,128)(2,1)}, u32[]{:S(2)}, u32[]{:S(2)}) collective-permute-start(bf16[1024,768]{1,0:T(8,128)(2,1)} %get-tuple-element.198), channel_id=1, source_target_pairs={{0,1},{1,0},{2,3},{3,2},{4,5},{5,4},{6,7},{7,6},{8,9},{9,8},{10,11... | collective-permute-start | bytes 4718600 | tf_op jit(solution)/shard_map/ppermute | solution.py:21
  239.5 30.2 %collective-permute-start.45 = (bf16[2,128,2048]{2,1,0:T(8,128)(2,1)}, bf16[2,128,2048]{2,1,0:T(8,128)(2,1)}, u32[]{:S(2)}, u32[]{:S(2)}) collective-permute-start(bf16[2,128,2048]{2,1,0:T(8,128)(2,1)} %fusion.22), channel_id=1, source_target_pairs={{0,16},{1,17},{2,18},{3,19},{4,20},{5,21},{6,22},{7,23},{8,24},{9,... | collective-permute-start | bytes 3145736 | tf_op jit(solution)/shard_map/ppermute | solution.py:21
  243.4 40.2 %collective-permute-start.47 = (bf16[4,1,2,64,768]{4,3,2,0,1:T(8,128)(2,1)}, bf16[4,1,2,64,768]{4,3,2,0,1:T(8,128)(2,1)}, u32[]{:S(2)}, u32[]{:S(2)}) collective-permute-start(bf16[4,1,2,64,768]{4,3,2,0,1:T(8,128)(2,1)} %fusion.28), channel_id=1, source_target_pairs={{0,4},{1,5},{2,6},{3,7},{4,0},{5,1},{6,2},{7,3},{8,12},{9,13},{10,... | collective-permute-start | bytes 2359304 | tf_op jit(solution)/shard_map/ppermute | solution.py:21
  247.9 58.9 %collective-permute-start.51 = (bf16[2,2,64,2048]{3,2,1,0:T(8,128)(2,1)}, bf16[2,2,64,2048]{3,2,1,0:T(8,128)(2,1)S(1)}, u32[]{:S(2)}, u32[]{:S(2)}) collective-permute-start(bf16[2,2,64,2048]{3,2,1,0:T(8,128)(2,1)} %fusion.19), channel_id=1, source_target_pairs={{0,2},{1,3},{2,0},{3,1},{4,6},{5,7},{6,4},{7,5},{8,10},{9,11},{10,... | collective-permute-start | bytes 3145736 | tf_op jit(solution)/shard_map/ppermute | solution.py:21
  279.1 37.9 %collective-permute-start.50 = (bf16[4,1,2,64,768]{4,3,2,0,1:T(8,128)(2,1)S(1)}, bf16[4,1,2,64,768]{4,3,2,0,1:T(8,128)(2,1)S(1)}, u32[]{:S(2)}, u32[]{:S(2)}) collective-permute-start(bf16[4,1,2,64,768]{4,3,2,0,1:T(8,128)(2,1)S(1)} %fusion.29), channel_id=1, source_target_pairs={{0,4},{1,5},{2,6},{3,7},{4,0},{5,1},{6,2},{7,3},{8,12},{9,13},{10,... | collective-permute-start | bytes 2359304 | tf_op jit(solution)/shard_map/ppermute | solution.py:21
  279.2 25.6 %collective-permute-start.54 = (bf16[4,4,128,256]{3,2,1,0:T(8,128)(2,1)S(1)}, bf16[4,4,128,256]{3,2,1,0:T(8,128)(2,1)S(1)}, u32[]{:S(2)}, u32[]{:S(2)}) collective-permute-start(bf16[4,4,128,256]{3,2,1,0:T(8,128)(2,1)S(1)} %copy-done.70), channel_id=1, source_target_pairs={{0,1},{1,0},{2,3},{3,2},{4,5},{5,4},{6,7},{7,6},{8,9},{9,8},{10,11... | collective-permute-start | bytes 3145736 | tf_op jit(solution)/shard_map/ppermute | solution.py:21
  284.0 33.0 %collective-permute-start.48 = (bf16[128,2048]{1,0:T(8,128)(2,1)S(1)}, bf16[128,2048]{1,0:T(8,128)(2,1)S(1)}, u32[]{:S(2)}, u32[]{:S(2)}) collective-permute-start(bf16[128,2048]{1,0:T(8,128)(2,1)S(1)} %fusion.37), channel_id=1, source_target_pairs={{0,16},{1,17},{2,18},{3,19},{4,20},{5,21},{6,22},{7,23},{8,24},{9,... | collective-permute-start | bytes 1572872 | tf_op jit(solution)/shard_map/ppermute | solution.py:21
  287.0 30.0 %collective-permute-start.49 = (bf16[4,64,768]{2,1,0:T(8,128)(2,1)S(1)}, bf16[4,64,768]{2,1,0:T(8,128)(2,1)S(1)}, u32[]{:S(2)}, u32[]{:S(2)}) collective-permute-start(bf16[4,64,768]{2,1,0:T(8,128)(2,1)S(1)} %get-tuple-element.292), channel_id=1, source_target_pairs={{0,2},{1,3},{2,0},{3,1},{4,6},{5,7},{6,4},{7,5},{8,10},{9,11},{10,... | collective-permute-start | bytes 1179656 | tf_op jit(solution)/shard_map/ppermute | solution.py:21
  305.1 23.1 %collective-permute-start.55 = (bf16[2,4,128,256]{3,2,1,0:T(8,128)(2,1)S(1)}, bf16[2,4,128,256]{3,2,1,0:T(8,128)(2,1)S(1)}, u32[]{:S(2)}, u32[]{:S(2)}) collective-permute-start(bf16[2,4,128,256]{3,2,1,0:T(8,128)(2,1)S(1)} %fusion.39), channel_id=1, source_target_pairs={{0,2},{1,3},{2,0},{3,1},{4,6},{5,7},{6,4},{7,5},{8,10},{9,11},{10,... | collective-permute-start | bytes 1572872 | tf_op jit(solution)/shard_map/ppermute | solution.py:21
  306.8 24.5 %collective-permute-start.56 = (bf16[4,2,2,64,512]{4,3,2,1,0:T(8,128)(2,1)S(1)}, bf16[4,2,2,64,512]{4,3,2,1,0:T(8,128)(2,1)S(1)}, u32[]{:S(2)}, u32[]{:S(2)}) collective-permute-start(bf16[4,2,2,64,512]{4,3,2,1,0:T(8,128)(2,1)S(1)} %fusion.20), channel_id=1, source_target_pairs={{0,1},{1,0},{2,3},{3,2},{4,5},{5,4},{6,7},{7,6},{8,9},{9,8},{10,11... | collective-permute-start | bytes 3145736 | tf_op jit(solution)/shard_map/ppermute | solution.py:21
  317.2 31.1 %collective-permute-start.52 = (bf16[4,64,768]{2,1,0:T(8,128)(2,1)S(1)}, bf16[4,64,768]{2,1,0:T(8,128)(2,1)S(1)}, u32[]{:S(2)}, u32[]{:S(2)}) collective-permute-start(bf16[4,64,768]{2,1,0:T(8,128)(2,1)S(1)} %get-tuple-element.293), channel_id=1, source_target_pairs={{0,2},{1,3},{2,0},{3,1},{4,6},{5,7},{6,4},{7,5},{8,10},{9,11},{10,... | collective-permute-start | bytes 1179656 | tf_op jit(solution)/shard_map/ppermute | solution.py:21
  353.5 22.9 %collective-permute-start.59 = (bf16[2,2,64,768]{3,2,1,0:T(8,128)(2,1)S(1)}, bf16[2,2,64,768]{3,2,1,0:T(8,128)(2,1)S(1)}, u32[]{:S(2)}, u32[]{:S(2)}) collective-permute-start(bf16[2,2,64,768]{3,2,1,0:T(8,128)(2,1)S(1)} %pad_maximum_fusion.16), channel_id=1, source_target_pairs={{0,16},{1,17},{2,18},{3,19},{4,20},{5,21},{6,22},{7,23},{8,24},{9,... | collective-permute-start | bytes 1179656 | tf_op jit(solution)/shard_map/ppermute | solution.py:21
  356.5 35.2 %collective-permute-start.70 = (bf16[1,176,1024]{2,1,0:T(8,128)(2,1)S(1)}, bf16[1,176,1024]{2,1,0:T(8,128)(2,1)S(1)}, u32[]{:S(2)}, u32[]{:S(2)}) collective-permute-start(bf16[1,176,1024]{2,1,0:T(8,128)(2,1)S(1)} %fusion.42), channel_id=1, source_target_pairs={{0,4},{1,5},{2,6},{3,7},{4,0},{5,1},{6,2},{7,3},{8,12},{9,13},{10,... | collective-permute-start | bytes 1081352 | tf_op jit(solution)/shard_map/ppermute | solution.py:21
  358.5 36.1 %collective-permute-start.72 = (bf16[128,2048]{1,0:T(8,128)(2,1)S(1)}, bf16[128,2048]{1,0:T(8,128)(2,1)S(1)}, u32[]{:S(2)}, u32[]{:S(2)}) collective-permute-start(bf16[128,2048]{1,0:T(8,128)(2,1)S(1)} %fusion.38), channel_id=1, source_target_pairs={{0,2},{1,3},{2,0},{3,1},{4,6},{5,7},{6,4},{7,5},{8,10},{9,11},{10,... | collective-permute-start | bytes 1572872 | tf_op jit(solution)/shard_map/ppermute | solution.py:21
  376.9 24.2 %collective-permute-start.69 = (bf16[2,64,2048]{2,1,0:T(8,128)(2,1)S(1)}, bf16[2,64,2048]{2,1,0:T(8,128)(2,1)S(1)}, u32[]{:S(2)}, u32[]{:S(2)}) collective-permute-start(bf16[2,64,2048]{2,1,0:T(8,128)(2,1)S(1)} %fusion.33), channel_id=1, source_target_pairs={{0,1},{1,0},{2,3},{3,2},{4,5},{5,4},{6,7},{7,6},{8,9},{9,8},{10,11... | collective-permute-start | bytes 1572872 | tf_op jit(solution)/shard_map/ppermute | solution.py:21
  (129 other events, 1514.7 us)
